TPU v7x, 256 devices: a whole 4x4x8 slice. The times are simulated.
256 devices in a mesh: rep: 8 (over x, y_lo), row: 32 (over y_hi, z, core).
Axes of the slice: x: 4, y: 4 (y_hi: 2, y_lo: 2; y = y_hi * 2 + y_lo), z: 8, core: 2. Of those that a mesh axis runs over, the one named last changes fastest.
Arguments:
- features: bfloat16 [32, 2048, 128], P('row', 'rep'), may hold values from -6 to 6
- weight: bfloat16 [128, 128], replicated, may hold values from -0.5 to 0.5
- cotangent: bfloat16 [32, 2048, 128], P('row', 'rep'), may hold values from -6 to 6
- tiles: bfloat16 [32, 8, 256, 128, 128], P('row', 'rep'), may hold values from -0.0625 to 0.0625
- row_ids: int32 [32, 8, 256], P('row', 'rep'), may hold values from 0 to 15
- col_ids: int32 [32, 8, 256], P('row', 'rep'), may hold values from 0 to 63
- counts: int32 [32, 8], P('row', 'rep'), may hold values from 64 to 256, as said below
Outputs:
- hidden: bfloat16 [32, 2048, 128], P('row', 'rep')
- grad_features: bfloat16 [32, 2048, 128], P('row', 'rep')
- grad_weight: float32 [128, 128], replicated
Inputs may be any that keep to these rules, and one draw needn't show every extreme that they name: In every draw some group and slab has exactly 256 tiles in use. A count above 128 is exactly 256; for every slab r and group i < 16, counts[i, r] and counts[i + 16, r] are never both above 128.
All inputs are finite; a program needn't handle non-finite values.
Results may differ from a plain program's by a relative error of at most 0.017.
Values may be sent and summed in bfloat16 or wider, within the bound.
No kernel may reach another device: no remote copies, remote signals or barrier semaphores. Data moves between devices by JAX's collectives and lax.ppermute only.
A program may use at most 128 MiB of HBM per device.

v0:
```python
import jax
import jax.numpy as jnp
from jax import lax
from jax.sharding import PartitionSpec as P


def tile_pass(tiles, row_part, col_part, low, high, source, target_blocks, forward, width):
    length = tiles.shape[0]
    block = tiles.shape[1]
    feats = source.shape[2]
    turns = jnp.maximum(high - low + width - 1, 0) // width

    def step(turn, total):
        begin = low + turn * width
        start = jnp.clip(begin, 0, length - width)
        piece = lax.dynamic_slice_in_dim(tiles, start, width, 0)
        row_slice = lax.dynamic_slice_in_dim(row_part, start, width, 0)
        col_slice = lax.dynamic_slice_in_dim(col_part, start, width, 0)
        index = start + jnp.arange(width, dtype=jnp.int32)
        valid = (index >= begin) & (index < high)
        if forward:
            inputs = jnp.take(source, col_slice, axis=0)
            products = jnp.einsum("tab,tbf->taf", piece, inputs, preferred_element_type=jnp.float32)
            target = row_slice
        else:
            inputs = jnp.take(source, row_slice, axis=0)
            products = jnp.einsum("tab,taf->tbf", piece, inputs, preferred_element_type=jnp.float32)
            target = col_slice
        select = (target[None, :] == jnp.arange(target_blocks, dtype=jnp.int32)[:, None]) & valid[
            None, :
        ]
        return total + jnp.einsum("qt,taf->qaf", select.astype(jnp.float32), products)

    initial = jnp.zeros((target_blocks, block, feats), jnp.float32)
    return lax.fori_loop(0, turns, step, initial)


def local(features, weight, cotangent, tiles, row_ids, col_ids, counts):
    local_x = features[0]
    local_cot = cotangent[0]
    nodes = local_x.shape[0]
    feats = local_x.shape[1]
    own_tiles = tiles[0, 0]
    own_rows = row_ids[0, 0]
    own_cols = col_ids[0, 0]
    count = counts[0, 0]
    capacity = own_tiles.shape[0]
    block = own_tiles.shape[1]
    row_blocks = lax.axis_size("rep") * nodes // block
    col_blocks = lax.axis_size("row") * nodes // block
    spare = 3 * capacity // 8
    width = min(32, spare)
    xw = jnp.dot(local_x, weight, preferred_element_type=jnp.float32).astype(jnp.bfloat16)
    slab = lax.all_gather(xw, "row", axis=0, tiled=True)
    slab_blocks = slab.reshape(col_blocks, block, feats)
    zpart = tile_pass(own_tiles, own_rows, own_cols, 0, count, slab_blocks, row_blocks, True, width)
    zpart = zpart.reshape(row_blocks * block, feats)
    zmine = lax.psum_scatter(zpart, "rep", scatter_dimension=0, tiled=True)
    sigma = jax.nn.sigmoid(zmine)
    out_rows = (zmine * sigma).astype(jnp.bfloat16)
    grad_pre = (local_cot.astype(jnp.float32) * sigma * (1.0 + zmine * (1.0 - sigma))).astype(
        jnp.bfloat16
    )
    grad_full = lax.all_gather(grad_pre, "rep", axis=0, tiled=True)
    grad_blocks = grad_full.reshape(row_blocks, block, feats)
    slab_part = tile_pass(
        own_tiles, own_rows, own_cols, 0, count, grad_blocks, col_blocks, False, width
    )
    grad_sum = lax.psum_scatter(
        slab_part.reshape(col_blocks * block, feats), "row", scatter_dimension=0, tiled=True
    )
    grad_xw = grad_sum.astype(jnp.bfloat16)
    grad_feats = lax.dot_general(
        grad_xw, weight, (((1,), (1,)), ((), ())), preferred_element_type=jnp.float32
    )
    weight_part = lax.dot_general(
        local_x, grad_xw, (((0,), (0,)), ((), ())), preferred_element_type=jnp.float32
    )
    grad_weight = lax.psum(weight_part, ("rep", "row"))
    return (out_rows[None], grad_feats.astype(jnp.bfloat16)[None], grad_weight)


def solution(mesh):
    return jax.shard_map(
        local,
        mesh=mesh,
        in_specs=(
            P("row", "rep", None),
            P(),
            P("row", "rep", None),
            P("row", "rep", None, None, None),
            P("row", "rep", None),
            P("row", "rep", None),
            P("row", "rep"),
        ),
        out_specs=(P("row", "rep", None), P("row", "rep", None), P()),
        check_vma=False,
    )
```

profile of v0, /device:TPU:1, one launch (start us, length us, event | category | flops | bytes accessed | tf_op | source)
XLA Modules:
  0.0 677.4 jit_solution(2880640638468539834)
XLA Ops:
  7.2 0.8 copy-done
  8.0 1.5 convolution_convert_fusion.1
  10.3 85.3 %all-gather.2.cloned.1.call-done = bf16[8192,128]{1,0:T(8,128)(2,1)} async-done(((bf16[256,128]{1,0:T(8,128)(2,1)}), bf16[8192,128]{1,0:T(8,128)(2,1)}) %all-gather.2.cloned.1.call-update) | async-done | bytes 2097168 | tf_op jit(solution)/shard_map/all_gather | solution.py:54
  95.7 21.1 %while.20 = (s32[]{:T(128)}, f32[16,128,128]{2,0,1:T(8,128)S(1)}, s32[]{:T(128)}, s32[256]{0:T(256)}, s32[]{:T(128)}, /*index=5*/bf16[256,128,128]{2,1,0:T(8,128...) while((s32[]{:T(128)}, f32[16,128,128]{2,0,1:T(8,128)S(1)}, ...), condition=%wide.region_1.2_spmd, body=%wide.region_0.1_spmd.sunk | while | flops 151783744 | bytes 8395429 | solution.py:35
  95.7 0.8 dynamic_slice.31
  96.4 1.4 compare_and_fusion.6
  97.8 2.3 gather_fusion
  100.2 1.7 fusion.55
  103.5 1.4 compare_and_fusion.6
  104.9 2.3 gather_fusion
  107.2 1.7 fusion.55
  110.5 1.4 compare_and_fusion.6
  111.9 2.3 gather_fusion
  114.3 1.7 fusion.55
  116.8 1.3 copy.12
  118.2 68.9 %reduce-scatter.3.cloned.1.call-done = f32[256,128]{1,0:T(8,128)} async-done(((f32[2048,128]{1,0:T(8,128)}), f32[256,128]{1,0:T(8,128)}) %reduce-scatter.3.cloned.1.call-update) | async-done | bytes 131088 | tf_op jit(solution)/shard_map/reduce_scatter | solution.py:58
  187.1 1.6 fusion.32
  188.7 22.5 %all_gather.7 = bf16[2048,128]{1,0:T(8,128)(2,1)S(1)} all-gather(bf16[256,128]{1,0:T(8,128)(2,1)S(1)} %get-tuple-element.135), channel_id=1, replica_groups=mesh['rep'=8,'row'=32] {'rep'}, dimensions={0}, use_global_device_ids=true | all-gather | bytes 589824 | tf_op jit(solution)/shard_map/all_gather | solution.py:64
  211.2 2.5 broadcast_in_dim.44
  213.7 25.8 %while.21 = (s32[]{:T(128)}, f32[64,128,128]{2,0,1:T(8,128)}, s32[]{:T(128)}, s32[256]{0:T(256)S(1)}, s32[]{:T(128)}, /*index=5*/bf16[256,128,128]{2,1,0:T(8,128...) while((s32[]{:T(128)}, f32[64,128,128]{2,0,1:T(8,128)}, ...), condition=%wide.region_4.5_spmd, body=%wide.region_3.4_spmd.sunk | while | flops 202904896 | bytes 14686885 | solution.py:35
  215.3 1.8 fusion.61
  217.1 5.2 convolution_add_fusion.2
  223.9 1.8 fusion.61
  225.7 5.2 convolution_add_fusion.2
  232.5 1.8 fusion.61
  234.3 5.2 convolution_add_fusion.2
  239.5 6.6 copy.13
  246.1 176.0 %reduce-scatter.5.cloned.1.call-done = f32[256,128]{1,0:T(8,128)} async-done(((f32[8192,128]{1,0:T(8,128)}), f32[256,128]{1,0:T(8,128)}) %reduce-scatter.5.cloned.1.call-update) | async-done | bytes 131088 | tf_op jit(solution)/shard_map/reduce_scatter | solution.py:69
  422.2 1.7 convolution_bitcast_fusion
  423.9 1.7 fusion.30
  425.6 243.7 %all-reduce.2.cloned.1.call-done = f32[128,128]{0,1:T(8,128)} async-done(((f32[128,128]{0,1:T(8,128)}), f32[128,128]{0,1:T(8,128)}) %all-reduce.2.cloned.1.call-update) | async-done | bytes 65552 | tf_op jit(solution)/shard_map/psum | solution.py:79
  669.3 1.6 copy.14
  (38 shorter events, 8.8 us)
Async XLA Ops:
  7.2 0.8 copy-start
  7.2 88.4 %all-gather.2.cloned.1.call-start = ((), (), s32[]{:S(2)}) async-start(), calls=%async_computation.2 | async-start | bytes 2162688 | tf_op jit(solution)/shard_map/all_gather | solution.py:54
  9.6 177.5 %reduce-scatter.3.cloned.1.call-start = ((), (), s32[]{:S(2)}) async-start(), calls=%async_computation.3 | async-start | bytes 1179648 | tf_op jit(solution)/shard_map/reduce_scatter | solution.py:58
  95.6 91.5 %copy-start.2 = (bf16[1,256,128]{2,1,0:T(8,128)(2,1)S(1)}, bf16[1,256,128]{2,1,0:T(8,128)(2,1)}, u32[]{:S(2)}) copy-start(bf16[1,256,128]{2,1,0:T(8,128)(2,1)} %param.13) | copy-start | bytes 196612
  116.8 96.9 %copy-start.3 = (s32[256]{0:T(256)S(1)}, s32[256]{0:T(256)}, u32[]{:S(2)}) copy-start(s32[256]{0:T(256)} %get-tuple-element.338) | copy-start | bytes 3076
  116.8 96.9 %copy-start.4 = (s32[256]{0:T(256)S(1)}, s32[256]{0:T(256)}, u32[]{:S(2)}) copy-start(s32[256]{0:T(256)} %get-tuple-element.339) | copy-start | bytes 3076
  118.1 304.0 %reduce-scatter.5.cloned.1.call-start = ((), (), s32[]{:S(2)}) async-start(), calls=%async_computation.4 | async-start | bytes 4325376 | tf_op jit(solution)/shard_map/reduce_scatter | solution.py:69
  246.1 177.9 %copy-start.1 = (bf16[128,128]{1,0:T(8,128)(2,1)S(1)}, bf16[128,128]{1,0:T(8,128)(2,1)}, u32[]{:S(2)}) copy-start(bf16[128,128]{1,0:T(8,128)(2,1)} %param.12) | copy-start | bytes 98308
  246.1 423.3 %all-reduce.2.cloned.1.call-start = ((), (), s32[]{:S(2)}) async-start(), calls=%async_computation.5 | async-start | bytes 131072 | tf_op jit(solution)/shard_map/psum | solution.py:79
Sparse Core Ops, SparseCore 0:
  11.4 84.1 all-gather.1
  118.2 68.8 reduce-scatter.2
  246.2 175.9 reduce-scatter.4
  429.0 240.2 all-reduce.1
where the time goes:
time: 679 us; the launch traced here: 677 us
  waiting for transfers between devices  574 us (85%)
  matrix products  33.5 us (5%)
  local copies, waits for them, and re-layouts  24.6 us (4%)
  blocking collectives  22.5 us (3%)
  between operations  14.5 us (2%)
  other arithmetic  8.02 us (1%)
    psum x1, waiting for transfers between devices, local(): grad_weight = lax.psum(weight_part, ('rep', 'row'))  244 us
    reduce_scatter x1, waiting for transfers between devices, local(): lax.psum_scatter(slab_part.reshape(col_blocks * block, feats), 'row', sca...  176 us
    all_gather x1, waiting for transfers between devices, local(): slab = lax.all_gather(xw, 'row', axis=0, tiled=True)  85.3 us
    reduce_scatter x1, waiting for transfers between devices, local(): zmine = lax.psum_scatter(zpart, 'rep', scatter_dimension=0, tiled=True)  68.9 us
    all_gather x1, blocking collectives, local(): grad_full = lax.all_gather(grad_pre, 'rep', axis=0, tiled=True)  22.5 us
    dot_general x6, matrix products, step(): jnp.einsum('qt,taf->qaf', select.astype(jnp.float32), products)  17.9 us
  transfers between devices with their start and end apart: 4, of which 4 were waited for; matrix products, arithmetic and copies ran while one was open for 0% of the time, Pallas kernels for 0%

commit v1 on v0

v1 whole, which is shorter than its diff:
```python
import jax
import jax.numpy as jnp
from jax import lax
from jax.experimental import pallas as pl
from jax.experimental.pallas import tpu as pltpu
from jax.sharding import Mesh, PartitionSpec as P

CHUNK = 32
BLOCK = 128
ROWS = 16
COLS = 64
HALF = COLS // 2
SIZES = (4, 2, 2, 8, 2)
AXES = ("x", "ylo", "yhi", "z", "core")
REP = ("x", "ylo")
COLUMN = ("yhi", "z")
ROW = ("yhi", "z", "core")
SWAP = ((0, 1), (1, 0))


def tile_copy(tiles, buffer, sems, chunk):
    span = pl.ds(chunk * CHUNK, CHUNK)
    return pltpu.make_async_copy(tiles.at[span], buffer.at[span], sems.at[chunk])


def forward_kernel(count, rows, cols, tiles, own, other, out, buffer, xs, acc, sems, xsems):
    chunks = (count[0] + CHUNK - 1) // CHUNK
    first = pltpu.make_async_copy(own, xs.at[pl.ds(0, HALF)], xsems.at[0])
    second = pltpu.make_async_copy(other, xs.at[pl.ds(HALF, HALF)], xsems.at[1])
    first.start()
    second.start()

    @pl.loop(0, chunks)
    def _(c):
        tile_copy(tiles, buffer, sems, c).start()

    acc[...] = jnp.zeros_like(acc)
    first.wait()
    second.wait()

    @pl.loop(0, chunks)
    def _(c):
        tile_copy(tiles, buffer, sems, c).wait()
        base = c * CHUNK
        products = [
            jnp.dot(buffer[base + u], xs[cols[base + u]], preferred_element_type=jnp.float32)
            for u in range(CHUNK)
        ]
        for u in range(CHUNK):
            acc[rows[base + u]] += products[u]

    out[...] = acc[:ROWS].astype(jnp.bfloat16)


def backward_kernel(count, rows, cols, tiles, grads, own, other, buffer, acc, sems):
    chunks = (count[0] + CHUNK - 1) // CHUNK

    @pl.loop(0, chunks)
    def _(c):
        tile_copy(tiles, buffer, sems, c).start()

    acc[...] = jnp.zeros_like(acc)

    @pl.loop(0, chunks)
    def _(c):
        tile_copy(tiles, buffer, sems, c).wait()
        base = c * CHUNK
        products = [
            jnp.dot(grads[rows[base + u]], buffer[base + u], preferred_element_type=jnp.float32)
            for u in range(CHUNK)
        ]
        for u in range(CHUNK):
            acc[cols[base + u]] += products[u]

    own[...] = acc[:HALF]
    other[...] = acc[HALF:COLS].astype(jnp.bfloat16)


SMEM = pl.BlockSpec(memory_space=pltpu.SMEM)
VMEM = pl.BlockSpec(memory_space=pltpu.VMEM)
HBM = pl.BlockSpec(memory_space=pl.ANY)


def forward_pass(count, rows, cols, tiles, own, other):
    cap = tiles.shape[0]
    return pl.pallas_call(
        forward_kernel,
        out_shape=jax.ShapeDtypeStruct((ROWS, BLOCK, BLOCK), jnp.bfloat16),
        in_specs=[SMEM, SMEM, SMEM, HBM, HBM, HBM],
        out_specs=VMEM,
        scratch_shapes=[
            pltpu.VMEM((cap, BLOCK, BLOCK), jnp.bfloat16),
            pltpu.VMEM((COLS, BLOCK, BLOCK), jnp.bfloat16),
            pltpu.VMEM((ROWS + 1, BLOCK, BLOCK), jnp.float32),
            pltpu.SemaphoreType.DMA((cap // CHUNK,)),
            pltpu.SemaphoreType.DMA((2,)),
        ],
        compiler_params=pltpu.CompilerParams(vmem_limit_bytes=32 << 20),
        cost_estimate=pl.CostEstimate(flops=1 << 30, bytes_accessed=11 << 20, transcendentals=0),
        name="forward_tiles",
    )(count, rows, cols, tiles, own, other)


def backward_pass(count, rows, cols, tiles, grads):
    cap = tiles.shape[0]
    return pl.pallas_call(
        backward_kernel,
        out_shape=(
            jax.ShapeDtypeStruct((HALF, BLOCK, BLOCK), jnp.float32),
            jax.ShapeDtypeStruct((HALF, BLOCK, BLOCK), jnp.bfloat16),
        ),
        in_specs=[SMEM, SMEM, SMEM, HBM, VMEM],
        out_specs=(VMEM, VMEM),
        scratch_shapes=[
            pltpu.VMEM((cap, BLOCK, BLOCK), jnp.bfloat16),
            pltpu.VMEM((COLS + 1, BLOCK, BLOCK), jnp.float32),
            pltpu.SemaphoreType.DMA((cap // CHUNK,)),
        ],
        compiler_params=pltpu.CompilerParams(vmem_limit_bytes=32 << 20),
        cost_estimate=pl.CostEstimate(flops=1 << 30, bytes_accessed=12 << 20, transcendentals=0),
        name="backward_tiles",
    )(count, rows, cols, tiles, grads)


def spread(block, axes):
    n = lax.axis_size(axes)
    return lax.all_to_all(jnp.broadcast_to(block[None], (n, *block.shape)), axes, 0, 0)


def local(features, weight, cotangent, tiles, row_ids, col_ids, counts):
    x = features[0]
    nodes, feats = x.shape
    tiles = tiles[0, 0]
    cap = tiles.shape[0]
    count = counts[0]
    rows = row_ids[0, 0]
    core = lax.axis_index("core")

    cols = col_ids[0, 0]
    col_place = (((cols // 2) % 2) ^ core) * HALF + (cols // 4) * 2 + cols % 2
    valid = jnp.arange(cap, dtype=jnp.int32) < count[0]
    rows_into = jnp.where(valid, rows, ROWS)
    cols_into = jnp.where(valid, col_place, COLS)

    own_x = spread(x, COLUMN).reshape(HALF, BLOCK, feats)
    other_x = lax.ppermute(own_x, "core", SWAP)
    y_part = forward_pass(count, rows_into, col_place, tiles, own_x, other_x)

    reps = lax.axis_size(REP)
    y_parts = lax.all_to_all(y_part.reshape(reps, nodes, feats), REP, 0, 0)
    y = jnp.sum(y_parts.astype(jnp.float32), axis=0)
    z = jnp.dot(y, weight.astype(jnp.float32), precision=lax.Precision.HIGHEST)
    sigma = jax.nn.sigmoid(z)
    hidden = (z * sigma).astype(jnp.bfloat16)
    grad_pre = (
        cotangent[0].astype(jnp.float32) * sigma * (1.0 + z * (1.0 - sigma))
    ).astype(jnp.bfloat16)

    weight_part = lax.dot_general(
        y.astype(jnp.bfloat16), grad_pre, (((0,), (0,)), ((), ())),
        preferred_element_type=jnp.float32,
    ).astype(jnp.bfloat16).reshape(reps, feats // reps, feats)
    grad_t = jnp.swapaxes(grad_pre.reshape(nodes // BLOCK, BLOCK, feats), 1, 2)
    grad_t = grad_t.reshape(1, nodes, feats)
    sent = jnp.concatenate(
        [jnp.broadcast_to(grad_t, (reps, nodes, feats)), weight_part], axis=1
    )
    got = lax.all_to_all(sent, REP, 0, 0)
    grads = got[:, :nodes].reshape(ROWS, feats, BLOCK)
    weight_rep = jnp.sum(got[:, nodes:].astype(jnp.float32), axis=0)
    weight_chip = weight_rep + lax.ppermute(weight_rep, "core", SWAP)

    slab_own, slab_other = backward_pass(count, rows, cols_into, tiles, grads)
    slab_chip = slab_own + lax.ppermute(slab_other, "core", SWAP).astype(jnp.float32)
    peers = lax.axis_size(COLUMN)
    sent = jnp.concatenate(
        [
            slab_chip.astype(jnp.bfloat16).reshape(peers, nodes, feats),
            jnp.broadcast_to(
                weight_chip.astype(jnp.bfloat16)[None], (peers, *weight_chip.shape)
            ),
        ],
        axis=1,
    )
    got = lax.all_to_all(sent, COLUMN, 0, 0).astype(jnp.float32)
    total = jnp.sum(got, axis=0)
    grad_xw_t = total[:nodes].astype(jnp.bfloat16).reshape(nodes // BLOCK, feats, BLOCK)
    grad_feats = jnp.einsum(
        "hfn,kf->hnk", grad_xw_t, weight, preferred_element_type=jnp.float32
    ).astype(jnp.bfloat16)
    grad_weight = spread(total[nodes:], REP).reshape(feats, feats)
    return hidden[None], grad_feats.reshape(1, nodes, feats), grad_weight


def solution(mesh):
    mesh = Mesh(mesh.devices.reshape(SIZES), AXES)
    placed = P(ROW, REP)
    return jax.shard_map(
        local,
        mesh=mesh,
        in_specs=(placed, P(), placed, placed, placed, placed, placed),
        out_specs=(placed, placed, P()),
        check_vma=False,
    )
```

time: 679 us -> 140 us (0.21)
  the two profiles are of different devices: /device:TPU:1 before, /device:TPU:8 now
where the time goes in v1:
time: 140 us; the launch traced here: 139 us
  blocking collectives  107 us (76%)
  local copies, waits for them, and re-layouts  9.35 us (7%)
  waiting for transfers between devices  8.26 us (6%)
  starting transfers between devices  6.16 us (4%)
  Pallas kernels  4.32 us (3%)
  matrix products  1.9 us (1%)
  between operations  1.47 us (1%)
    all_to_all x1, blocking collectives, local(): got = lax.all_to_all(sent, COLUMN, 0, 0).astype(jnp.float32)  40.6 us
    all_to_all x1, blocking collectives, spread(): lax.all_to_all(jnp.broadcast_to(block[None], (n, *block.shape)), axes, 0, 0)  38.5 us
    all_to_all x1, blocking collectives, local(): y_parts = lax.all_to_all(y_part.reshape(reps, nodes, feats), REP, 0, 0)  16.2 us
    all_to_all x1, blocking collectives, local(): got = lax.all_to_all(sent, REP, 0, 0)  11.4 us
    unnamed x13, local copies, waits for them, and re-layouts  7.41 us
    all_to_all x1, starting transfers between devices, spread(): lax.all_to_all(jnp.broadcast_to(block[None], (n, *block.shape)), axes, 0, 0)  5.48 us
    all_to_all x1, waiting for transfers between devices, spread(): lax.all_to_all(jnp.broadcast_to(block[None], (n, *block.shape)), axes, 0, 0)  4.24 us
  transfers between devices with their start and end apart: 4, of which 3 were waited for; matrix products, arithmetic and copies ran while one was open for 1% of the time, Pallas kernels for 0%

profile of v1, /device:TPU:8, one launch (start us, length us, event | category | flops | bytes accessed | tf_op | source)
XLA Modules:
  0.0 138.9 jit_solution(10968146748681832934)
XLA Ops:
  0.6 0.0 copy-start
  0.6 0.0 copy-start.4
  0.7 0.0 copy-start.3
  0.7 1.1 broadcast_in_dim.38
  1.7 38.5 %all_to_all.25 = bf16[16,256,128]{2,1,0:T(8,128)(2,1)S(1)} all-to-all(bf16[16,256,128]{2,1,0:T(8,128)(2,1)S(1)} %broadcast_in_dim.38), channel_id=1, replica_groups=mesh['x'=4,'ylo'=2,'yhi'=2,'z'=8,'core'=2] {'yhi','z'}, dimensions={0} | all-to-all | bytes 2097152 | tf_op jit(solution)/shard_map/all_to_all | solution.py:127
  40.3 0.0 collective-permute-start
  41.0 2.0 %collective-permute-done.other = bf16[32,128,128]{2,1,0:T(8,128)(2,1)S(1)} collective-permute-done((bf16[32,128,128]{2,1,0:T(8,128)(2,1)S(1)}, bf16[32,128,128]{2,1,0:T(8,128)(2,1)S(1)}, u32[]{:S(2)}, u32[]{:S(2)}) %collective-permute-start) | collective-permute-done | bytes 1048608 | tf_op jit(solution)/shard_map/ppermute | solution.py:146
  42.9 3.4 %copy-done.1 = bf16[1,1,256,128,128]{4,3,2,1,0:T(8,128)(2,1)S(1)} copy-done((bf16[1,1,256,128,128]{4,3,2,1,0:T(8,128)(2,1)S(1)}, bf16[1,1,256,128,128]{4,3,2,1,0:T(8,128)(2,1)}, u32[]{:S(2)}) %copy-start.1) | copy-done | bytes 8388632
  46.3 2.0 %forward_tiles.1 = bf16[16,128,128]{2,1,0:T(8,128)(2,1)S(1)} custom-call(s32[1]{0:T(128)} %bitcast.30.count, s32[256]{0:T(256)S(1)} %get-tuple-element.11.rows, s32[256]{0:T(256)S(1)} %get-tuple-element.8.cols, bf16[256,128,128]{2,1,0:T(8,128)(2,1)S(1)} %bitcast.33, bf16[32,128,128]{2,1,0:T(8,128)(2,1)S(1)} %bitcast.36, ...), custom_call_target="tpu_custom_call" | custom-call | flops 1073741824 | bytes 11534336 | tf_op jit(solution)/shard_map/forward_tiles/pallas_call | solution.py:86
  48.4 16.2 %all_to_all.26 = bf16[8,256,128]{2,1,0:T(8,128)(2,1)S(1)} all-to-all(bf16[8,256,128]{2,1,0:T(8,128)(2,1)S(1)} %bitcast.38), channel_id=1, replica_groups=mesh['x'=4,'ylo'=2,'yhi'=2,'z'=8,'core'=2] {'x','ylo'}, dimensions={0} | all-to-all | bytes 1048576 | tf_op jit(solution)/shard_map/all_to_all | solution.py:150
  64.5 0.1 convert_reduce_fusion.1
  64.6 0.9 fusion.1
  65.5 0.2 convolution_convert_fusion.1
  65.7 0.1 copy.10
  65.8 0.1 broadcast_in_dim.42
  65.9 11.4 %all_to_all.27 = bf16[8,272,128]{2,1,0:T(8,128)(2,1)S(1)} all-to-all(bf16[8,272,128]{2,1,0:T(8,128)(2,1)S(1)} %pad_maximum_fusion.1), channel_id=1, replica_groups=mesh['x'=4,'ylo'=2,'yhi'=2,'z'=8,'core'=2] {'x','ylo'}, dimensions={0} | all-to-all | bytes 1114112 | tf_op jit(solution)/shard_map/all_to_all | solution.py:168
  77.4 0.0 copy-start.2
  77.4 3.4 %copy-done.2 = bf16[1,1,256,128,128]{4,3,2,1,0:T(8,128)(2,1)S(1)} copy-done((bf16[1,1,256,128,128]{4,3,2,1,0:T(8,128)(2,1)S(1)}, bf16[1,1,256,128,128]{4,3,2,1,0:T(8,128)(2,1)}, u32[]{:S(2)}) %copy-start.2) | copy-done | bytes 8388632
  80.8 2.3 %backward_tiles.1 = (f32[32,128,128]{2,1,0:T(8,128)S(1)}, bf16[32,128,128]{2,1,0:T(8,128)(2,1)S(1)}) custom-call(s32[1]{0:T(128)} %bitcast.31.count, s32[256]{0:T(256)S(1)} %bitcast.40, s32[256]{0:T(256)S(1)} %get-tuple-element.7.cols, bf16[256,128,128]{2,1,0:T(8,128)(2,1)S(1)} %bitcast.34, bf16[16,128,128]{2,1,0:T(8,128)(2,1)S(1)} %bitcast.37), custom_call_target="tpu_custom_call" | custom-call | flops 1073741824 | bytes 12582912 | tf_op jit(solution)/shard_map/backward_tiles/pallas_call | solution.py:106
  83.0 0.1 collective-permute-start.1
  83.2 0.6 collective-permute-start.2
  83.7 2.1 %collective-permute-done.2 = f32[16,128]{1,0:T(8,128)S(1)} collective-permute-done((f32[16,128]{1,0:T(8,128)S(1)}, f32[16,128]{1,0:T(8,128)S(1)}, u32[]{:S(2)}, u32[]{:S(2)}) %collective-permute-start.2) | collective-permute-done | bytes 8224 | tf_op jit(solution)/shard_map/ppermute | solution.py:171
  85.8 0.0 collective-permute-done.1
  85.8 0.3 add_convert_fusion
  86.2 0.1 pad_maximum_fusion
  86.3 40.6 %all_to_all.28 = bf16[16,272,128]{2,1,0:T(8,128)(2,1)S(1)} all-to-all(bf16[16,272,128]{2,1,0:T(8,128)(2,1)S(1)} %pad_maximum_fusion), channel_id=1, replica_groups=mesh['x'=4,'ylo'=2,'yhi'=2,'z'=8,'core'=2] {'yhi','z'}, dimensions={0} | all-to-all | bytes 2228224 | tf_op jit(solution)/shard_map/all_to_all | solution.py:185
  126.9 0.2 convert_reduce_fusion
  127.1 0.6 broadcast_in_dim.44
  127.7 5.5 %all-to-all-start.4 = ((f32[8,16,128]{2,1,0:T(8,128)}), f32[8,16,128]{2,1,0:T(8,128)S(1)}, u32[]{:S(2)}, u32[]{:S(2)}) async-start(f32[8,16,128]{2,1,0:T(8,128)} %broadcast_in_dim.44), calls=%async_computation.4 | async-start | bytes 131072 | tf_op jit(solution)/shard_map/all_to_all | solution.py:127
  133.2 0.8 convolution_convert_fusion
  134.0 4.2 %all-to-all-done.4 = f32[8,16,128]{2,1,0:T(8,128)S(1)} async-done(((f32[8,16,128]{2,1,0:T(8,128)}), f32[8,16,128]{2,1,0:T(8,128)S(1)}, u32[]{:S(2)}, u32[]{:S(2)}) %all-to-all-start.4) | async-done | bytes 65568 | tf_op jit(solution)/shard_map/all_to_all | solution.py:127
  138.2 0.6 copy.15
  (14 shorter events, 0.1 us)
Async XLA Ops:
  0.6 64.0 %copy-start = (bf16[128,128]{1,0:T(8,128)(2,1)S(1)}, bf16[128,128]{1,0:T(8,128)(2,1)}, u32[]{:S(2)}) copy-start(bf16[128,128]{1,0:T(8,128)(2,1)} %param.8) | copy-start | bytes 98308
  0.6 40.3 %copy-start.4 = (s32[1,1,256]{2,1,0:T(1,128)S(1)}, s32[1,1,256]{2,1,0:T(1,128)}, u32[]{:S(2)}) copy-start(s32[1,1,256]{2,1,0:T(1,128)} %param.12) | copy-start | bytes 3076
  0.7 40.3 %copy-start.3 = (s32[1,1,256]{2,1,0:T(1,128)S(1)}, s32[1,1,256]{2,1,0:T(1,128)}, u32[]{:S(2)}) copy-start(s32[1,1,256]{2,1,0:T(1,128)} %param.11) | copy-start | bytes 3076
  40.3 2.7 %collective-permute-start = (bf16[32,128,128]{2,1,0:T(8,128)(2,1)S(1)}, bf16[32,128,128]{2,1,0:T(8,128)(2,1)S(1)}, u32[]{:S(2)}, u32[]{:S(2)}) collective-permute-start(bf16[32,128,128]{2,1,0:T(8,128)(2,1)S(1)} %bitcast.35), channel_id=1, source_target_pairs={{0,1},{1,0},{2,3},{3,2},{4,5},{5,4},{6,7},{7,6},{8,9},{9,8},{10,11... | collective-permute-start | bytes 3145736 | tf_op jit(solution)/shard_map/ppermute | solution.py:146
  42.9 3.4 %copy-start.1 = (bf16[1,1,256,128,128]{4,3,2,1,0:T(8,128)(2,1)S(1)}, bf16[1,1,256,128,128]{4,3,2,1,0:T(8,128)(2,1)}, u32[]{:S(2)}) copy-start(bf16[1,1,256,128,128]{4,3,2,1,0:T(8,128)(2,1)} %param.10) | copy-start | bytes 25165828
  46.3 18.3 %copy-start.5 = (bf16[1,256,128]{2,1,0:T(8,128)(2,1)S(1)}, bf16[1,256,128]{2,1,0:T(8,128)(2,1)}, u32[]{:S(2)}) copy-start(bf16[1,256,128]{2,1,0:T(8,128)(2,1)} %param.9) | copy-start | bytes 196612
  77.4 3.4 %copy-start.2 = (bf16[1,1,256,128,128]{4,3,2,1,0:T(8,128)(2,1)S(1)}, bf16[1,1,256,128,128]{4,3,2,1,0:T(8,128)(2,1)}, u32[]{:S(2)}) copy-start(bf16[1,1,256,128,128]{4,3,2,1,0:T(8,128)(2,1)} %param.10) | copy-start | bytes 25165828
  83.0 2.8 %collective-permute-start.1 = (bf16[32,128,128]{2,1,0:T(8,128)(2,1)S(1)}, bf16[32,128,128]{2,1,0:T(8,128)(2,1)S(1)}, u32[]{:S(2)}, u32[]{:S(2)}) collective-permute-start(bf16[32,128,128]{2,1,0:T(8,128)(2,1)S(1)} %get-tuple-element.6), channel_id=1, source_target_pairs={{0,1},{1,0},{2,3},{3,2},{4,5},{5,4},{6,7},{7,6},{8,9},{9,8},{10,11... | collective-permute-start | bytes 3145736 | tf_op jit(solution)/shard_map/ppermute | solution.py:174
  83.2 2.6 %collective-permute-start.2 = (f32[16,128]{1,0:T(8,128)S(1)}, f32[16,128]{1,0:T(8,128)S(1)}, u32[]{:S(2)}, u32[]{:S(2)}) collective-permute-start(f32[16,128]{1,0:T(8,128)S(1)} %convert_reduce_fusion.2), channel_id=1, source_target_pairs={{0,1},{1,0},{2,3},{3,2},{4,5},{5,4},{6,7},{7,6},{8,9},{9,8},{10,11... | collective-permute-start | bytes 24584 | tf_op jit(solution)/shard_map/ppermute | solution.py:171
  127.7 10.5 %all-to-all-start.4 = ((f32[8,16,128]{2,1,0:T(8,128)}), f32[8,16,128]{2,1,0:T(8,128)S(1)}, u32[]{:S(2)}, u32[]{:S(2)}) async-start(f32[8,16,128]{2,1,0:T(8,128)} %broadcast_in_dim.44), calls=%async_computation.4 | async-start | bytes 131072 | tf_op jit(solution)/shard_map/all_to_all | solution.py:127

commit v2 on v1

v2 whole, which is shorter than its diff:
```python
import jax
import jax.numpy as jnp
from jax import lax
from jax.experimental import pallas as pl
from jax.experimental.pallas import tpu as pltpu
from jax.sharding import Mesh, PartitionSpec as P

CHUNK = 32
BLOCK = 128
ROWS = 16
COLS = 64
PART = COLS // 4
SPAN = PART * BLOCK
EXTRA = BLOCK // 2
SIZES = (4, 2, 2, 4, 2, 2)
AXES = ("x", "ylo", "yhi", "zq", "zp", "core")
REP = ("x", "ylo")
ROW = ("yhi", "zq", "zp", "core")
PARITY = ("yhi", "zq")
ALONG = ("zq", "zp", "core")
SWAP = ((0, 1), (1, 0))
NEXT = tuple((2 * z, 2 * ((z + 1) % 8)) for z in range(8)) + tuple(
    (2 * z + 1, 2 * ((z + 7) % 8) + 1) for z in range(8)
)


def tile_copy(tiles, buffer, sems, chunk):
    span = pl.ds(chunk * CHUNK, CHUNK)
    return pltpu.make_async_copy(tiles.at[span], buffer.at[span], sems.at[chunk])


def forward_kernel(count, rows, cols, tiles, x0, x1, x2, x3, out, buffer, xs, acc, sems, xsems):
    chunks = (count[0] + CHUNK - 1) // CHUNK
    moves = [
        pltpu.make_async_copy(source, xs.at[pl.ds(k * PART, PART)], xsems.at[k])
        for k, source in enumerate((x0, x1, x2, x3))
    ]
    for move in moves:
        move.start()

    @pl.loop(0, chunks)
    def _(c):
        tile_copy(tiles, buffer, sems, c).start()

    acc[...] = jnp.zeros_like(acc)
    for move in moves:
        move.wait()

    @pl.loop(0, chunks)
    def _(c):
        tile_copy(tiles, buffer, sems, c).wait()
        base = c * CHUNK
        products = [
            jnp.dot(buffer[base + u], xs[cols[base + u]], preferred_element_type=jnp.float32)
            for u in range(CHUNK)
        ]
        for u in range(CHUNK):
            acc[rows[base + u]] += products[u]

    out[...] = acc[:ROWS].astype(jnp.bfloat16)


def backward_kernel(
    count, core, rows, cols, tiles, got, own, other, buffer, acc, weight_sum, sems
):
    chunks = (count[0] + CHUNK - 1) // CHUNK

    @pl.loop(0, chunks)
    def _(c):
        tile_copy(tiles, buffer, sems, c).start()

    acc[...] = jnp.zeros_like(acc)
    reps = got.shape[0]
    nodes = got.shape[1] - BLOCK
    weight_sum[...] = sum(got[k, nodes:].astype(jnp.float32) for k in range(reps))

    @pl.loop(0, chunks)
    def _(c):
        tile_copy(tiles, buffer, sems, c).wait()
        base = c * CHUNK
        products = []
        for u in range(CHUNK):
            row = rows[base + u]
            grad = got[row // 2, pl.ds(pl.multiple_of((row % 2) * BLOCK, BLOCK), BLOCK), :]
            products.append(
                jnp.dot(grad, buffer[base + u], preferred_element_type=jnp.float32)
            )
        for u in range(CHUNK):
            acc[cols[base + u]] += products[u]

    feats = own.shape[1]
    mine = core[0]
    own[:SPAN] = acc[2 * PART : 3 * PART].reshape(SPAN, feats)
    own[SPAN : 2 * SPAN] = acc[:PART].reshape(SPAN, feats)
    own[2 * SPAN :] = weight_sum[pl.ds(pl.multiple_of(mine * EXTRA, EXTRA), EXTRA), :]
    other[:SPAN] = acc[3 * PART : 4 * PART].reshape(SPAN, feats).astype(jnp.bfloat16)
    other[SPAN : 2 * SPAN] = acc[PART : 2 * PART].reshape(SPAN, feats).astype(jnp.bfloat16)
    other[2 * SPAN :] = weight_sum[
        pl.ds(pl.multiple_of((1 - mine) * EXTRA, EXTRA), EXTRA), :
    ].astype(jnp.bfloat16)


def away_kernel(own, other, out):
    for at, to, size in ((0, 0, SPAN), (2 * SPAN, SPAN, EXTRA)):
        total = own[pl.ds(at, size), :] + other[pl.ds(at, size), :].astype(jnp.float32)
        out[pl.ds(to, size), :] = total.astype(jnp.bfloat16)


def home_kernel(own, other, came, out):
    peers = out.shape[0]
    nodes = out.shape[1] - EXTRA
    weight = (
        own[2 * SPAN :] + other[2 * SPAN :].astype(jnp.float32) + came[SPAN:].astype(jnp.float32)
    ).astype(jnp.bfloat16)
    for k in range(peers):
        here = pl.ds(SPAN + k * nodes, nodes)
        total = own[here, :] + other[here, :].astype(jnp.float32)
        total = total + came[pl.ds(k * nodes, nodes), :].astype(jnp.float32)
        out[k, :nodes] = total.astype(jnp.bfloat16)
        out[k, nodes:] = weight


SMEM = pl.BlockSpec(memory_space=pltpu.SMEM)
VMEM = pl.BlockSpec(memory_space=pltpu.VMEM)
ANY = pl.BlockSpec(memory_space=pl.ANY)


def forward_pass(count, rows, cols, tiles, parts):
    cap = tiles.shape[0]
    return pl.pallas_call(
        forward_kernel,
        out_shape=jax.ShapeDtypeStruct((ROWS, BLOCK, BLOCK), jnp.bfloat16),
        in_specs=[SMEM, SMEM, SMEM, ANY, ANY, ANY, ANY, ANY],
        out_specs=VMEM,
        scratch_shapes=[
            pltpu.VMEM((cap, BLOCK, BLOCK), jnp.bfloat16),
            pltpu.VMEM((COLS, BLOCK, BLOCK), jnp.bfloat16),
            pltpu.VMEM((ROWS + 1, BLOCK, BLOCK), jnp.float32),
            pltpu.SemaphoreType.DMA((cap // CHUNK,)),
            pltpu.SemaphoreType.DMA((4,)),
        ],
        compiler_params=pltpu.CompilerParams(vmem_limit_bytes=20 << 20),
        cost_estimate=pl.CostEstimate(flops=1 << 30, bytes_accessed=11 << 20, transcendentals=0),
        name="forward_tiles",
    )(count, rows, cols, pltpu.with_memory_space_constraint(tiles, pltpu.HBM), *parts)


def backward_pass(count, core, rows, cols, tiles, got):
    cap = tiles.shape[0]
    feats = got.shape[2]
    return pl.pallas_call(
        backward_kernel,
        out_shape=(
            jax.ShapeDtypeStruct((2 * SPAN + EXTRA, feats), jnp.float32),
            jax.ShapeDtypeStruct((2 * SPAN + EXTRA, feats), jnp.bfloat16),
        ),
        in_specs=[SMEM, SMEM, SMEM, SMEM, ANY, VMEM],
        out_specs=(VMEM, VMEM),
        scratch_shapes=[
            pltpu.VMEM((cap, BLOCK, BLOCK), jnp.bfloat16),
            pltpu.VMEM((COLS + 1, BLOCK, BLOCK), jnp.float32),
            pltpu.VMEM((BLOCK, BLOCK), jnp.float32),
            pltpu.SemaphoreType.DMA((cap // CHUNK,)),
        ],
        compiler_params=pltpu.CompilerParams(vmem_limit_bytes=20 << 20),
        cost_estimate=pl.CostEstimate(flops=1 << 30, bytes_accessed=12 << 20, transcendentals=0),
        name="backward_tiles",
    )(count, core, rows, cols, pltpu.with_memory_space_constraint(tiles, pltpu.HBM), got)


def merge(kernel, shape, *arrays):
    return pl.pallas_call(
        kernel,
        out_shape=jax.ShapeDtypeStruct(shape, jnp.bfloat16),
        in_specs=[VMEM] * len(arrays),
        out_specs=VMEM,
        compiler_params=pltpu.CompilerParams(vmem_limit_bytes=16 << 20),
        cost_estimate=pl.CostEstimate(flops=1 << 20, bytes_accessed=4 << 20, transcendentals=0),
        name=kernel.__name__,
    )(*arrays)


def spread(block, axes):
    n = lax.axis_size(axes)
    return lax.all_to_all(jnp.broadcast_to(block[None], (n, *block.shape)), axes, 0, 0)


def local(features, weight, cotangent, tiles, row_ids, col_ids, counts):
    x = features[0]
    nodes, feats = x.shape
    tiles = tiles[0, 0]
    cap = tiles.shape[0]
    count = counts[0]
    rows = row_ids[0, 0]
    core = lax.axis_index("core")

    cols = col_ids[0, 0]
    z = (cols // 4) % 8
    part = ((z % 2) ^ lax.axis_index("zp")) * 2 + (((cols // 2) % 2) ^ core)
    place = part * PART + ((cols // 32) * 4 + z // 2) * 2 + cols % 2
    valid = jnp.arange(cap, dtype=jnp.int32) < count[0]
    rows_into = jnp.where(valid, rows, ROWS)
    place_into = jnp.where(valid, place, COLS)

    own = spread(x, PARITY)
    beside = lax.ppermute(own, ALONG, NEXT)
    own_other = lax.ppermute(own, "core", SWAP)
    beside_other = lax.ppermute(beside, "core", SWAP)
    parts = [p.reshape(PART, BLOCK, feats) for p in (own, own_other, beside, beside_other)]
    y_part = forward_pass(count, rows_into, place, tiles, parts)

    reps = lax.axis_size(REP)
    y_parts = lax.all_to_all(y_part.reshape(reps, nodes, feats), REP, 0, 0)
    y = jnp.sum(y_parts.astype(jnp.float32), axis=0)
    z = jnp.dot(y, weight.astype(jnp.float32), precision=lax.Precision.HIGHEST)
    sigma = jax.nn.sigmoid(z)
    hidden = (z * sigma).astype(jnp.bfloat16)
    grad_pre = (
        cotangent[0].astype(jnp.float32) * sigma * (1.0 + z * (1.0 - sigma))
    ).astype(jnp.bfloat16)

    weight_part = lax.dot_general(
        y.astype(jnp.bfloat16), grad_pre, (((0,), (0,)), ((), ())),
        preferred_element_type=jnp.float32,
    ).astype(jnp.bfloat16)
    grad_t = jnp.swapaxes(grad_pre.reshape(nodes // BLOCK, BLOCK, feats), 1, 2)
    got = spread(jnp.concatenate([grad_t.reshape(nodes, feats), weight_part]), REP)

    slab_own, slab_other = backward_pass(count, core[None], rows, place_into, tiles, got)
    slab_other = lax.ppermute(slab_other, "core", SWAP)
    away = merge(away_kernel, (SPAN + EXTRA, feats), slab_own, slab_other)
    came = lax.ppermute(away, ALONG, NEXT)
    peers = lax.axis_size(PARITY)
    sent = merge(home_kernel, (peers, nodes + EXTRA, feats), slab_own, slab_other, came)
    got = lax.all_to_all(sent, PARITY, 0, 0)
    total = jnp.sum(got.astype(jnp.float32), axis=0)
    grad_xw_t = total[:nodes].astype(jnp.bfloat16).reshape(nodes // BLOCK, feats, BLOCK)
    grad_feats = jnp.einsum(
        "hfn,kf->hnk", grad_xw_t, weight, preferred_element_type=jnp.float32
    ).astype(jnp.bfloat16)
    mine = total[nodes:]
    theirs = lax.ppermute(mine, "core", SWAP)
    grad_weight = jnp.where(
        core == 0, jnp.concatenate([mine, theirs]), jnp.concatenate([theirs, mine])
    )
    return hidden[None], grad_feats.reshape(1, nodes, feats), grad_weight


def solution(mesh):
    mesh = Mesh(mesh.devices.reshape(SIZES), AXES)
    placed = P(ROW, REP)
    return jax.shard_map(
        local,
        mesh=mesh,
        in_specs=(placed, P(), placed, placed, placed, placed, placed),
        out_specs=(placed, placed, P()),
        check_vma=False,
    )
```

time: 140 us -> 124 us (0.89)
  the two profiles are of different devices: /device:TPU:8 before, /device:TPU:1 now
where the time goes in v2:
time: 124 us
  blocking collectives  55 us (44%)
  waiting for transfers between devices  33.6 us (27%)
  starting transfers between devices  21.8 us (18%)
  Pallas kernels  8.27 us (7%)
  matrix products  1.9 us (2%)
  between operations  1.43 us (1%)
    all_to_all x2, blocking collectives, spread(): lax.all_to_all(jnp.broadcast_to(block[None], (n, *block.shape)), axes, 0, 0)  40.8 us
    all_to_all x1, waiting for transfers between devices, local(): got = lax.all_to_all(sent, PARITY, 0, 0)  20.1 us
    all_to_all x1, blocking collectives, local(): y_parts = lax.all_to_all(y_part.reshape(reps, nodes, feats), REP, 0, 0)  14.1 us
    ppermute x1, waiting for transfers between devices, local(): came = lax.ppermute(away, ALONG, NEXT)  6.72 us
    ppermute x1, starting transfers between devices, local(): own_other = lax.ppermute(own, 'core', SWAP)  5.11 us
    all_to_all x1, starting transfers between devices, local(): got = lax.all_to_all(sent, PARITY, 0, 0)  5.03 us
    ppermute x1, starting transfers between devices, local(): beside_other = lax.ppermute(beside, 'core', SWAP)  4.24 us
    ppermute x1, waiting for transfers between devices, local(): beside = lax.ppermute(own, ALONG, NEXT)  3.6 us
  transfers between devices with their start and end apart: 7, of which 5 were waited for; matrix products, arithmetic and copies ran while one was open for 1% of the time, Pallas kernels for 0%

profile of v2, /device:TPU:1, one launch (start us, length us, event | category | flops | bytes accessed | tf_op | source)
XLA Modules:
  0.0 124.0 jit_solution(6110211104423793388)
XLA Ops:
  0.6 0.0 copy-start
  0.7 0.9 broadcast_in_dim.28
  1.6 27.0 %all_to_all.20 = bf16[8,256,128]{2,1,0:T(8,128)(2,1)S(1)} all-to-all(bf16[8,256,128]{2,1,0:T(8,128)(2,1)S(1)} %broadcast_in_dim.28), channel_id=1, replica_groups=mesh['x'=4,'ylo'=2,'yhi'=2,'zq'=4,'zp'=2,'core'=2] {'yhi','zq'}, dimensions={0} | all-to-all | bytes 1048576 | tf_op jit(solution)/shard_map/all_to_all | solution.py:185
  28.6 0.7 collective-permute-start.1
  29.3 5.1 %collective-permute-start = (bf16[8,256,128]{2,1,0:T(8,128)(2,1)S(1)}, bf16[8,256,128]{2,1,0:T(8,128)(2,1)S(1)}, u32[]{:S(2)}, u32[]{:S(2)}) collective-permute-start(bf16[8,256,128]{2,1,0:T(8,128)(2,1)S(1)} %all_to_all.20), channel_id=1, source_target_pairs={{0,1},{1,0},{2,3},{3,2},{4,5},{5,4},{6,7},{7,6},{8,9},{9,8},{10,11... | collective-permute-start | bytes 1572872 | tf_op jit(solution)/shard_map/ppermute | solution.py:207
  34.5 3.6 %collective-permute-done.1 = bf16[8,256,128]{2,1,0:T(8,128)(2,1)S(1)} collective-permute-done((bf16[8,256,128]{2,1,0:T(8,128)(2,1)S(1)}, bf16[8,256,128]{2,1,0:T(8,128)(2,1)S(1)}, u32[]{:S(2)}, u32[]{:S(2)}) %collective-permute-start.1) | collective-permute-done | bytes 524320 | tf_op jit(solution)/shard_map/ppermute | solution.py:206
  38.1 4.2 %collective-permute-start.2 = (bf16[8,256,128]{2,1,0:T(8,128)(2,1)S(1)}, bf16[8,256,128]{2,1,0:T(8,128)(2,1)S(1)}, u32[]{:S(2)}, u32[]{:S(2)}) collective-permute-start(bf16[8,256,128]{2,1,0:T(8,128)(2,1)S(1)} %collective-permute-done.1), channel_id=1, source_target_pairs={{0,1},{1,0},{2,3},{3,2},{4,5},{5,4},{6,7},{7,6},{8,9},{9,8},{10,11... | collective-permute-start | bytes 1572872 | tf_op jit(solution)/shard_map/ppermute | solution.py:208
  43.0 0.0 collective-permute-done
  43.0 0.8 collective-permute-done.2
  43.8 3.5 %forward_tiles.1 = bf16[16,128,128]{2,1,0:T(8,128)(2,1)S(1)} custom-call(s32[1]{0:T(128)} %bitcast.30.count, s32[256]{0:T(256)S(1)} %get-tuple-element.11.rows, s32[256]{0:T(256)S(1)} %get-tuple-element.8.cols, bf16[256,128,128]{2,1,0:T(8,128)(2,1)} %bitcast.40, bf16[16,128,128]{2,1,0:T(8,128)(2,1)S(1)} %bitcast.33, bf16[16,128,128]{2,1,0:T(8,128)(2,1)S(1)} %bitcast.36, ...), custom_call_target="tpu_custom_call" | custom-call | flops 1073741824 | bytes 11534336 | tf_op jit(solution)/shard_map/forward_tiles/pallas_call | solution.py:130
  47.4 0.0 copy-start.3
  47.4 14.1 %all_to_all.21 = bf16[8,256,128]{2,1,0:T(8,128)(2,1)S(1)} all-to-all(bf16[8,256,128]{2,1,0:T(8,128)(2,1)S(1)} %bitcast.34), channel_id=1, replica_groups=mesh['x'=4,'ylo'=2,'yhi'=2,'zq'=4,'zp'=2,'core'=2] {'x','ylo'}, dimensions={0} | all-to-all | bytes 1048576 | tf_op jit(solution)/shard_map/all_to_all | solution.py:213
  61.5 0.1 convert_reduce_fusion.1
  61.6 0.9 fusion.1
  62.5 0.2 convolution_convert_fusion.1
  62.7 0.1 copy.11
  62.8 0.1 broadcast_in_dim.32
  63.0 13.8 %all_to_all.22.got = bf16[8,384,128]{2,1,0:T(8,128)(2,1)S(1)} all-to-all(bf16[8,384,128]{2,1,0:T(8,128)(2,1)S(1)} %broadcast_in_dim.32), channel_id=1, replica_groups=mesh['x'=4,'ylo'=2,'yhi'=2,'zq'=4,'zp'=2,'core'=2] {'x','ylo'}, dimensions={0} | all-to-all | bytes 1572864 | tf_op jit(solution)/shard_map/all_to_all | solution.py:185
  76.7 3.6 %backward_tiles.1 = (f32[4160,128]{1,0:T(8,128)S(1)}, bf16[4160,128]{1,0:T(8,128)(2,1)S(1)}) custom-call(s32[1]{0:T(128)} %bitcast.31.count, s32[1]{0:T(128)} %bitcast.12.core, s32[256]{0:T(256)S(1)} %bitcast.39, s32[256]{0:T(256)S(1)} %get-tuple-element.7.cols, bf16[256,128,128]{2,1,0:T(8,128)(2,1)} %bitcast.41, bf16[8,384,128]{2,1,0:T(8,128)(2,1)S(1)} %all_to_all.22.got), custom_call_target="tpu_custom_call" | custom-call | flops 1073741824 | bytes 12582912 | tf_op jit(solution)/shard_map/backward_tiles/pallas_call | solution.py:151
  80.3 3.0 %collective-permute-start.3 = (bf16[4160,128]{1,0:T(8,128)(2,1)S(1)}, bf16[4160,128]{1,0:T(8,128)(2,1)S(1)}, u32[]{:S(2)}, u32[]{:S(2)}) collective-permute-start(bf16[4160,128]{1,0:T(8,128)(2,1)S(1)} %get-tuple-element.6), channel_id=1, source_target_pairs={{0,1},{1,0},{2,3},{3,2},{4,5},{5,4},{6,7},{7,6},{8,9},{9,8},{10,11... | collective-permute-start | bytes 3194888 | tf_op jit(solution)/shard_map/ppermute | solution.py:230
  83.3 2.3 %collective-permute-done.3.other = bf16[4160,128]{1,0:T(8,128)(2,1)S(1)} collective-permute-done((bf16[4160,128]{1,0:T(8,128)(2,1)S(1)}, bf16[4160,128]{1,0:T(8,128)(2,1)S(1)}, u32[]{:S(2)}, u32[]{:S(2)}) %collective-permute-start.3) | collective-permute-done | bytes 1064992 | tf_op jit(solution)/shard_map/ppermute | solution.py:230
  85.6 0.1 away_kernel.1
  85.8 1.9 %collective-permute-start.4 = (bf16[2112,128]{1,0:T(8,128)(2,1)S(1)}, bf16[2112,128]{1,0:T(8,128)(2,1)S(1)}, u32[]{:S(2)}, u32[]{:S(2)}) collective-permute-start(bf16[2112,128]{1,0:T(8,128)(2,1)S(1)} %away_kernel.1), channel_id=1, source_target_pairs={{0,2},{2,4},{4,6},{6,8},{8,10},{10,12},{12,14},{14,0},{1,15},{3,1}... | collective-permute-start | bytes 1622024 | tf_op jit(solution)/shard_map/ppermute | solution.py:232
  87.7 6.7 %collective-permute-done.4.came = bf16[2112,128]{1,0:T(8,128)(2,1)S(1)} collective-permute-done((bf16[2112,128]{1,0:T(8,128)(2,1)S(1)}, bf16[2112,128]{1,0:T(8,128)(2,1)S(1)}, u32[]{:S(2)}, u32[]{:S(2)}) %collective-permute-start.4) | collective-permute-done | bytes 540704 | tf_op jit(solution)/shard_map/ppermute | solution.py:232
  94.4 1.0 home_kernel.1
  95.4 5.0 %all-to-all-start.3 = ((bf16[8,320,128]{2,1,0:T(8,128)(2,1)}), bf16[8,320,128]{2,1,0:T(8,128)(2,1)S(1)}, u32[]{:S(2)}, u32[]{:S(2)}) async-start(bf16[8,320,128]{2,1,0:T(8,128)(2,1)} %home_kernel.1), calls=%async_computation.3 | async-start | bytes 1310720 | tf_op jit(solution)/shard_map/all_to_all | solution.py:235
  100.4 20.1 %all-to-all-done.3 = bf16[8,320,128]{2,1,0:T(8,128)(2,1)S(1)} async-done(((bf16[8,320,128]{2,1,0:T(8,128)(2,1)}), bf16[8,320,128]{2,1,0:T(8,128)(2,1)S(1)}, u32[]{:S(2)}, u32[]{:S(2)}) %all-to-all-start.3) | async-done | bytes 655392 | tf_op jit(solution)/shard_map/all_to_all | solution.py:235
  120.5 0.1 convert_reduce_fusion
  120.6 1.9 %collective-permute-start.5 = (f32[64,128]{1,0:T(8,128)S(1)}, f32[64,128]{1,0:T(8,128)S(1)}, u32[]{:S(2)}, u32[]{:S(2)}) collective-permute-start(f32[64,128]{1,0:T(8,128)S(1)} %slice.10), channel_id=1, source_target_pairs={{0,1},{1,0},{2,3},{3,2},{4,5},{5,4},{6,7},{7,6},{8,9},{9,8},{10,11... | collective-permute-start | bytes 98312 | tf_op jit(solution)/shard_map/ppermute | solution.py:242
  122.5 0.8 convolution_convert_fusion
  123.3 0.0 collective-permute-done.5
  123.4 0.6 maximum_select_fusion
  (10 shorter events, 0.1 us)
Async XLA Ops:
  0.6 61.0 %copy-start = (bf16[128,128]{1,0:T(8,128)(2,1)S(1)}, bf16[128,128]{1,0:T(8,128)(2,1)}, u32[]{:S(2)}) copy-start(bf16[128,128]{1,0:T(8,128)(2,1)} %param.8) | copy-start | bytes 98308
  0.6 42.3 %copy-start.2 = (s32[1,1,256]{2,1,0:T(1,128)S(1)}, s32[1,1,256]{2,1,0:T(1,128)}, u32[]{:S(2)}) copy-start(s32[1,1,256]{2,1,0:T(1,128)} %param.12) | copy-start | bytes 3076
  0.7 42.3 %copy-start.1 = (s32[1,1,256]{2,1,0:T(1,128)S(1)}, s32[1,1,256]{2,1,0:T(1,128)}, u32[]{:S(2)}) copy-start(s32[1,1,256]{2,1,0:T(1,128)} %param.11) | copy-start | bytes 3076
  28.6 9.4 %collective-permute-start.1 = (bf16[8,256,128]{2,1,0:T(8,128)(2,1)S(1)}, bf16[8,256,128]{2,1,0:T(8,128)(2,1)S(1)}, u32[]{:S(2)}, u32[]{:S(2)}) collective-permute-start(bf16[8,256,128]{2,1,0:T(8,128)(2,1)S(1)} %all_to_all.20), channel_id=1, source_target_pairs={{0,2},{2,4},{4,6},{6,8},{8,10},{10,12},{12,14},{14,0},{1,15},{3,1}... | collective-permute-start | bytes 1572872 | tf_op jit(solution)/shard_map/ppermute | solution.py:206
  29.3 13.7 %collective-permute-start = (bf16[8,256,128]{2,1,0:T(8,128)(2,1)S(1)}, bf16[8,256,128]{2,1,0:T(8,128)(2,1)S(1)}, u32[]{:S(2)}, u32[]{:S(2)}) collective-permute-start(bf16[8,256,128]{2,1,0:T(8,128)(2,1)S(1)} %all_to_all.20), channel_id=1, source_target_pairs={{0,1},{1,0},{2,3},{3,2},{4,5},{5,4},{6,7},{7,6},{8,9},{9,8},{10,11... | collective-permute-start | bytes 1572872 | tf_op jit(solution)/shard_map/ppermute | solution.py:207
  38.1 5.8 %collective-permute-start.2 = (bf16[8,256,128]{2,1,0:T(8,128)(2,1)S(1)}, bf16[8,256,128]{2,1,0:T(8,128)(2,1)S(1)}, u32[]{:S(2)}, u32[]{:S(2)}) collective-permute-start(bf16[8,256,128]{2,1,0:T(8,128)(2,1)S(1)} %collective-permute-done.1), channel_id=1, source_target_pairs={{0,1},{1,0},{2,3},{3,2},{4,5},{5,4},{6,7},{7,6},{8,9},{9,8},{10,11... | collective-permute-start | bytes 1572872 | tf_op jit(solution)/shard_map/ppermute | solution.py:208
  47.4 14.2 %copy-start.3 = (bf16[1,256,128]{2,1,0:T(8,128)(2,1)S(1)}, bf16[1,256,128]{2,1,0:T(8,128)(2,1)}, u32[]{:S(2)}) copy-start(bf16[1,256,128]{2,1,0:T(8,128)(2,1)} %param.9) | copy-start | bytes 196612
  80.3 5.3 %collective-permute-start.3 = (bf16[4160,128]{1,0:T(8,128)(2,1)S(1)}, bf16[4160,128]{1,0:T(8,128)(2,1)S(1)}, u32[]{:S(2)}, u32[]{:S(2)}) collective-permute-start(bf16[4160,128]{1,0:T(8,128)(2,1)S(1)} %get-tuple-element.6), channel_id=1, source_target_pairs={{0,1},{1,0},{2,3},{3,2},{4,5},{5,4},{6,7},{7,6},{8,9},{9,8},{10,11... | collective-permute-start | bytes 3194888 | tf_op jit(solution)/shard_map/ppermute | solution.py:230
  85.8 8.6 %collective-permute-start.4 = (bf16[2112,128]{1,0:T(8,128)(2,1)S(1)}, bf16[2112,128]{1,0:T(8,128)(2,1)S(1)}, u32[]{:S(2)}, u32[]{:S(2)}) collective-permute-start(bf16[2112,128]{1,0:T(8,128)(2,1)S(1)} %away_kernel.1), channel_id=1, source_target_pairs={{0,2},{2,4},{4,6},{6,8},{8,10},{10,12},{12,14},{14,0},{1,15},{3,1}... | collective-permute-start | bytes 1622024 | tf_op jit(solution)/shard_map/ppermute | solution.py:232
  95.4 25.1 %all-to-all-start.3 = ((bf16[8,320,128]{2,1,0:T(8,128)(2,1)}), bf16[8,320,128]{2,1,0:T(8,128)(2,1)S(1)}, u32[]{:S(2)}, u32[]{:S(2)}) async-start(bf16[8,320,128]{2,1,0:T(8,128)(2,1)} %home_kernel.1), calls=%async_computation.3 | async-start | bytes 1310720 | tf_op jit(solution)/shard_map/all_to_all | solution.py:235
  120.6 2.7 %collective-permute-start.5 = (f32[64,128]{1,0:T(8,128)S(1)}, f32[64,128]{1,0:T(8,128)S(1)}, u32[]{:S(2)}, u32[]{:S(2)}) collective-permute-start(f32[64,128]{1,0:T(8,128)S(1)} %slice.10), channel_id=1, source_target_pairs={{0,1},{1,0},{2,3},{3,2},{4,5},{5,4},{6,7},{7,6},{8,9},{9,8},{10,11... | collective-permute-start | bytes 98312 | tf_op jit(solution)/shard_map/ppermute | solution.py:242

commit v3 on v2

v3 whole, which is shorter than its diff:
```python
import functools

import jax
import jax.numpy as jnp
from jax import lax
from jax.experimental import pallas as pl
from jax.experimental.pallas import tpu as pltpu
from jax.sharding import Mesh, PartitionSpec as P

CHUNK = 32
BLOCK = 128
ROWS = 16
PLACES = 32
PART = PLACES // 2
ROW_AT, PLACE_AT = 8, 13
SPARE = (ROWS << ROW_AT) | (PLACES << PLACE_AT)
SPAN = PART * BLOCK
EXTRA = BLOCK // 2
SIZES = (4, 2, 2, 4, 2, 2)
AXES = ("x", "ylo", "yhi", "zq", "zp", "core")
REP = ("x", "ylo")
ROW = ("yhi", "zq", "zp", "core")
PARITY = ("yhi", "zq")
ALONG = ("zq", "zp", "core")
SWAP = ((0, 1), (1, 0))
NEXT = tuple((2 * z, 2 * ((z + 1) % 8)) for z in range(8)) + tuple(
    (2 * z + 1, 2 * ((z + 7) % 8) + 1) for z in range(8)
)


def tile_copy(tiles, buffer, sems, chunk):
    span = pl.ds(chunk * CHUNK, CHUNK)
    return pltpu.make_async_copy(tiles.at[span], buffer.at[span], sems.at[chunk])


def tile_groups(part, counts, lists, group, ready):
    count = counts[part]

    def step(k, done):
        base = k * CHUNK
        last = lists[part, jnp.minimum(base + CHUNK, count) - 1] & 255
        done = ready(done, last // CHUNK + 1)
        group([lists[part, base + u] for u in range(CHUNK)])
        return done

    return lax.fori_loop(0, (count + CHUNK - 1) // CHUNK, step, 0)


def forward_kernel(part, counts, lists, tiles, *rest):
    if part == 0:
        x0, x1, out, buffer, xs, acc, xsems, sems = rest
    else:
        before, x0, x1, out, xs, acc, xsems = rest
        buffer = tiles
    chunks = (counts[0] + counts[1] + CHUNK - 1) // CHUNK
    moves = [
        pltpu.make_async_copy(source, xs.at[pl.ds(k * PART, PART)], xsems.at[k])
        for k, source in enumerate((x0, x1))
    ]
    for move in moves:
        move.start()
    if part == 0:

        @pl.loop(0, chunks)
        def _(c):
            tile_copy(tiles, buffer, sems, c).start()

        acc[...] = jnp.zeros_like(acc)
    else:
        acc[:ROWS] = before[...]
    for move in moves:
        move.wait()

    def ready(done, need):
        if part == 0:

            @pl.loop(done, need)
            def _(c):
                tile_copy(tiles, buffer, sems, c).wait()

        return need

    def group(codes):
        products = [
            jnp.dot(
                buffer[code & 255],
                xs[(code >> PLACE_AT) & (PLACES - 1)],
                preferred_element_type=jnp.float32,
            )
            for code in codes
        ]
        for code, product in zip(codes, products):
            acc[(code >> ROW_AT) & 31] += product

    done = tile_groups(part, counts, lists, group, ready)
    ready(done, chunks)
    out[...] = acc[:ROWS].astype(out.dtype)


def backward_kernel(part, counts, core, lists, tiles, got, own, other, buffer, acc, *rest):
    weight_sum, sems = rest if part == 1 else (None, *rest)
    last = lists[part, jnp.maximum(counts[part], 1) - 1] & 255
    chunks = jnp.where(counts[part] > 0, last // CHUNK + 1, 0)

    @pl.loop(0, chunks)
    def _(c):
        tile_copy(tiles, buffer, sems, c).start()

    acc[...] = jnp.zeros_like(acc)
    nodes = got.shape[1] - BLOCK
    if part == 1:
        reps = got.shape[0]
        weight_sum[...] = sum(got[k, nodes:].astype(jnp.float32) for k in range(reps))

    def ready(done, need):
        @pl.loop(done, need)
        def _(c):
            tile_copy(tiles, buffer, sems, c).wait()

        return need

    def group(codes):
        products = []
        for code in codes:
            row = (code >> ROW_AT) & (ROWS - 1)
            grad = got[row // 2, pl.ds(pl.multiple_of((row % 2) * BLOCK, BLOCK), BLOCK), :]
            products.append(
                jnp.dot(grad, buffer[code & 255], preferred_element_type=jnp.float32)
            )
        for code, product in zip(codes, products):
            acc[code >> PLACE_AT] += product

    tile_groups(part, counts, lists, group, ready)
    feats = own.shape[1]
    own[:SPAN] = acc[:PART].reshape(SPAN, feats)
    other[:SPAN] = acc[PART:PLACES].reshape(SPAN, feats).astype(jnp.bfloat16)
    if part == 1:
        mine = pl.multiple_of(core[0] * EXTRA, EXTRA)
        theirs = pl.multiple_of((1 - core[0]) * EXTRA, EXTRA)
        own[SPAN:] = weight_sum[pl.ds(mine, EXTRA), :]
        other[SPAN:] = weight_sum[pl.ds(theirs, EXTRA), :].astype(jnp.bfloat16)


def away_kernel(own, other, out):
    out[...] = (own[...] + other[...].astype(jnp.float32)).astype(jnp.bfloat16)


def home_kernel(own, other, away_own, away_other, came, out):
    peers = out.shape[0]
    nodes = out.shape[1] - EXTRA
    weight = away_own[SPAN:] + away_other[SPAN:].astype(jnp.float32)
    weight = (weight + came[SPAN:].astype(jnp.float32)).astype(jnp.bfloat16)
    for k in range(peers):
        here = pl.ds(k * nodes, nodes)
        total = own[here, :] + other[here, :].astype(jnp.float32)
        total = total + came[here, :].astype(jnp.float32)
        out[k, :nodes] = total.astype(jnp.bfloat16)
        out[k, nodes:] = weight


SMEM = pl.BlockSpec(memory_space=pltpu.SMEM)
VMEM = pl.BlockSpec(memory_space=pltpu.VMEM)
ANY = pl.BlockSpec(memory_space=pl.ANY)


def forward_pass(part, counts, lists, tiles, parts, before=()):
    cap = tiles.shape[0]
    out = jax.ShapeDtypeStruct(
        (ROWS, BLOCK, BLOCK), jnp.float32 if part == 0 else jnp.bfloat16
    )
    scratch = [
        pltpu.VMEM((PLACES, BLOCK, BLOCK), jnp.bfloat16),
        pltpu.VMEM((ROWS + 1, BLOCK, BLOCK), jnp.float32),
        pltpu.SemaphoreType.DMA((2,)),
    ]
    if part == 0:
        scratch.append(pltpu.SemaphoreType.DMA((cap // CHUNK,)))
    return pl.pallas_call(
        functools.partial(forward_kernel, part),
        out_shape=(out, pltpu.VMEM((cap, BLOCK, BLOCK), jnp.bfloat16)) if part == 0 else out,
        in_specs=[SMEM, SMEM, ANY if part == 0 else VMEM] + [VMEM] * len(before) + [ANY, ANY],
        out_specs=(VMEM, VMEM) if part == 0 else VMEM,
        scratch_shapes=scratch,
        compiler_params=pltpu.CompilerParams(vmem_limit_bytes=20 << 20),
        cost_estimate=pl.CostEstimate(flops=1 << 30, bytes_accessed=9 << 20, transcendentals=0),
        name=f"forward_tiles_{part}",
    )(
        counts,
        lists,
        pltpu.with_memory_space_constraint(tiles, pltpu.HBM if part == 0 else pltpu.VMEM),
        *before,
        *parts,
    )


def backward_pass(part, counts, core, lists, tiles, got):
    cap = tiles.shape[0]
    feats = got.shape[2]
    size = SPAN + EXTRA * part
    scratch = [
        pltpu.VMEM((cap, BLOCK, BLOCK), jnp.bfloat16),
        pltpu.VMEM((PLACES + 1, BLOCK, BLOCK), jnp.float32),
        pltpu.SemaphoreType.DMA((cap // CHUNK,)),
    ]
    if part == 1:
        scratch.insert(2, pltpu.VMEM((BLOCK, BLOCK), jnp.float32))
    return pl.pallas_call(
        functools.partial(backward_kernel, part),
        out_shape=(
            jax.ShapeDtypeStruct((size, feats), jnp.float32),
            jax.ShapeDtypeStruct((size, feats), jnp.bfloat16),
        ),
        in_specs=[SMEM, SMEM, SMEM, ANY, VMEM],
        out_specs=(VMEM, VMEM),
        scratch_shapes=scratch,
        compiler_params=pltpu.CompilerParams(vmem_limit_bytes=20 << 20),
        cost_estimate=pl.CostEstimate(flops=1 << 30, bytes_accessed=9 << 20, transcendentals=0),
        name=f"backward_tiles_{part}",
    )(counts, core, lists, pltpu.with_memory_space_constraint(tiles, pltpu.HBM), got)


def merge(kernel, shape, *arrays):
    return pl.pallas_call(
        kernel,
        out_shape=jax.ShapeDtypeStruct(shape, jnp.bfloat16),
        in_specs=[VMEM] * len(arrays),
        out_specs=VMEM,
        compiler_params=pltpu.CompilerParams(vmem_limit_bytes=16 << 20),
        cost_estimate=pl.CostEstimate(flops=1 << 20, bytes_accessed=4 << 20, transcendentals=0),
        name=kernel.__name__,
    )(*arrays)


def spread(block, axes):
    n = lax.axis_size(axes)
    return lax.all_to_all(jnp.broadcast_to(block[None], (n, *block.shape)), axes, 0, 0)


def tile_lists(rows, cols, count, parity, core):
    slots = jnp.arange(rows.shape[0], dtype=jnp.int32)
    z = (cols // 4) % 8
    part = (z % 2) ^ parity
    place = (((cols // 2) % 2) ^ core) * PART + ((cols // 32) * 4 + z // 2) * 2 + cols % 2
    code = slots | (rows << ROW_AT) | (place << PLACE_AT)
    part = jnp.where(slots < count, part, 2)
    earlier = (slots[None, :] < slots[:, None]) & (part[None, :] == part[:, None])
    rank = jnp.sum(earlier.astype(jnp.int32), axis=1)
    parts = jnp.arange(2, dtype=jnp.int32)[:, None]
    mine = part[None, :] == parts
    hit = mine[:, None, :] & (rank[None, None, :] == slots[None, :, None])
    lists = SPARE + jnp.sum(jnp.where(hit, code - SPARE, 0), axis=2)
    return jnp.sum(mine.astype(jnp.int32), axis=1), lists


def local(features, weight, cotangent, tiles, row_ids, col_ids, counts):
    x = features[0]
    nodes, feats = x.shape
    tiles = tiles[0, 0]
    core = lax.axis_index("core")
    counts, lists = tile_lists(
        row_ids[0, 0], col_ids[0, 0], counts[0, 0], lax.axis_index("zp"), core
    )
    blocks = (PART, BLOCK, feats)

    own = spread(x, PARITY)
    beside = lax.ppermute(own, ALONG, NEXT)
    own_other = lax.ppermute(own, "core", SWAP)
    y_part, held = forward_pass(
        0, counts, lists, tiles, (own.reshape(blocks), own_other.reshape(blocks))
    )
    beside, y_part = lax.optimization_barrier((beside, y_part))
    beside_other = lax.ppermute(beside, "core", SWAP)
    y_part = forward_pass(
        1, counts, lists, held, (beside.reshape(blocks), beside_other.reshape(blocks)), (y_part,)
    )

    reps = lax.axis_size(REP)
    y_parts = lax.all_to_all(y_part.reshape(reps, nodes, feats), REP, 0, 0)
    y = jnp.sum(y_parts.astype(jnp.float32), axis=0)
    z = jnp.dot(y, weight.astype(jnp.float32), precision=lax.Precision.HIGHEST)
    sigma = jax.nn.sigmoid(z)
    hidden = (z * sigma).astype(jnp.bfloat16)
    grad_pre = (
        cotangent[0].astype(jnp.float32) * sigma * (1.0 + z * (1.0 - sigma))
    ).astype(jnp.bfloat16)

    weight_part = lax.dot_general(
        y.astype(jnp.bfloat16), grad_pre, (((0,), (0,)), ((), ())),
        preferred_element_type=jnp.float32,
    ).astype(jnp.bfloat16)
    grad_t = jnp.swapaxes(grad_pre.reshape(nodes // BLOCK, BLOCK, feats), 1, 2)
    got = spread(jnp.concatenate([grad_t.reshape(nodes, feats), weight_part]), REP)

    core_id = core[None]
    away_own, away_other = backward_pass(1, counts, core_id, lists, tiles, got)
    away_other = lax.ppermute(away_other, "core", SWAP)
    away = merge(away_kernel, away_own.shape, away_own, away_other)
    core_id, away = lax.optimization_barrier((core_id, away))
    came = lax.ppermute(away, ALONG, NEXT)
    home_own, home_other = backward_pass(0, counts, core_id, lists, tiles, got)
    home_other = lax.ppermute(home_other, "core", SWAP)
    peers = lax.axis_size(PARITY)
    sent = merge(
        home_kernel, (peers, nodes + EXTRA, feats), home_own, home_other, away_own, away_other, came
    )
    got = lax.all_to_all(sent, PARITY, 0, 0)
    total = jnp.sum(got.astype(jnp.float32), axis=0)
    grad_xw_t = total[:nodes].astype(jnp.bfloat16).reshape(nodes // BLOCK, feats, BLOCK)
    grad_feats = jnp.einsum(
        "hfn,kf->hnk", grad_xw_t, weight, preferred_element_type=jnp.float32
    ).astype(jnp.bfloat16)
    mine = total[nodes:]
    theirs = lax.ppermute(mine, "core", SWAP)
    grad_weight = jnp.where(
        core == 0, jnp.concatenate([mine, theirs]), jnp.concatenate([theirs, mine])
    )
    return hidden[None], grad_feats.reshape(1, nodes, feats), grad_weight


def solution(mesh):
    mesh = Mesh(mesh.devices.reshape(SIZES), AXES)
    placed = P(ROW, REP)
    return jax.shard_map(
        local,
        mesh=mesh,
        in_specs=(placed, P(), placed, placed, placed, placed, placed),
        out_specs=(placed, placed, P()),
        check_vma=False,
    )
```

time: 124 us -> 122 us (0.984); the launches traced: 124 us -> 120 us
  blocking collectives: 55 us -> 25.3 us
  starting transfers between devices: 21.8 us -> 32.8 us
  waiting for transfers between devices: 33.6 us -> 41.5 us
  Pallas kernels: 8.27 us -> 12.6 us
  other arithmetic: 0.83 us -> 2.71 us
    all_to_all x2 -> x1, blocking collectives: 40.8 us -> 12.8 us  [spread(): lax.all_to_all(jnp.broadcast_to(block[None], (n, *block.shape)), axes, 0, 0)]
    all_to_all x0 -> x1, waiting for transfers between devices: none -> 12.8 us  [spread(): lax.all_to_all(jnp.broadcast_to(block[None], (n, *block.shape)), axes, 0, 0)]
    all_to_all x0 -> x1, starting transfers between devices: none -> 11.6 us  [spread(): lax.all_to_all(jnp.broadcast_to(block[None], (n, *block.shape)), axes, 0, 0)]
    ppermute x1, waiting for transfers between devices: 6.72 us -> 1.23 us  [local(): came = lax.ppermute(away, ALONG, NEXT)]
    pallas_call x2 -> x4, Pallas kernels: 7.11 us -> 11.5 us  [the longest x2 6.53 us: backward_pass(): pl.pallas_call(functools.partial(backward_kernel, part), out_shape=(jax.S...]
    ppermute x1, starting transfers between devices: 4.24 us -> 0.74 us  [local(): beside_other = lax.ppermute(beside, 'core', SWAP)]
    all_to_all x1, waiting for transfers between devices: 20.1 us -> 16.7 us  [local(): got = lax.all_to_all(sent, PARITY, 0, 0)]
    ppermute x1 -> x2, starting transfers between devices: 3 us -> 5.96 us  [the longest x1 3.64 us: local(): away_other = lax.ppermute(away_other, 'core', SWAP)]
  transfers between devices with their start and end apart: 7 -> 9, of which waited for: 5 -> 8; matrix products, arithmetic and copies ran while one was open for 1% -> 2% of each run, Pallas kernels for 0% -> 5%
where the time goes in v3:
time: 122 us; the launch traced here: 120 us
  waiting for transfers between devices  41.5 us (34%)
  starting transfers between devices  32.8 us (27%)
  blocking collectives  25.3 us (21%)
  Pallas kernels  12.6 us (10%)
  other arithmetic  2.71 us (2%)
  local copies, waits for them, and re-layouts  1.97 us (2%)
  matrix products  1.9 us (2%)
  between operations  1.43 us (1%)
    all_to_all x1, waiting for transfers between devices, local(): got = lax.all_to_all(sent, PARITY, 0, 0)  16.7 us
    all_to_all x1, blocking collectives, spread(): lax.all_to_all(jnp.broadcast_to(block[None], (n, *block.shape)), axes, 0, 0)  12.8 us
    all_to_all x1, waiting for transfers between devices, spread(): lax.all_to_all(jnp.broadcast_to(block[None], (n, *block.shape)), axes, 0, 0)  12.8 us
    all_to_all x1, blocking collectives, local(): y_parts = lax.all_to_all(y_part.reshape(reps, nodes, feats), REP, 0, 0)  12.4 us
    all_to_all x1, starting transfers between devices, spread(): lax.all_to_all(jnp.broadcast_to(block[None], (n, *block.shape)), axes, 0, 0)  11.6 us
    all_to_all x1, starting transfers between devices, local(): got = lax.all_to_all(sent, PARITY, 0, 0)  6.7 us
    pallas_call x2, Pallas kernels, backward_pass(): pl.pallas_call(functools.partial(backward_kernel, part), out_shape=(jax.S...  6.53 us
    ppermute x1, waiting for transfers between devices, local(): beside = lax.ppermute(own, ALONG, NEXT)  4.94 us
  transfers between devices with their start and end apart: 9, of which 8 were waited for; matrix products, arithmetic and copies ran while one was open for 2% of the time, Pallas kernels for 5%

profile of v3, /device:TPU:1, one launch (start us, length us, event | category | flops | bytes accessed | tf_op | source)
XLA Modules:
  0.0 120.2 jit_solution(18354135995874079368)
XLA Ops:
  0.6 1.7 %broadcast_in_dim.23 = bf16[8,256,128]{2,1,0:T(8,128)(2,1)} broadcast(bf16[256,128]{1,0:T(8,128)(2,1)} %bitcast.41), dimensions={1,2} | broadcast | bytes 589824 | tf_op jit(solution)/shard_map/broadcast_in_dim | solution.py:236
  2.4 11.6 %all-to-all-start = ((bf16[8,256,128]{2,1,0:T(8,128)(2,1)}), bf16[8,256,128]{2,1,0:T(8,128)(2,1)S(1)}, u32[]{:S(2)}, u32[]{:S(2)}) async-start(bf16[8,256,128]{2,1,0:T(8,128)(2,1)} %broadcast_in_dim.23), calls=%async_computation | async-start | bytes 1048576 | tf_op jit(solution)/shard_map/all_to_all | solution.py:236
  14.7 0.7 broadcast_shift-left_fusion
  15.3 0.7 or_add_fusion
  16.1 0.2 convert_reduce_fusion.2
  16.3 12.8 %all-to-all-done = bf16[8,256,128]{2,1,0:T(8,128)(2,1)S(1)} async-done(((bf16[8,256,128]{2,1,0:T(8,128)(2,1)}), bf16[8,256,128]{2,1,0:T(8,128)(2,1)S(1)}, u32[]{:S(2)}, u32[]{:S(2)}) %all-to-all-start) | async-done | bytes 524320 | tf_op jit(solution)/shard_map/all_to_all | solution.py:236
  29.1 3.3 %collective-permute-start = (bf16[8,256,128]{2,1,0:T(8,128)(2,1)S(1)}, bf16[8,256,128]{2,1,0:T(8,128)(2,1)S(1)}, u32[]{:S(2)}, u32[]{:S(2)}) collective-permute-start(bf16[8,256,128]{2,1,0:T(8,128)(2,1)S(1)} %all-to-all-done), channel_id=1, source_target_pairs={{0,1},{1,0},{2,3},{3,2},{4,5},{5,4},{6,7},{7,6},{8,9},{9,8},{10,11... | collective-permute-start | bytes 1572872 | tf_op jit(solution)/shard_map/ppermute | solution.py:267
  32.4 0.2 select_reduce_fusion
  32.6 1.2 %collective-permute-done = bf16[8,256,128]{2,1,0:T(8,128)(2,1)S(1)} collective-permute-done((bf16[8,256,128]{2,1,0:T(8,128)(2,1)S(1)}, bf16[8,256,128]{2,1,0:T(8,128)(2,1)S(1)}, u32[]{:S(2)}, u32[]{:S(2)}) %collective-permute-start) | collective-permute-done | bytes 524320 | tf_op jit(solution)/shard_map/ppermute | solution.py:267
  33.9 3.2 %forward_tiles_0.1 = (f32[16,128,128]{2,1,0:T(8,128)S(1)}, bf16[256,128,128]{2,1,0:T(8,128)(2,1)S(1)}) custom-call(s32[2]{0:T(128)S(1)} %get-tuple-element.27.counts, s32[2,256]{1,0:T(2,128)S(1)} %get-tuple-element.28.lists, bf16[256,128,128]{2,1,0:T(8,128)(2,1)} %bitcast.35, bf16[16,128,128]{2,1,0:T(8,128)(2,1)S(1)} %bitcast.31, ...), custom_call_target="tpu_custom_call" | custom-call | flops 1073741824 | bytes 9437184 | tf_op jit(solution)/shard_map/forward_tiles_0/pallas_call | solution.py:178
  37.1 4.9 %collective-permute-done.1 = bf16[8,256,128]{2,1,0:T(8,128)(2,1)S(1)} collective-permute-done((bf16[8,256,128]{2,1,0:T(8,128)(2,1)S(1)}, bf16[8,256,128]{2,1,0:T(8,128)(2,1)S(1)}, u32[]{:S(2)}, u32[]{:S(2)}) %collective-permute-start.1) | collective-permute-done | bytes 524320 | tf_op jit(solution)/shard_map/ppermute | solution.py:266
  42.0 0.7 collective-permute-start.2
  42.7 1.5 %collective-permute-done.2 = bf16[8,256,128]{2,1,0:T(8,128)(2,1)S(1)} collective-permute-done((bf16[8,256,128]{2,1,0:T(8,128)(2,1)S(1)}, bf16[8,256,128]{2,1,0:T(8,128)(2,1)S(1)}, u32[]{:S(2)}, u32[]{:S(2)}) %collective-permute-start.2) | collective-permute-done | bytes 524320 | tf_op jit(solution)/shard_map/ppermute | solution.py:272
  44.3 1.8 %forward_tiles_1.1 = bf16[16,128,128]{2,1,0:T(8,128)(2,1)S(1)} custom-call(s32[2]{0:T(128)S(1)} %get-tuple-element.27.counts, s32[2,256]{1,0:T(2,128)S(1)} %get-tuple-element.28.lists, bf16[256,128,128]{2,1,0:T(8,128)(2,1)S(1)} %get-tuple-element.13.tiles, f32[16,128,128]{2,1,0:T(8,128)S(1)} %get-tuple-element.15.rest_0_, ...), custom_call_target="tpu_custom_call" | custom-call | flops 1073741824 | bytes 9437184 | tf_op jit(solution)/shard_map/forward_tiles_1/pallas_call | solution.py:178
  46.1 12.4 %all_to_all.20 = bf16[8,256,128]{2,1,0:T(8,128)(2,1)S(1)} all-to-all(bf16[8,256,128]{2,1,0:T(8,128)(2,1)S(1)} %bitcast.30), channel_id=1, replica_groups=mesh['x'=4,'ylo'=2,'yhi'=2,'zq'=4,'zp'=2,'core'=2] {'x','ylo'}, dimensions={0} | all-to-all | bytes 1048576 | tf_op jit(solution)/shard_map/all_to_all | solution.py:278
  58.6 0.9 fusion.2
  59.5 0.2 convolution_convert_fusion.1
  59.9 12.8 %all_to_all.21.got = bf16[8,384,128]{2,1,0:T(8,128)(2,1)S(1)} all-to-all(bf16[8,384,128]{2,1,0:T(8,128)(2,1)S(1)} %broadcast_in_dim.44), channel_id=1, replica_groups=mesh['x'=4,'ylo'=2,'yhi'=2,'zq'=4,'zp'=2,'core'=2] {'x','ylo'}, dimensions={0} | all-to-all | bytes 1572864 | tf_op jit(solution)/shard_map/all_to_all | solution.py:236
  72.8 3.4 %backward_tiles_1.1 = (f32[2112,128]{1,0:T(8,128)S(1)}, bf16[2112,128]{1,0:T(8,128)(2,1)S(1)}) custom-call(s32[2]{0:T(128)S(1)} %get-tuple-element.27.counts, s32[1]{0:T(128)} %bitcast.11.core, s32[2,256]{1,0:T(2,128)S(1)} %get-tuple-element.28.lists, bf16[256,128,128]{2,1,0:T(8,128)(2,1)} %bitcast.36, bf16[8,384,128]{2,1,0:T(8,128)(2,1)S(1)} %all_to_all.21.got), custom_call_target="tpu_custom_call" | custom-call | flops 1073741824 | bytes 9437184 | tf_op jit(solution)/shard_map/backward_tiles_1/pallas_call | solution.py:207
  76.2 3.6 %collective-permute-start.3 = (bf16[2112,128]{1,0:T(8,128)(2,1)S(1)}, bf16[2112,128]{1,0:T(8,128)(2,1)S(1)}, u32[]{:S(2)}, u32[]{:S(2)}) collective-permute-start(bf16[2112,128]{1,0:T(8,128)(2,1)S(1)} %get-tuple-element.18), channel_id=1, source_target_pairs={{0,1},{1,0},{2,3},{3,2},{4,5},{5,4},{6,7},{7,6},{8,9},{9,8},{10,11... | collective-permute-start | bytes 1622024 | tf_op jit(solution)/shard_map/ppermute | solution.py:296
  79.8 1.6 %collective-permute-done.3.other.away_other = bf16[2112,128]{1,0:T(8,128)(2,1)S(1)} collective-permute-done((bf16[2112,128]{1,0:T(8,128)(2,1)S(1)}, bf16[2112,128]{1,0:T(8,128)(2,1)S(1)}, u32[]{:S(2)}, u32[]{:S(2)}) %collective-permute-start.3) | collective-permute-done | bytes 540704 | tf_op jit(solution)/shard_map/ppermute | solution.py:296
  81.5 0.3 collective-permute-start.5
  81.9 3.1 %backward_tiles_0.1 = (f32[2048,128]{1,0:T(8,128)S(1)}, bf16[2048,128]{1,0:T(8,128)(2,1)S(1)}) custom-call(s32[2]{0:T(128)S(1)} %get-tuple-element.27.counts, s32[1]{0:T(128)} %bitcast.11.core, s32[2,256]{1,0:T(2,128)S(1)} %get-tuple-element.28.lists, bf16[256,128,128]{2,1,0:T(8,128)(2,1)} %bitcast.37, bf16[8,384,128]{2,1,0:T(8,128)(2,1)S(1)} %all_to_all.21.got), custom_call_target="tpu_custom_call" | custom-call | flops 1073741824 | bytes 9437184 | tf_op jit(solution)/shard_map/backward_tiles_0/pallas_call | solution.py:207
  85.0 2.3 %collective-permute-start.4 = (bf16[2048,128]{1,0:T(8,128)(2,1)S(1)}, bf16[2048,128]{1,0:T(8,128)(2,1)S(1)}, u32[]{:S(2)}, u32[]{:S(2)}) collective-permute-start(bf16[2048,128]{1,0:T(8,128)(2,1)S(1)} %get-tuple-element.21), channel_id=1, source_target_pairs={{0,1},{1,0},{2,3},{3,2},{4,5},{5,4},{6,7},{7,6},{8,9},{9,8},{10,11... | collective-permute-start | bytes 1572872 | tf_op jit(solution)/shard_map/ppermute | solution.py:301
  87.4 1.5 %collective-permute-done.4.other = bf16[2048,128]{1,0:T(8,128)(2,1)S(1)} collective-permute-done((bf16[2048,128]{1,0:T(8,128)(2,1)S(1)}, bf16[2048,128]{1,0:T(8,128)(2,1)S(1)}, u32[]{:S(2)}, u32[]{:S(2)}) %collective-permute-start.4) | collective-permute-done | bytes 524320 | tf_op jit(solution)/shard_map/ppermute | solution.py:301
  88.9 1.2 %collective-permute-done.5.came = bf16[2112,128]{1,0:T(8,128)(2,1)S(1)} collective-permute-done((bf16[2112,128]{1,0:T(8,128)(2,1)S(1)}, bf16[2112,128]{1,0:T(8,128)(2,1)S(1)}, u32[]{:S(2)}, u32[]{:S(2)}) %collective-permute-start.5) | collective-permute-done | bytes 540704 | tf_op jit(solution)/shard_map/ppermute | solution.py:299
  90.1 1.0 home_kernel.1
  91.1 6.7 %all-to-all-start.3 = ((bf16[8,320,128]{2,1,0:T(8,128)(2,1)}), bf16[8,320,128]{2,1,0:T(8,128)(2,1)S(1)}, u32[]{:S(2)}, u32[]{:S(2)}) async-start(bf16[8,320,128]{2,1,0:T(8,128)(2,1)} %home_kernel.1), calls=%async_computation.3 | async-start | bytes 1310720 | tf_op jit(solution)/shard_map/all_to_all | solution.py:306
  97.8 16.7 %all-to-all-done.3 = bf16[8,320,128]{2,1,0:T(8,128)(2,1)S(1)} async-done(((bf16[8,320,128]{2,1,0:T(8,128)(2,1)}), bf16[8,320,128]{2,1,0:T(8,128)(2,1)S(1)}, u32[]{:S(2)}, u32[]{:S(2)}) %all-to-all-start.3) | async-done | bytes 655392 | tf_op jit(solution)/shard_map/all_to_all | solution.py:306
  114.6 4.1 %collective-permute-start.6 = (f32[64,128]{1,0:T(8,128)S(1)}, f32[64,128]{1,0:T(8,128)S(1)}, u32[]{:S(2)}, u32[]{:S(2)}) collective-permute-start(f32[64,128]{1,0:T(8,128)S(1)} %slice.10), channel_id=1, source_target_pairs={{0,1},{1,0},{2,3},{3,2},{4,5},{5,4},{6,7},{7,6},{8,9},{9,8},{10,11... | collective-permute-start | bytes 98312 | tf_op jit(solution)/shard_map/ppermute | solution.py:313
  118.7 0.8 convolution_convert_fusion
  119.6 0.6 maximum_select_fusion
  (18 shorter events, 0.8 us)
Async XLA Ops:
  0.6 58.0 %copy-start = (bf16[128,128]{1,0:T(8,128)(2,1)S(1)}, bf16[128,128]{1,0:T(8,128)(2,1)}, u32[]{:S(2)}) copy-start(bf16[128,128]{1,0:T(8,128)(2,1)} %param.8) | copy-start | bytes 98308
  2.4 26.7 %all-to-all-start = ((bf16[8,256,128]{2,1,0:T(8,128)(2,1)}), bf16[8,256,128]{2,1,0:T(8,128)(2,1)S(1)}, u32[]{:S(2)}, u32[]{:S(2)}) async-start(bf16[8,256,128]{2,1,0:T(8,128)(2,1)} %broadcast_in_dim.23), calls=%async_computation | async-start | bytes 1048576 | tf_op jit(solution)/shard_map/all_to_all | solution.py:236
  29.1 4.8 %collective-permute-start = (bf16[8,256,128]{2,1,0:T(8,128)(2,1)S(1)}, bf16[8,256,128]{2,1,0:T(8,128)(2,1)S(1)}, u32[]{:S(2)}, u32[]{:S(2)}) collective-permute-start(bf16[8,256,128]{2,1,0:T(8,128)(2,1)S(1)} %all-to-all-done), channel_id=1, source_target_pairs={{0,1},{1,0},{2,3},{3,2},{4,5},{5,4},{6,7},{7,6},{8,9},{9,8},{10,11... | collective-permute-start | bytes 1572872 | tf_op jit(solution)/shard_map/ppermute | solution.py:267
  32.3 9.7 %collective-permute-start.1 = (bf16[8,256,128]{2,1,0:T(8,128)(2,1)S(1)}, bf16[8,256,128]{2,1,0:T(8,128)(2,1)S(1)}, u32[]{:S(2)}, u32[]{:S(2)}) collective-permute-start(bf16[8,256,128]{2,1,0:T(8,128)(2,1)S(1)} %all-to-all-done), channel_id=1, source_target_pairs={{0,2},{2,4},{4,6},{6,8},{8,10},{10,12},{12,14},{14,0},{1,15},{3,1}... | collective-permute-start | bytes 1572872 | tf_op jit(solution)/shard_map/ppermute | solution.py:266
  37.1 21.5 %copy-start.1 = (bf16[1,256,128]{2,1,0:T(8,128)(2,1)S(1)}, bf16[1,256,128]{2,1,0:T(8,128)(2,1)}, u32[]{:S(2)}) copy-start(bf16[1,256,128]{2,1,0:T(8,128)(2,1)} %param.9) | copy-start | bytes 196612
  42.0 2.3 %collective-permute-start.2 = (bf16[8,256,128]{2,1,0:T(8,128)(2,1)S(1)}, bf16[8,256,128]{2,1,0:T(8,128)(2,1)S(1)}, u32[]{:S(2)}, u32[]{:S(2)}) collective-permute-start(bf16[8,256,128]{2,1,0:T(8,128)(2,1)S(1)} %collective-permute-done.1), channel_id=1, source_target_pairs={{0,1},{1,0},{2,3},{3,2},{4,5},{5,4},{6,7},{7,6},{8,9},{9,8},{10,11... | collective-permute-start | bytes 1572872 | tf_op jit(solution)/shard_map/ppermute | solution.py:272
  76.2 5.2 %collective-permute-start.3 = (bf16[2112,128]{1,0:T(8,128)(2,1)S(1)}, bf16[2112,128]{1,0:T(8,128)(2,1)S(1)}, u32[]{:S(2)}, u32[]{:S(2)}) collective-permute-start(bf16[2112,128]{1,0:T(8,128)(2,1)S(1)} %get-tuple-element.18), channel_id=1, source_target_pairs={{0,1},{1,0},{2,3},{3,2},{4,5},{5,4},{6,7},{7,6},{8,9},{9,8},{10,11... | collective-permute-start | bytes 1622024 | tf_op jit(solution)/shard_map/ppermute | solution.py:296
  81.5 8.6 %collective-permute-start.5 = (bf16[2112,128]{1,0:T(8,128)(2,1)S(1)}, bf16[2112,128]{1,0:T(8,128)(2,1)S(1)}, u32[]{:S(2)}, u32[]{:S(2)}) collective-permute-start(bf16[2112,128]{1,0:T(8,128)(2,1)S(1)} %away_kernel.1), channel_id=1, source_target_pairs={{0,2},{2,4},{4,6},{6,8},{8,10},{10,12},{12,14},{14,0},{1,15},{3,1}... | collective-permute-start | bytes 1622024 | tf_op jit(solution)/shard_map/ppermute | solution.py:299
  85.0 3.9 %collective-permute-start.4 = (bf16[2048,128]{1,0:T(8,128)(2,1)S(1)}, bf16[2048,128]{1,0:T(8,128)(2,1)S(1)}, u32[]{:S(2)}, u32[]{:S(2)}) collective-permute-start(bf16[2048,128]{1,0:T(8,128)(2,1)S(1)} %get-tuple-element.21), channel_id=1, source_target_pairs={{0,1},{1,0},{2,3},{3,2},{4,5},{5,4},{6,7},{7,6},{8,9},{9,8},{10,11... | collective-permute-start | bytes 1572872 | tf_op jit(solution)/shard_map/ppermute | solution.py:301
  91.1 23.4 %all-to-all-start.3 = ((bf16[8,320,128]{2,1,0:T(8,128)(2,1)}), bf16[8,320,128]{2,1,0:T(8,128)(2,1)S(1)}, u32[]{:S(2)}, u32[]{:S(2)}) async-start(bf16[8,320,128]{2,1,0:T(8,128)(2,1)} %home_kernel.1), calls=%async_computation.3 | async-start | bytes 1310720 | tf_op jit(solution)/shard_map/all_to_all | solution.py:306
  114.6 5.0 %collective-permute-start.6 = (f32[64,128]{1,0:T(8,128)S(1)}, f32[64,128]{1,0:T(8,128)S(1)}, u32[]{:S(2)}, u32[]{:S(2)}) collective-permute-start(f32[64,128]{1,0:T(8,128)S(1)} %slice.10), channel_id=1, source_target_pairs={{0,1},{1,0},{2,3},{3,2},{4,5},{5,4},{6,7},{7,6},{8,9},{9,8},{10,11... | collective-permute-start | bytes 98312 | tf_op jit(solution)/shard_map/ppermute | solution.py:313

commit v4 on v3

--- a/solution.py
+++ b/solution.py
@@ -97,27 +97,12 @@
     out[...] = acc[:ROWS].astype(out.dtype)
 
 
-def backward_kernel(part, counts, core, lists, tiles, got, own, other, buffer, acc, *rest):
-    weight_sum, sems = rest if part == 1 else (None, *rest)
-    last = lists[part, jnp.maximum(counts[part], 1) - 1] & 255
-    chunks = jnp.where(counts[part] > 0, last // CHUNK + 1, 0)
-
-    @pl.loop(0, chunks)
-    def _(c):
-        tile_copy(tiles, buffer, sems, c).start()
-
+def backward_kernel(part, counts, core, lists, buffer, got, own, other, acc, weight_sum=None):
     acc[...] = jnp.zeros_like(acc)
     nodes = got.shape[1] - BLOCK
     if part == 1:
         reps = got.shape[0]
         weight_sum[...] = sum(got[k, nodes:].astype(jnp.float32) for k in range(reps))
-
-    def ready(done, need):
-        @pl.loop(done, need)
-        def _(c):
-            tile_copy(tiles, buffer, sems, c).wait()
-
-        return need
 
     def group(codes):
         products = []
@@ -130,7 +115,7 @@
         for code, product in zip(codes, products):
             acc[code >> PLACE_AT] += product
 
-    tile_groups(part, counts, lists, group, ready)
+    tile_groups(part, counts, lists, group, lambda done, need: need)
     feats = own.shape[1]
     own[:SPAN] = acc[:PART].reshape(SPAN, feats)
     other[:SPAN] = acc[PART:PLACES].reshape(SPAN, feats).astype(jnp.bfloat16)
@@ -139,6 +124,29 @@
         theirs = pl.multiple_of((1 - core[0]) * EXTRA, EXTRA)
         own[SPAN:] = weight_sum[pl.ds(mine, EXTRA), :]
         other[SPAN:] = weight_sum[pl.ds(theirs, EXTRA), :].astype(jnp.bfloat16)
+
+
+def middle_kernel(y_parts, weight, cotangent, hidden, sent):
+    reps, nodes, feats = y_parts.shape
+    y = sum(y_parts[k].astype(jnp.float32) for k in range(reps))
+    z = jnp.dot(
+        y,
+        weight[...].astype(jnp.float32),
+        precision=lax.Precision.HIGHEST,
+        preferred_element_type=jnp.float32,
+    )
+    sigma = jax.nn.sigmoid(z)
+    hidden[...] = (z * sigma).astype(jnp.bfloat16)
+    grad = cotangent[...].astype(jnp.float32) * sigma * (1.0 + z * (1.0 - sigma))
+    weight_part = jnp.dot(
+        y.T.astype(jnp.bfloat16), grad.astype(jnp.bfloat16), preferred_element_type=jnp.float32
+    ).astype(jnp.bfloat16)
+    for at in range(0, nodes, BLOCK):
+        grad_t = grad[at : at + BLOCK].T.astype(jnp.bfloat16)
+        for k in range(reps):
+            sent[k, pl.ds(at, BLOCK), :] = grad_t
+    for k in range(reps):
+        sent[k, nodes:] = weight_part
 
 
 def away_kernel(own, other, out):
@@ -156,6 +164,17 @@
         total = total + came[here, :].astype(jnp.float32)
         out[k, :nodes] = total.astype(jnp.bfloat16)
         out[k, nodes:] = weight
+
+
+def end_kernel(got, weight, grad_feats, weight_rows):
+    total = sum(got[k].astype(jnp.float32) for k in range(got.shape[0]))
+    nodes = grad_feats.shape[0]
+    for at in range(0, nodes, BLOCK):
+        grad_xw = total[at : at + BLOCK].T.astype(jnp.bfloat16)
+        grad_feats[pl.ds(at, BLOCK), :] = lax.dot_general(
+            grad_xw, weight[...], (((1,), (1,)), ((), ())), preferred_element_type=jnp.float32
+        ).astype(jnp.bfloat16)
+    weight_rows[...] = total[nodes:]
 
 
 SMEM = pl.BlockSpec(memory_space=pltpu.SMEM)
@@ -193,38 +212,34 @@
     )
 
 
-def backward_pass(part, counts, core, lists, tiles, got):
-    cap = tiles.shape[0]
+def backward_pass(part, counts, core, lists, held, got):
     feats = got.shape[2]
     size = SPAN + EXTRA * part
-    scratch = [
-        pltpu.VMEM((cap, BLOCK, BLOCK), jnp.bfloat16),
-        pltpu.VMEM((PLACES + 1, BLOCK, BLOCK), jnp.float32),
-        pltpu.SemaphoreType.DMA((cap // CHUNK,)),
-    ]
+    scratch = [pltpu.VMEM((PLACES + 1, BLOCK, BLOCK), jnp.float32)]
     if part == 1:
-        scratch.insert(2, pltpu.VMEM((BLOCK, BLOCK), jnp.float32))
+        scratch.append(pltpu.VMEM((BLOCK, BLOCK), jnp.float32))
     return pl.pallas_call(
         functools.partial(backward_kernel, part),
         out_shape=(
             jax.ShapeDtypeStruct((size, feats), jnp.float32),
             jax.ShapeDtypeStruct((size, feats), jnp.bfloat16),
         ),
-        in_specs=[SMEM, SMEM, SMEM, ANY, VMEM],
+        in_specs=[SMEM, SMEM, SMEM, VMEM, VMEM],
         out_specs=(VMEM, VMEM),
         scratch_shapes=scratch,
         compiler_params=pltpu.CompilerParams(vmem_limit_bytes=20 << 20),
-        cost_estimate=pl.CostEstimate(flops=1 << 30, bytes_accessed=9 << 20, transcendentals=0),
+        cost_estimate=pl.CostEstimate(flops=1 << 30, bytes_accessed=1 << 20, transcendentals=0),
         name=f"backward_tiles_{part}",
-    )(counts, core, lists, pltpu.with_memory_space_constraint(tiles, pltpu.HBM), got)
-
-
-def merge(kernel, shape, *arrays):
+    )(counts, core, lists, pltpu.with_memory_space_constraint(held, pltpu.VMEM), got)
+
+
+def merge(kernel, out_shape, *arrays):
+    out_specs = (VMEM,) * len(out_shape) if isinstance(out_shape, tuple) else VMEM
     return pl.pallas_call(
         kernel,
-        out_shape=jax.ShapeDtypeStruct(shape, jnp.bfloat16),
+        out_shape=out_shape,
         in_specs=[VMEM] * len(arrays),
-        out_specs=VMEM,
+        out_specs=out_specs,
         compiler_params=pltpu.CompilerParams(vmem_limit_bytes=16 << 20),
         cost_estimate=pl.CostEstimate(flops=1 << 20, bytes_accessed=4 << 20, transcendentals=0),
         name=kernel.__name__,
@@ -276,40 +291,43 @@
 
     reps = lax.axis_size(REP)
     y_parts = lax.all_to_all(y_part.reshape(reps, nodes, feats), REP, 0, 0)
-    y = jnp.sum(y_parts.astype(jnp.float32), axis=0)
-    z = jnp.dot(y, weight.astype(jnp.float32), precision=lax.Precision.HIGHEST)
-    sigma = jax.nn.sigmoid(z)
-    hidden = (z * sigma).astype(jnp.bfloat16)
-    grad_pre = (
-        cotangent[0].astype(jnp.float32) * sigma * (1.0 + z * (1.0 - sigma))
-    ).astype(jnp.bfloat16)
-
-    weight_part = lax.dot_general(
-        y.astype(jnp.bfloat16), grad_pre, (((0,), (0,)), ((), ())),
-        preferred_element_type=jnp.float32,
-    ).astype(jnp.bfloat16)
-    grad_t = jnp.swapaxes(grad_pre.reshape(nodes // BLOCK, BLOCK, feats), 1, 2)
-    got = spread(jnp.concatenate([grad_t.reshape(nodes, feats), weight_part]), REP)
-
-    core_id = core[None]
-    away_own, away_other = backward_pass(1, counts, core_id, lists, tiles, got)
+    hidden, sent = pl.pallas_call(
+        middle_kernel,
+        out_shape=(
+            jax.ShapeDtypeStruct((nodes, feats), jnp.bfloat16),
+            pltpu.VMEM((reps, nodes + feats, feats), jnp.bfloat16),
+        ),
+        in_specs=[VMEM, VMEM, VMEM],
+        out_specs=(VMEM, VMEM),
+        compiler_params=pltpu.CompilerParams(vmem_limit_bytes=16 << 20),
+        cost_estimate=pl.CostEstimate(flops=1 << 25, bytes_accessed=4 << 20, transcendentals=1 << 15),
+        name="middle",
+    )(y_parts, weight, cotangent[0])
+    got = lax.all_to_all(sent, REP, 0, 0)
+    away_own, away_other = backward_pass(1, counts, core[None], lists, held, got)
     away_other = lax.ppermute(away_other, "core", SWAP)
-    away = merge(away_kernel, away_own.shape, away_own, away_other)
-    core_id, away = lax.optimization_barrier((core_id, away))
+    away = merge(
+        away_kernel, jax.ShapeDtypeStruct(away_own.shape, jnp.bfloat16), away_own, away_other
+    )
+    counts, away = lax.optimization_barrier((counts, away))
     came = lax.ppermute(away, ALONG, NEXT)
-    home_own, home_other = backward_pass(0, counts, core_id, lists, tiles, got)
+    home_own, home_other = backward_pass(0, counts, core[None], lists, held, got)
     home_other = lax.ppermute(home_other, "core", SWAP)
     peers = lax.axis_size(PARITY)
     sent = merge(
-        home_kernel, (peers, nodes + EXTRA, feats), home_own, home_other, away_own, away_other, came
+        home_kernel,
+        pltpu.VMEM((peers, nodes + EXTRA, feats), jnp.bfloat16),
+        home_own, home_other, away_own, away_other, came,
     )
     got = lax.all_to_all(sent, PARITY, 0, 0)
-    total = jnp.sum(got.astype(jnp.float32), axis=0)
-    grad_xw_t = total[:nodes].astype(jnp.bfloat16).reshape(nodes // BLOCK, feats, BLOCK)
-    grad_feats = jnp.einsum(
-        "hfn,kf->hnk", grad_xw_t, weight, preferred_element_type=jnp.float32
-    ).astype(jnp.bfloat16)
-    mine = total[nodes:]
+    grad_feats, mine = merge(
+        end_kernel,
+        (
+            jax.ShapeDtypeStruct((nodes, feats), jnp.bfloat16),
+            jax.ShapeDtypeStruct((EXTRA, feats), jnp.float32),
+        ),
+        got, weight,
+    )
     theirs = lax.ppermute(mine, "core", SWAP)
     grad_weight = jnp.where(
         core == 0, jnp.concatenate([mine, theirs]), jnp.concatenate([theirs, mine])

time: 122 us -> 118 us (0.967)
  blocking collectives: 25.3 us -> 46.1 us
  waiting for transfers between devices: 41.5 us -> 26.5 us
  starting transfers between devices: 32.8 us -> 26.7 us
  matrix products: 1.9 us -> 0 us
    all_to_all x1 -> x2, blocking collectives: 12.8 us -> 33.6 us  [the longest x1 19.3 us: local(): got = lax.all_to_all(sent, PARITY, 0, 0)]
    all_to_all x1 -> x0, waiting for transfers between devices: 16.7 us -> none  [local(): got = lax.all_to_all(sent, PARITY, 0, 0)]
    all_to_all x1 -> x0, starting transfers between devices: 6.7 us -> none  [local(): got = lax.all_to_all(sent, PARITY, 0, 0)]
    pallas_call x2, Pallas kernels: 6.53 us -> 4.19 us  [backward_pass(): pl.pallas_call(functools.partial(backward_kernel, part), out_shape=(jax.S...]
    dot_general x3 -> x0, matrix products: 1.9 us -> none  [the longest x1 0.88 us: local(): z = jnp.dot(y, weight.astype(jnp.float32), precision=lax.Precision.HIGHEST)]
    ppermute x1, waiting for transfers between devices: 1.23 us -> 2.92 us  [local(): came = lax.ppermute(away, ALONG, NEXT)]
    ppermute x1, starting transfers between devices: 4.1 us -> 5.34 us  [local(): theirs = lax.ppermute(mine, 'core', SWAP)]
  transfers between devices with their start and end apart: 9 -> 8, of which waited for: 8 -> 8; matrix products, arithmetic and copies ran while one was open for 2% -> 2% of each run, Pallas kernels for 5% -> 5%
where the time goes in v4:
time: 118 us; the launch traced here: 117 us
  blocking collectives  46.1 us (39%)
  starting transfers between devices  26.7 us (23%)
  waiting for transfers between devices  26.5 us (22%)
  Pallas kernels  12.1 us (10%)
  other arithmetic  2.55 us (2%)
  local copies, waits for them, and re-layouts  1.72 us (1%)
  between operations  1.37 us (1%)
    all_to_all x1, blocking collectives, local(): got = lax.all_to_all(sent, PARITY, 0, 0)  19.3 us
    all_to_all x1, blocking collectives, local(): got = lax.all_to_all(sent, REP, 0, 0)  14.3 us
    all_to_all x1, waiting for transfers between devices, spread(): lax.all_to_all(jnp.broadcast_to(block[None], (n, *block.shape)), axes, 0, 0)  12.8 us
    all_to_all x1, blocking collectives, local(): y_parts = lax.all_to_all(y_part.reshape(reps, nodes, feats), REP, 0, 0)  12.5 us
    all_to_all x1, starting transfers between devices, spread(): lax.all_to_all(jnp.broadcast_to(block[None], (n, *block.shape)), axes, 0, 0)  11.6 us
    pallas_call x2, Pallas kernels, forward_pass(): pl.pallas_call(functools.partial(forward_kernel, part), out_shape=(out, p...  5.76 us
    ppermute x1, starting transfers between devices, local(): theirs = lax.ppermute(mine, 'core', SWAP)  5.34 us
    pallas_call x2, Pallas kernels, backward_pass(): pl.pallas_call(functools.partial(backward_kernel, part), out_shape=(jax.S...  4.19 us
  transfers between devices with their start and end apart: 8, of which 8 were waited for; matrix products, arithmetic and copies ran while one was open for 2% of the time, Pallas kernels for 5%

profile of v4, /device:TPU:1, one launch (start us, length us, event | category | flops | bytes accessed | tf_op | source)
XLA Modules:
  0.0 117.1 jit_solution(18113984852138543954)
XLA Ops:
  0.6 1.7 %broadcast_in_dim.36 = bf16[8,256,128]{2,1,0:T(8,128)(2,1)} broadcast(bf16[256,128]{1,0:T(8,128)(2,1)} %bitcast.22), dimensions={1,2} | broadcast | bytes 589824 | tf_op jit(solution)/shard_map/broadcast_in_dim | solution.py:251
  2.3 11.6 %all-to-all-start = ((bf16[8,256,128]{2,1,0:T(8,128)(2,1)}), bf16[8,256,128]{2,1,0:T(8,128)(2,1)S(1)}, u32[]{:S(2)}, u32[]{:S(2)}) async-start(bf16[8,256,128]{2,1,0:T(8,128)(2,1)} %broadcast_in_dim.36), calls=%async_computation | async-start | bytes 1048576 | tf_op jit(solution)/shard_map/all_to_all | solution.py:251
  14.6 0.7 broadcast_shift-left_fusion
  15.3 0.7 or_add_fusion
  16.0 0.2 convert_reduce_fusion
  16.3 12.8 %all-to-all-done = bf16[8,256,128]{2,1,0:T(8,128)(2,1)S(1)} async-done(((bf16[8,256,128]{2,1,0:T(8,128)(2,1)}), bf16[8,256,128]{2,1,0:T(8,128)(2,1)S(1)}, u32[]{:S(2)}, u32[]{:S(2)}) %all-to-all-start) | async-done | bytes 524320 | tf_op jit(solution)/shard_map/all_to_all | solution.py:251
  29.1 3.3 %collective-permute-start = (bf16[8,256,128]{2,1,0:T(8,128)(2,1)S(1)}, bf16[8,256,128]{2,1,0:T(8,128)(2,1)S(1)}, u32[]{:S(2)}, u32[]{:S(2)}) collective-permute-start(bf16[8,256,128]{2,1,0:T(8,128)(2,1)S(1)} %all-to-all-done), channel_id=1, source_target_pairs={{0,1},{1,0},{2,3},{3,2},{4,5},{5,4},{6,7},{7,6},{8,9},{9,8},{10,11... | collective-permute-start | bytes 1572872 | tf_op jit(solution)/shard_map/ppermute | solution.py:282
  32.3 0.2 select_reduce_fusion
  32.6 1.2 %collective-permute-done = bf16[8,256,128]{2,1,0:T(8,128)(2,1)S(1)} collective-permute-done((bf16[8,256,128]{2,1,0:T(8,128)(2,1)S(1)}, bf16[8,256,128]{2,1,0:T(8,128)(2,1)S(1)}, u32[]{:S(2)}, u32[]{:S(2)}) %collective-permute-start) | collective-permute-done | bytes 524320 | tf_op jit(solution)/shard_map/ppermute | solution.py:282
  33.9 4.0 %forward_tiles_0.1 = (f32[16,128,128]{2,1,0:T(8,128)S(1)}, bf16[256,128,128]{2,1,0:T(8,128)(2,1)S(1)}) custom-call(s32[2]{0:T(128)S(1)} %get-tuple-element.25.counts, s32[2,256]{1,0:T(2,128)S(1)} %get-tuple-element.34.lists, bf16[256,128,128]{2,1,0:T(8,128)(2,1)} %bitcast.21, bf16[16,128,128]{2,1,0:T(8,128)(2,1)S(1)} %bitcast.16, ...), custom_call_target="tpu_custom_call" | custom-call | flops 1073741824 | bytes 9437184 | tf_op jit(solution)/shard_map/forward_tiles_0/pallas_call | solution.py:197
  37.9 4.1 %collective-permute-done.1 = bf16[8,256,128]{2,1,0:T(8,128)(2,1)S(1)} collective-permute-done((bf16[8,256,128]{2,1,0:T(8,128)(2,1)S(1)}, bf16[8,256,128]{2,1,0:T(8,128)(2,1)S(1)}, u32[]{:S(2)}, u32[]{:S(2)}) %collective-permute-start.1) | collective-permute-done | bytes 524320 | tf_op jit(solution)/shard_map/ppermute | solution.py:281
  42.0 0.7 collective-permute-start.2
  42.7 1.5 %collective-permute-done.2 = bf16[8,256,128]{2,1,0:T(8,128)(2,1)S(1)} collective-permute-done((bf16[8,256,128]{2,1,0:T(8,128)(2,1)S(1)}, bf16[8,256,128]{2,1,0:T(8,128)(2,1)S(1)}, u32[]{:S(2)}, u32[]{:S(2)}) %collective-permute-start.2) | collective-permute-done | bytes 524320 | tf_op jit(solution)/shard_map/ppermute | solution.py:287
  44.3 1.8 %forward_tiles_1.1 = bf16[16,128,128]{2,1,0:T(8,128)(2,1)S(1)} custom-call(s32[2]{0:T(128)S(1)} %get-tuple-element.25.counts, s32[2,256]{1,0:T(2,128)S(1)} %get-tuple-element.34.lists, bf16[256,128,128]{2,1,0:T(8,128)(2,1)S(1)} %get-tuple-element.17.tiles.buffer, f32[16,128,128]{2,1,0:T(8,128)S(1)} %get-tuple-element.19.rest_0_, ...), custom_call_target="tpu_custom_call" | custom-call | flops 1073741824 | bytes 9437184 | tf_op jit(solution)/shard_map/forward_tiles_1/pallas_call | solution.py:197
  46.0 12.5 %all_to_all.20.y_parts = bf16[8,256,128]{2,1,0:T(8,128)(2,1)S(1)} all-to-all(bf16[8,256,128]{2,1,0:T(8,128)(2,1)S(1)} %bitcast.15), channel_id=1, replica_groups=mesh['x'=4,'ylo'=2,'yhi'=2,'zq'=4,'zp'=2,'core'=2] {'x','ylo'}, dimensions={0} | all-to-all | bytes 1048576 | tf_op jit(solution)/shard_map/all_to_all | solution.py:293
  58.6 0.9 middle.1
  59.5 14.3 %all_to_all.21.got = bf16[8,384,128]{2,1,0:T(8,128)(2,1)S(1)} all-to-all(bf16[8,384,128]{2,1,0:T(8,128)(2,1)S(1)} %get-tuple-element.22), channel_id=1, replica_groups=mesh['x'=4,'ylo'=2,'yhi'=2,'zq'=4,'zp'=2,'core'=2] {'x','ylo'}, dimensions={0} | all-to-all | bytes 1572864 | tf_op jit(solution)/shard_map/all_to_all | solution.py:306
  73.8 1.9 %backward_tiles_1.1 = (f32[2112,128]{1,0:T(8,128)S(1)}, bf16[2112,128]{1,0:T(8,128)(2,1)S(1)}) custom-call(s32[2]{0:T(128)S(1)} %get-tuple-element.25.counts, s32[1]{0:T(128)} %bitcast.12.core, s32[2,256]{1,0:T(2,128)S(1)} %get-tuple-element.34.lists, bf16[256,128,128]{2,1,0:T(8,128)(2,1)S(1)} %get-tuple-element.17.tiles.buffer, ...), custom_call_target="tpu_custom_call" | custom-call | flops 1073741824 | bytes 1048576 | tf_op jit(solution)/shard_map/backward_tiles_1/pallas_call | solution.py:221
  75.7 2.8 %collective-permute-start.3 = (bf16[2112,128]{1,0:T(8,128)(2,1)S(1)}, bf16[2112,128]{1,0:T(8,128)(2,1)S(1)}, u32[]{:S(2)}, u32[]{:S(2)}) collective-permute-start(bf16[2112,128]{1,0:T(8,128)(2,1)S(1)} %get-tuple-element.24), channel_id=1, source_target_pairs={{0,1},{1,0},{2,3},{3,2},{4,5},{5,4},{6,7},{7,6},{8,9},{9,8},{10,11... | collective-permute-start | bytes 1622024 | tf_op jit(solution)/shard_map/ppermute | solution.py:308
  78.5 1.6 %collective-permute-done.3.other.away_other = bf16[2112,128]{1,0:T(8,128)(2,1)S(1)} collective-permute-done((bf16[2112,128]{1,0:T(8,128)(2,1)S(1)}, bf16[2112,128]{1,0:T(8,128)(2,1)S(1)}, u32[]{:S(2)}, u32[]{:S(2)}) %collective-permute-start.3) | collective-permute-done | bytes 540704 | tf_op jit(solution)/shard_map/ppermute | solution.py:308
  80.0 0.1 away_kernel.1
  80.2 1.0 collective-permute-start.5
  81.2 2.3 %backward_tiles_0.1 = (f32[2048,128]{1,0:T(8,128)S(1)}, bf16[2048,128]{1,0:T(8,128)(2,1)S(1)}) custom-call(s32[2]{0:T(128)S(1)} %get-tuple-element.25.counts, s32[1]{0:T(128)} %bitcast.12.core, s32[2,256]{1,0:T(2,128)S(1)} %get-tuple-element.34.lists, bf16[256,128,128]{2,1,0:T(8,128)(2,1)S(1)} %get-tuple-element.17.tiles.buffer, ...), custom_call_target="tpu_custom_call" | custom-call | flops 1073741824 | bytes 1048576 | tf_op jit(solution)/shard_map/backward_tiles_0/pallas_call | solution.py:221
  83.5 2.0 %collective-permute-start.4 = (bf16[2048,128]{1,0:T(8,128)(2,1)S(1)}, bf16[2048,128]{1,0:T(8,128)(2,1)S(1)}, u32[]{:S(2)}, u32[]{:S(2)}) collective-permute-start(bf16[2048,128]{1,0:T(8,128)(2,1)S(1)} %get-tuple-element.27), channel_id=1, source_target_pairs={{0,1},{1,0},{2,3},{3,2},{4,5},{5,4},{6,7},{7,6},{8,9},{9,8},{10,11... | collective-permute-start | bytes 1572872 | tf_op jit(solution)/shard_map/ppermute | solution.py:315
  85.5 1.5 %collective-permute-done.4.other = bf16[2048,128]{1,0:T(8,128)(2,1)S(1)} collective-permute-done((bf16[2048,128]{1,0:T(8,128)(2,1)S(1)}, bf16[2048,128]{1,0:T(8,128)(2,1)S(1)}, u32[]{:S(2)}, u32[]{:S(2)}) %collective-permute-start.4) | collective-permute-done | bytes 524320 | tf_op jit(solution)/shard_map/ppermute | solution.py:315
  87.0 2.9 %collective-permute-done.5.came = bf16[2112,128]{1,0:T(8,128)(2,1)S(1)} collective-permute-done((bf16[2112,128]{1,0:T(8,128)(2,1)S(1)}, bf16[2112,128]{1,0:T(8,128)(2,1)S(1)}, u32[]{:S(2)}, u32[]{:S(2)}) %collective-permute-start.5) | collective-permute-done | bytes 540704 | tf_op jit(solution)/shard_map/ppermute | solution.py:313
  89.9 0.2 home_kernel.1
  90.1 19.3 %all_to_all.22.got = bf16[8,320,128]{2,1,0:T(8,128)(2,1)S(1)} all-to-all(bf16[8,320,128]{2,1,0:T(8,128)(2,1)S(1)} %home_kernel.1), channel_id=1, replica_groups=mesh['x'=4,'ylo'=2,'yhi'=2,'zq'=4,'zp'=2,'core'=2] {'yhi','zq'}, dimensions={0} | all-to-all | bytes 1310720 | tf_op jit(solution)/shard_map/all_to_all | solution.py:322
  109.4 0.9 end_kernel.1
  110.3 5.3 %collective-permute-start.6 = (f32[64,128]{1,0:T(8,128)S(1)}, f32[64,128]{1,0:T(8,128)S(1)}, u32[]{:S(2)}, u32[]{:S(2)}) collective-permute-start(f32[64,128]{1,0:T(8,128)S(1)} %get-tuple-element.30), channel_id=1, source_target_pairs={{0,1},{1,0},{2,3},{3,2},{4,5},{5,4},{6,7},{7,6},{8,9},{9,8},{10,11... | collective-permute-start | bytes 98312 | tf_op jit(solution)/shard_map/ppermute | solution.py:331
  115.6 0.9 collective-permute-done.6
  116.5 0.6 maximum_select_fusion
  (9 shorter events, 0.2 us)
Async XLA Ops:
  2.3 26.7 %all-to-all-start = ((bf16[8,256,128]{2,1,0:T(8,128)(2,1)}), bf16[8,256,128]{2,1,0:T(8,128)(2,1)S(1)}, u32[]{:S(2)}, u32[]{:S(2)}) async-start(bf16[8,256,128]{2,1,0:T(8,128)(2,1)} %broadcast_in_dim.36), calls=%async_computation | async-start | bytes 1048576 | tf_op jit(solution)/shard_map/all_to_all | solution.py:251
  29.1 4.8 %collective-permute-start = (bf16[8,256,128]{2,1,0:T(8,128)(2,1)S(1)}, bf16[8,256,128]{2,1,0:T(8,128)(2,1)S(1)}, u32[]{:S(2)}, u32[]{:S(2)}) collective-permute-start(bf16[8,256,128]{2,1,0:T(8,128)(2,1)S(1)} %all-to-all-done), channel_id=1, source_target_pairs={{0,1},{1,0},{2,3},{3,2},{4,5},{5,4},{6,7},{7,6},{8,9},{9,8},{10,11... | collective-permute-start | bytes 1572872 | tf_op jit(solution)/shard_map/ppermute | solution.py:282
  32.3 9.7 %collective-permute-start.1 = (bf16[8,256,128]{2,1,0:T(8,128)(2,1)S(1)}, bf16[8,256,128]{2,1,0:T(8,128)(2,1)S(1)}, u32[]{:S(2)}, u32[]{:S(2)}) collective-permute-start(bf16[8,256,128]{2,1,0:T(8,128)(2,1)S(1)} %all-to-all-done), channel_id=1, source_target_pairs={{0,2},{2,4},{4,6},{6,8},{8,10},{10,12},{12,14},{14,0},{1,15},{3,1}... | collective-permute-start | bytes 1572872 | tf_op jit(solution)/shard_map/ppermute | solution.py:281
  37.9 20.7 %copy-start = (bf16[128,128]{1,0:T(8,128)(2,1)S(1)}, bf16[128,128]{1,0:T(8,128)(2,1)}, u32[]{:S(2)}) copy-start(bf16[128,128]{1,0:T(8,128)(2,1)} %weight.3) | copy-start | bytes 98308
  37.9 20.7 %copy-start.1 = (bf16[1,256,128]{2,1,0:T(8,128)(2,1)S(1)}, bf16[1,256,128]{2,1,0:T(8,128)(2,1)}, u32[]{:S(2)}) copy-start(bf16[1,256,128]{2,1,0:T(8,128)(2,1)} %param.9) | copy-start | bytes 196612
  42.0 2.3 %collective-permute-start.2 = (bf16[8,256,128]{2,1,0:T(8,128)(2,1)S(1)}, bf16[8,256,128]{2,1,0:T(8,128)(2,1)S(1)}, u32[]{:S(2)}, u32[]{:S(2)}) collective-permute-start(bf16[8,256,128]{2,1,0:T(8,128)(2,1)S(1)} %collective-permute-done.1), channel_id=1, source_target_pairs={{0,1},{1,0},{2,3},{3,2},{4,5},{5,4},{6,7},{7,6},{8,9},{9,8},{10,11... | collective-permute-start | bytes 1572872 | tf_op jit(solution)/shard_map/ppermute | solution.py:287
  75.7 4.3 %collective-permute-start.3 = (bf16[2112,128]{1,0:T(8,128)(2,1)S(1)}, bf16[2112,128]{1,0:T(8,128)(2,1)S(1)}, u32[]{:S(2)}, u32[]{:S(2)}) collective-permute-start(bf16[2112,128]{1,0:T(8,128)(2,1)S(1)} %get-tuple-element.24), channel_id=1, source_target_pairs={{0,1},{1,0},{2,3},{3,2},{4,5},{5,4},{6,7},{7,6},{8,9},{9,8},{10,11... | collective-permute-start | bytes 1622024 | tf_op jit(solution)/shard_map/ppermute | solution.py:308
  80.2 9.7 %collective-permute-start.5 = (bf16[2112,128]{1,0:T(8,128)(2,1)S(1)}, bf16[2112,128]{1,0:T(8,128)(2,1)S(1)}, u32[]{:S(2)}, u32[]{:S(2)}) collective-permute-start(bf16[2112,128]{1,0:T(8,128)(2,1)S(1)} %away_kernel.1), channel_id=1, source_target_pairs={{0,2},{2,4},{4,6},{6,8},{8,10},{10,12},{12,14},{14,0},{1,15},{3,1}... | collective-permute-start | bytes 1622024 | tf_op jit(solution)/shard_map/ppermute | solution.py:313
  83.5 3.5 %collective-permute-start.4 = (bf16[2048,128]{1,0:T(8,128)(2,1)S(1)}, bf16[2048,128]{1,0:T(8,128)(2,1)S(1)}, u32[]{:S(2)}, u32[]{:S(2)}) collective-permute-start(bf16[2048,128]{1,0:T(8,128)(2,1)S(1)} %get-tuple-element.27), channel_id=1, source_target_pairs={{0,1},{1,0},{2,3},{3,2},{4,5},{5,4},{6,7},{7,6},{8,9},{9,8},{10,11... | collective-permute-start | bytes 1572872 | tf_op jit(solution)/shard_map/ppermute | solution.py:315
  110.3 6.2 %collective-permute-start.6 = (f32[64,128]{1,0:T(8,128)S(1)}, f32[64,128]{1,0:T(8,128)S(1)}, u32[]{:S(2)}, u32[]{:S(2)}) collective-permute-start(f32[64,128]{1,0:T(8,128)S(1)} %get-tuple-element.30), channel_id=1, source_target_pairs={{0,1},{1,0},{2,3},{3,2},{4,5},{5,4},{6,7},{7,6},{8,9},{9,8},{10,11... | collective-permute-start | bytes 98312 | tf_op jit(solution)/shard_map/ppermute | solution.py:331

commit v5 on v4

--- a/solution.py
+++ b/solution.py
@@ -14,6 +14,9 @@
 PART = PLACES // 2
 ROW_AT, PLACE_AT = 8, 13
 SPARE = (ROWS << ROW_AT) | (PLACES << PLACE_AT)
+CAP = 256
+COUNT_AT = CAP
+WIDTH = CAP + 128
 SPAN = PART * BLOCK
 EXTRA = BLOCK // 2
 SIZES = (4, 2, 2, 4, 2, 2)
@@ -33,8 +36,8 @@
     return pltpu.make_async_copy(tiles.at[span], buffer.at[span], sems.at[chunk])
 
 
-def tile_groups(part, counts, lists, group, ready):
-    count = counts[part]
+def tile_groups(part, lists, group, ready):
+    count = lists[part, COUNT_AT]
 
     def step(k, done):
         base = k * CHUNK
@@ -46,13 +49,13 @@
     return lax.fori_loop(0, (count + CHUNK - 1) // CHUNK, step, 0)
 
 
-def forward_kernel(part, counts, lists, tiles, *rest):
+def forward_kernel(part, lists, tiles, *rest):
     if part == 0:
         x0, x1, out, buffer, xs, acc, xsems, sems = rest
     else:
         before, x0, x1, out, xs, acc, xsems = rest
         buffer = tiles
-    chunks = (counts[0] + counts[1] + CHUNK - 1) // CHUNK
+    chunks = (lists[0, COUNT_AT] + lists[1, COUNT_AT] + CHUNK - 1) // CHUNK
     moves = [
         pltpu.make_async_copy(source, xs.at[pl.ds(k * PART, PART)], xsems.at[k])
         for k, source in enumerate((x0, x1))
@@ -92,12 +95,12 @@
         for code, product in zip(codes, products):
             acc[(code >> ROW_AT) & 31] += product
 
-    done = tile_groups(part, counts, lists, group, ready)
+    done = tile_groups(part, lists, group, ready)
     ready(done, chunks)
     out[...] = acc[:ROWS].astype(out.dtype)
 
 
-def backward_kernel(part, counts, core, lists, buffer, got, own, other, acc, weight_sum=None):
+def backward_kernel(part, lists, buffer, got, own, other, acc, weight_sum=None):
     acc[...] = jnp.zeros_like(acc)
     nodes = got.shape[1] - BLOCK
     if part == 1:
@@ -115,13 +118,14 @@
         for code, product in zip(codes, products):
             acc[code >> PLACE_AT] += product
 
-    tile_groups(part, counts, lists, group, lambda done, need: need)
+    tile_groups(part, lists, group, lambda done, need: need)
     feats = own.shape[1]
     own[:SPAN] = acc[:PART].reshape(SPAN, feats)
     other[:SPAN] = acc[PART:PLACES].reshape(SPAN, feats).astype(jnp.bfloat16)
     if part == 1:
-        mine = pl.multiple_of(core[0] * EXTRA, EXTRA)
-        theirs = pl.multiple_of((1 - core[0]) * EXTRA, EXTRA)
+        core = lax.axis_index("core")
+        mine = pl.multiple_of(core * EXTRA, EXTRA)
+        theirs = pl.multiple_of((1 - core) * EXTRA, EXTRA)
         own[SPAN:] = weight_sum[pl.ds(mine, EXTRA), :]
         other[SPAN:] = weight_sum[pl.ds(theirs, EXTRA), :].astype(jnp.bfloat16)
 
@@ -166,23 +170,84 @@
         out[k, nodes:] = weight
 
 
-def end_kernel(got, weight, grad_feats, weight_rows):
-    total = sum(got[k].astype(jnp.float32) for k in range(got.shape[0]))
+def weight_kernel(got, weight_rows):
+    nodes = got.shape[1] - EXTRA
+    weight_rows[...] = sum(got[k, nodes:].astype(jnp.float32) for k in range(got.shape[0]))
+
+
+def feats_kernel(got, weight, grad_feats):
     nodes = grad_feats.shape[0]
     for at in range(0, nodes, BLOCK):
-        grad_xw = total[at : at + BLOCK].T.astype(jnp.bfloat16)
-        grad_feats[pl.ds(at, BLOCK), :] = lax.dot_general(
-            grad_xw, weight[...], (((1,), (1,)), ((), ())), preferred_element_type=jnp.float32
+        here = pl.ds(at, BLOCK)
+        total = sum(got[k, here].astype(jnp.float32) for k in range(got.shape[0]))
+        grad_feats[here, :] = lax.dot_general(
+            total.T.astype(jnp.bfloat16),
+            weight[...],
+            (((1,), (1,)), ((), ())),
+            preferred_element_type=jnp.float32,
         ).astype(jnp.bfloat16)
-    weight_rows[...] = total[nodes:]
-
-
-SMEM = pl.BlockSpec(memory_space=pltpu.SMEM)
+
+
+def join_kernel(mine, theirs, grad_weight):
+    core = lax.axis_index("core")
+    at = pl.multiple_of(core * EXTRA, EXTRA)
+    grad_weight[pl.ds(at, EXTRA), :] = mine[...]
+    at = pl.multiple_of((1 - core) * EXTRA, EXTRA)
+    grad_weight[pl.ds(at, EXTRA), :] = theirs[...]
+
+
+def fan_kernel(block, out, sem):
+    copy = pltpu.make_async_copy(block, out.at[0], sem)
+    copy.start()
+    copy.wait()
+    for k in range(1, out.shape[0]):
+        out[k] = out[0]
+
+
+def lists_kernel(count, row_ids, col_ids, out, rows, cols, held, sems):
+    moves = [
+        pltpu.make_async_copy(row_ids, rows, sems.at[0]),
+        pltpu.make_async_copy(col_ids, cols, sems.at[1]),
+    ]
+    for move in moves:
+        move.start()
+    for move in moves:
+        move.wait()
+    slots = lax.broadcasted_iota(jnp.int32, (1, CAP), 1)
+    block = cols[...]
+    z = (block >> 2) & 7
+    core = ((block >> 1) & 1) ^ lax.axis_index("core")
+    part = (z & 1) ^ lax.axis_index("zp")
+    place = core * PART + ((block >> 5) * 4 + (z >> 1)) * 2 + (block & 1)
+    code = slots | (rows[...] << ROW_AT) | (place << PLACE_AT)
+    part = jnp.where(slots < count[0], part, 2).astype(jnp.float32)
+    code = (code - SPARE).astype(jnp.float32)
+
+    square = (CAP, CAP)
+    across = jnp.broadcast_to(part, square)
+    down = across.T
+    code = jnp.broadcast_to(code, square).T
+    lane = lax.broadcasted_iota(jnp.int32, square, 1)
+    earlier = (lane < lax.broadcasted_iota(jnp.int32, square, 0)) & (across == down)
+    rank = jnp.sum(jnp.where(earlier, 1.0, 0.0), axis=1, keepdims=True)
+    at_rank = rank == lane.astype(jnp.float32)
+    for p in range(2):
+        listed = jnp.where(at_rank & (down == p), code, 0.0)
+        entries = jnp.sum(listed, axis=0, keepdims=True).astype(jnp.int32) + SPARE
+        size = jnp.sum(jnp.where(part == p, 1.0, 0.0), axis=1, keepdims=True)
+        held[pl.ds(p, 1), :CAP] = entries
+        held[pl.ds(p, 1), CAP:] = jnp.broadcast_to(size, (1, WIDTH - CAP)).astype(jnp.int32)
+    copy = pltpu.make_async_copy(held, out, sems.at[2])
+    copy.start()
+    copy.wait()
+
+
+SMEM = pl.BSMEM = pl.BSMEM = pl.BlockSpec(memory_space=pltpu.SMEM)
 VMEM = pl.BlockSpec(memory_space=pltpu.VMEM)
 ANY = pl.BlockSpec(memory_space=pl.ANY)
 
 
-def forward_pass(part, counts, lists, tiles, parts, before=()):
+def forward_pass(part, lists, tiles, parts, before=()):
     cap = tiles.shape[0]
     out = jax.ShapeDtypeStruct(
         (ROWS, BLOCK, BLOCK), jnp.float32 if part == 0 else jnp.bfloat16
@@ -197,22 +262,21 @@
     return pl.pallas_call(
         functools.partial(forward_kernel, part),
         out_shape=(out, pltpu.VMEM((cap, BLOCK, BLOCK), jnp.bfloat16)) if part == 0 else out,
-        in_specs=[SMEM, SMEM, ANY if part == 0 else VMEM] + [VMEM] * len(before) + [ANY, ANY],
+        in_specs=[SMEM, ANY if part == 0 else VMEM] + [VMEM] * len(before) + [ANY, ANY],
         out_specs=(VMEM, VMEM) if part == 0 else VMEM,
         scratch_shapes=scratch,
         compiler_params=pltpu.CompilerParams(vmem_limit_bytes=20 << 20),
         cost_estimate=pl.CostEstimate(flops=1 << 30, bytes_accessed=9 << 20, transcendentals=0),
         name=f"forward_tiles_{part}",
     )(
-        counts,
-        lists,
+        pltpu.with_memory_space_constraint(lists, pltpu.SMEM),
         pltpu.with_memory_space_constraint(tiles, pltpu.HBM if part == 0 else pltpu.VMEM),
         *before,
         *parts,
     )
 
 
-def backward_pass(part, counts, core, lists, held, got):
+def backward_pass(part, lists, held, got):
     feats = got.shape[2]
     size = SPAN + EXTRA * part
     scratch = [pltpu.VMEM((PLACES + 1, BLOCK, BLOCK), jnp.float32)]
@@ -224,13 +288,13 @@
             jax.ShapeDtypeStruct((size, feats), jnp.float32),
             jax.ShapeDtypeStruct((size, feats), jnp.bfloat16),
         ),
-        in_specs=[SMEM, SMEM, SMEM, VMEM, VMEM],
+        in_specs=[SMEM, VMEM, VMEM],
         out_specs=(VMEM, VMEM),
         scratch_shapes=scratch,
         compiler_params=pltpu.CompilerParams(vmem_limit_bytes=20 << 20),
         cost_estimate=pl.CostEstimate(flops=1 << 30, bytes_accessed=1 << 20, transcendentals=0),
         name=f"backward_tiles_{part}",
-    )(counts, core, lists, pltpu.with_memory_space_constraint(held, pltpu.VMEM), got)
+    )(pltpu.with_memory_space_constraint(lists, pltpu.SMEM), pltpu.with_memory_space_constraint(held, pltpu.VMEM), got)
 
 
 def merge(kernel, out_shape, *arrays):
@@ -248,45 +312,58 @@
 
 def spread(block, axes):
     n = lax.axis_size(axes)
-    return lax.all_to_all(jnp.broadcast_to(block[None], (n, *block.shape)), axes, 0, 0)
-
-
-def tile_lists(rows, cols, count, parity, core):
-    slots = jnp.arange(rows.shape[0], dtype=jnp.int32)
-    z = (cols // 4) % 8
-    part = (z % 2) ^ parity
-    place = (((cols // 2) % 2) ^ core) * PART + ((cols // 32) * 4 + z // 2) * 2 + cols % 2
-    code = slots | (rows << ROW_AT) | (place << PLACE_AT)
-    part = jnp.where(slots < count, part, 2)
-    earlier = (slots[None, :] < slots[:, None]) & (part[None, :] == part[:, None])
-    rank = jnp.sum(earlier.astype(jnp.int32), axis=1)
-    parts = jnp.arange(2, dtype=jnp.int32)[:, None]
-    mine = part[None, :] == parts
-    hit = mine[:, None, :] & (rank[None, None, :] == slots[None, :, None])
-    lists = SPARE + jnp.sum(jnp.where(hit, code - SPARE, 0), axis=2)
-    return jnp.sum(mine.astype(jnp.int32), axis=1), lists
+    blocks = pl.pallas_call(
+        fan_kernel,
+        out_shape=pltpu.VMEM((n, *block.shape), block.dtype),
+        in_specs=[ANY],
+        out_specs=VMEM,
+        scratch_shapes=[pltpu.SemaphoreType.DMA],
+        compiler_params=pltpu.CompilerParams(vmem_limit_bytes=16 << 20),
+        cost_estimate=pl.CostEstimate(flops=0, bytes_accessed=1 << 16, transcendentals=0),
+        name="fan",
+    )(pltpu.with_memory_space_constraint(block, pltpu.HBM))
+    return lax.all_to_all(blocks, axes, 0, 0)
+
+
+def tile_lists(count, rows, cols):
+    return pl.pallas_call(
+        lists_kernel,
+        out_shape=pltpu.SMEM((2, WIDTH), jnp.int32),
+        in_specs=[SMEM, ANY, ANY],
+        out_specs=SMEM,
+        scratch_shapes=[
+            pltpu.VMEM((1, CAP), jnp.int32),
+            pltpu.VMEM((1, CAP), jnp.int32),
+            pltpu.VMEM((2, WIDTH), jnp.int32),
+            pltpu.SemaphoreType.DMA((3,)),
+        ],
+        compiler_params=pltpu.CompilerParams(vmem_limit_bytes=16 << 20),
+        cost_estimate=pl.CostEstimate(flops=1 << 20, bytes_accessed=1 << 12, transcendentals=0),
+        name="lists",
+    )(
+        count,
+        pltpu.with_memory_space_constraint(rows, pltpu.HBM),
+        pltpu.with_memory_space_constraint(cols, pltpu.HBM),
+    )
 
 
 def local(features, weight, cotangent, tiles, row_ids, col_ids, counts):
     x = features[0]
     nodes, feats = x.shape
     tiles = tiles[0, 0]
-    core = lax.axis_index("core")
-    counts, lists = tile_lists(
-        row_ids[0, 0], col_ids[0, 0], counts[0, 0], lax.axis_index("zp"), core
-    )
+    lists = tile_lists(counts[0], row_ids[0], col_ids[0])
     blocks = (PART, BLOCK, feats)
 
     own = spread(x, PARITY)
     beside = lax.ppermute(own, ALONG, NEXT)
     own_other = lax.ppermute(own, "core", SWAP)
     y_part, held = forward_pass(
-        0, counts, lists, tiles, (own.reshape(blocks), own_other.reshape(blocks))
+        0, lists, tiles, (own.reshape(blocks), own_other.reshape(blocks))
     )
     beside, y_part = lax.optimization_barrier((beside, y_part))
     beside_other = lax.ppermute(beside, "core", SWAP)
     y_part = forward_pass(
-        1, counts, lists, held, (beside.reshape(blocks), beside_other.reshape(blocks)), (y_part,)
+        1, lists, held, (beside.reshape(blocks), beside_other.reshape(blocks)), (y_part,)
     )
 
     reps = lax.axis_size(REP)
@@ -304,14 +381,14 @@
         name="middle",
     )(y_parts, weight, cotangent[0])
     got = lax.all_to_all(sent, REP, 0, 0)
-    away_own, away_other = backward_pass(1, counts, core[None], lists, held, got)
+    away_own, away_other = backward_pass(1, lists, held, got)
     away_other = lax.ppermute(away_other, "core", SWAP)
     away = merge(
         away_kernel, jax.ShapeDtypeStruct(away_own.shape, jnp.bfloat16), away_own, away_other
     )
-    counts, away = lax.optimization_barrier((counts, away))
+    held, away = lax.optimization_barrier((held, away))
     came = lax.ppermute(away, ALONG, NEXT)
-    home_own, home_other = backward_pass(0, counts, core[None], lists, held, got)
+    home_own, home_other = backward_pass(0, lists, held, got)
     home_other = lax.ppermute(home_other, "core", SWAP)
     peers = lax.axis_size(PARITY)
     sent = merge(
@@ -320,17 +397,13 @@
         home_own, home_other, away_own, away_other, came,
     )
     got = lax.all_to_all(sent, PARITY, 0, 0)
-    grad_feats, mine = merge(
-        end_kernel,
-        (
-            jax.ShapeDtypeStruct((nodes, feats), jnp.bfloat16),
-            jax.ShapeDtypeStruct((EXTRA, feats), jnp.float32),
-        ),
-        got, weight,
-    )
+    mine = merge(weight_kernel, jax.ShapeDtypeStruct((EXTRA, feats), jnp.float32), got)
     theirs = lax.ppermute(mine, "core", SWAP)
-    grad_weight = jnp.where(
-        core == 0, jnp.concatenate([mine, theirs]), jnp.concatenate([theirs, mine])
+    grad_feats = merge(
+        feats_kernel, jax.ShapeDtypeStruct((nodes, feats), jnp.bfloat16), got, weight
+    )
+    grad_weight = merge(
+        join_kernel, jax.ShapeDtypeStruct((feats, feats), jnp.float32), mine, theirs
     )
     return hidden[None], grad_feats.reshape(1, nodes, feats), grad_weight
 

time: 118 us -> 116 us (0.983)
  blocking collectives: 46.1 us -> 74.6 us
  waiting for transfers between devices: 26.5 us -> 10.3 us
  starting transfers between devices: 26.7 us -> 11.2 us
  Pallas kernels: 12.1 us -> 17.6 us
  other arithmetic: 2.55 us -> 0 us
  local copies, waits for them, and re-layouts: 1.72 us -> 0.01 us
    all_to_all x0 -> x1, blocking collectives: none -> 27 us  [spread(): return lax.all_to_all(blocks, axes, 0, 0)]
    all_to_all x1 -> x0, waiting for transfers between devices: 12.8 us -> none  [spread(): lax.all_to_all(jnp.broadcast_to(block[None], (n, *block.shape)), axes, 0, 0)]
    all_to_all x1 -> x0, starting transfers between devices: 11.6 us -> none  [spread(): lax.all_to_all(jnp.broadcast_to(block[None], (n, *block.shape)), axes, 0, 0)]
    all_to_all x1, blocking collectives: 19.3 us -> 22.2 us  [local(): got = lax.all_to_all(sent, PARITY, 0, 0)]
    ppermute x1, waiting for transfers between devices: 4.1 us -> 1.3 us  [local(): beside = lax.ppermute(own, ALONG, NEXT)]
    pallas_call x0 -> x2, Pallas kernels: none -> 2.49 us  [the longest x1 1.59 us: tile_lists(): pl.pallas_call(lists_kernel, out_shape=pltpu.SMEM((2, WIDTH), jnp.int32),...]
    broadcast_in_dim x1 -> x0, local copies, waits for them, and re-layouts: 1.71 us -> none  [spread(): jnp.broadcast_to(block[None], (n, *block.shape))]
    ppermute x1, starting transfers between devices: 1.96 us -> 0.28 us  [local(): home_other = lax.ppermute(home_other, 'core', SWAP)]
  transfers between devices with their start and end apart: 8 -> 7, of which waited for: 8 -> 5; matrix products, arithmetic and copies ran while one was open for 2% -> 0% of each run, Pallas kernels for 5% -> 8%
where the time goes in v5:
time: 116 us; the launch traced here: 115 us
  blocking collectives  74.6 us (64%)
  Pallas kernels  17.6 us (15%)
  starting transfers between devices  11.2 us (10%)
  waiting for transfers between devices  10.3 us (9%)
  between operations  1.38 us (1%)
    all_to_all x1, blocking collectives, spread(): return lax.all_to_all(blocks, axes, 0, 0)  27 us
    all_to_all x1, blocking collectives, local(): got = lax.all_to_all(sent, PARITY, 0, 0)  22.2 us
    all_to_all x1, blocking collectives, local(): got = lax.all_to_all(sent, REP, 0, 0)  14.3 us
    all_to_all x1, blocking collectives, local(): y_parts = lax.all_to_all(y_part.reshape(reps, nodes, feats), REP, 0, 0)  11.1 us
    pallas_call x2, Pallas kernels, forward_pass(): pl.pallas_call(functools.partial(forward_kernel, part), out_shape=(out, p...  7.27 us
    pallas_call x2, Pallas kernels, backward_pass(): pl.pallas_call(functools.partial(backward_kernel, part), out_shape=(jax.S...  5.11 us
    ppermute x1, waiting for transfers between devices, local(): came = lax.ppermute(away, ALONG, NEXT)  4.22 us
    ppermute x1, starting transfers between devices, local(): theirs = lax.ppermute(mine, 'core', SWAP)  4.17 us
  transfers between devices with their start and end apart: 7, of which 5 were waited for; matrix products, arithmetic and copies ran while one was open for 0% of the time, Pallas kernels for 8%

profile of v5, /device:TPU:1, one launch (start us, length us, event | category | flops | bytes accessed | tf_op | source)
XLA Modules:
  0.0 115.2 jit_solution(1754256208573716706)
XLA Ops:
  0.6 0.9 fan.1
  1.5 27.0 %all_to_all.20 = bf16[8,256,128]{2,1,0:T(8,128)(2,1)S(1)} all-to-all(bf16[8,256,128]{2,1,0:T(8,128)(2,1)S(1)} %fan.1), channel_id=1, replica_groups=mesh['x'=4,'ylo'=2,'yhi'=2,'zq'=4,'zp'=2,'core'=2] {'yhi','zq'}, dimensions={0} | all-to-all | bytes 1048576 | tf_op jit(solution)/shard_map/all_to_all | solution.py:325
  28.6 3.3 %collective-permute-start = (bf16[8,256,128]{2,1,0:T(8,128)(2,1)S(1)}, bf16[8,256,128]{2,1,0:T(8,128)(2,1)S(1)}, u32[]{:S(2)}, u32[]{:S(2)}) collective-permute-start(bf16[8,256,128]{2,1,0:T(8,128)(2,1)S(1)} %all_to_all.20), channel_id=1, source_target_pairs={{0,1},{1,0},{2,3},{3,2},{4,5},{5,4},{6,7},{7,6},{8,9},{9,8},{10,11... | collective-permute-start | bytes 1572872 | tf_op jit(solution)/shard_map/ppermute | solution.py:359
  31.9 0.9 collective-permute-start.1
  33.4 1.6 %lists.1 = s32[2,384]{1,0:T(2,128)S(4)} custom-call(s32[1]{0:T(128)} %bitcast.13.count, s32[1,256]{1,0:T(1,128)} %bitcast.23, s32[1,256]{1,0:T(1,128)} %bitcast.24), custom_call_target="tpu_custom_call" | custom-call | flops 1048576 | bytes 4096 | tf_op jit(solution)/shard_map/lists/pallas_call | solution.py:329
  35.0 0.0 collective-permute-done
  35.0 4.6 %forward_tiles_0.1 = (f32[16,128,128]{2,1,0:T(8,128)S(1)}, bf16[256,128,128]{2,1,0:T(8,128)(2,1)S(1)}) custom-call(s32[2,384]{1,0:T(2,128)S(4)} %lists.1, bf16[256,128,128]{2,1,0:T(8,128)(2,1)} %bitcast.20, bf16[16,128,128]{2,1,0:T(8,128)(2,1)S(1)} %bitcast.14, bf16[16,128,128]{2,1,0:T(8,128)(2,1)S(1)} %bitcast.17), custom_call_target="tpu_custom_call" | custom-call | flops 1073741824 | bytes 9437184 | tf_op jit(solution)/shard_map/forward_tiles_0/pallas_call | solution.py:262
  39.7 0.0 copy-start
  39.7 0.0 copy-start.1
  39.7 1.3 %collective-permute-done.1 = bf16[8,256,128]{2,1,0:T(8,128)(2,1)S(1)} collective-permute-done((bf16[8,256,128]{2,1,0:T(8,128)(2,1)S(1)}, bf16[8,256,128]{2,1,0:T(8,128)(2,1)S(1)}, u32[]{:S(2)}, u32[]{:S(2)}) %collective-permute-start.1) | collective-permute-done | bytes 524320 | tf_op jit(solution)/shard_map/ppermute | solution.py:358
  41.0 1.3 %collective-permute-start.2 = (bf16[8,256,128]{2,1,0:T(8,128)(2,1)S(1)}, bf16[8,256,128]{2,1,0:T(8,128)(2,1)S(1)}, u32[]{:S(2)}, u32[]{:S(2)}) collective-permute-start(bf16[8,256,128]{2,1,0:T(8,128)(2,1)S(1)} %collective-permute-done.1), channel_id=1, source_target_pairs={{0,1},{1,0},{2,3},{3,2},{4,5},{5,4},{6,7},{7,6},{8,9},{9,8},{10,11... | collective-permute-start | bytes 1572872 | tf_op jit(solution)/shard_map/ppermute | solution.py:364
  42.2 1.5 %collective-permute-done.2 = bf16[8,256,128]{2,1,0:T(8,128)(2,1)S(1)} collective-permute-done((bf16[8,256,128]{2,1,0:T(8,128)(2,1)S(1)}, bf16[8,256,128]{2,1,0:T(8,128)(2,1)S(1)}, u32[]{:S(2)}, u32[]{:S(2)}) %collective-permute-start.2) | collective-permute-done | bytes 524320 | tf_op jit(solution)/shard_map/ppermute | solution.py:364
  43.8 2.6 %forward_tiles_1.1 = bf16[16,128,128]{2,1,0:T(8,128)(2,1)S(1)} custom-call(s32[2,384]{1,0:T(2,128)S(4)} %lists.1, bf16[256,128,128]{2,1,0:T(8,128)(2,1)S(1)} %get-tuple-element.23.tiles.buffer, f32[16,128,128]{2,1,0:T(8,128)S(1)} %get-tuple-element.17.rest_0_, bf16[16,128,128]{2,1,0:T(8,128)(2,1)S(1)} %bitcast.16, bf16[16,128,128]{2,1,0:T(8,128)(2,1)S(1)} %bitcast.18), custom_call_target="tpu_custom_call" | custom-call | flops 1073741824 | bytes 9437184 | tf_op jit(solution)/shard_map/forward_tiles_1/pallas_call | solution.py:262
  46.4 11.1 %all_to_all.21.y_parts = bf16[8,256,128]{2,1,0:T(8,128)(2,1)S(1)} all-to-all(bf16[8,256,128]{2,1,0:T(8,128)(2,1)S(1)} %bitcast.15), channel_id=1, replica_groups=mesh['x'=4,'ylo'=2,'yhi'=2,'zq'=4,'zp'=2,'core'=2] {'x','ylo'}, dimensions={0} | all-to-all | bytes 1048576 | tf_op jit(solution)/shard_map/all_to_all | solution.py:370
  57.5 0.0 copy-done
  57.5 0.9 middle.1
  58.5 14.3 %all_to_all.22.got = bf16[8,384,128]{2,1,0:T(8,128)(2,1)S(1)} all-to-all(bf16[8,384,128]{2,1,0:T(8,128)(2,1)S(1)} %get-tuple-element.20), channel_id=1, replica_groups=mesh['x'=4,'ylo'=2,'yhi'=2,'zq'=4,'zp'=2,'core'=2] {'x','ylo'}, dimensions={0} | all-to-all | bytes 1572864 | tf_op jit(solution)/shard_map/all_to_all | solution.py:383
  72.8 2.8 %backward_tiles_1.1 = (f32[2112,128]{1,0:T(8,128)S(1)}, bf16[2112,128]{1,0:T(8,128)(2,1)S(1)}) custom-call(s32[2,384]{1,0:T(2,128)S(4)} %lists.1, bf16[256,128,128]{2,1,0:T(8,128)(2,1)S(1)} %get-tuple-element.23.tiles.buffer, bf16[8,384,128]{2,1,0:T(8,128)(2,1)S(1)} %all_to_all.22.got), custom_call_target="tpu_custom_call" | custom-call | flops 1073741824 | bytes 1048576 | tf_op jit(solution)/shard_map/backward_tiles_1/pallas_call | solution.py:285
  75.6 1.2 %collective-permute-start.3 = (bf16[2112,128]{1,0:T(8,128)(2,1)S(1)}, bf16[2112,128]{1,0:T(8,128)(2,1)S(1)}, u32[]{:S(2)}, u32[]{:S(2)}) collective-permute-start(bf16[2112,128]{1,0:T(8,128)(2,1)S(1)} %get-tuple-element.22), channel_id=1, source_target_pairs={{0,1},{1,0},{2,3},{3,2},{4,5},{5,4},{6,7},{7,6},{8,9},{9,8},{10,11... | collective-permute-start | bytes 1622024 | tf_op jit(solution)/shard_map/ppermute | solution.py:385
  76.9 1.6 %collective-permute-done.3.other.away_other = bf16[2112,128]{1,0:T(8,128)(2,1)S(1)} collective-permute-done((bf16[2112,128]{1,0:T(8,128)(2,1)S(1)}, bf16[2112,128]{1,0:T(8,128)(2,1)S(1)}, u32[]{:S(2)}, u32[]{:S(2)}) %collective-permute-start.3) | collective-permute-done | bytes 540704 | tf_op jit(solution)/shard_map/ppermute | solution.py:385
  78.4 0.1 away_kernel.1
  78.5 0.1 collective-permute-start.5
  78.6 2.3 %backward_tiles_0.1 = (f32[2048,128]{1,0:T(8,128)S(1)}, bf16[2048,128]{1,0:T(8,128)(2,1)S(1)}) custom-call(s32[2,384]{1,0:T(2,128)S(4)} %lists.1, bf16[256,128,128]{2,1,0:T(8,128)(2,1)S(1)} %get-tuple-element.23.tiles.buffer, bf16[8,384,128]{2,1,0:T(8,128)(2,1)S(1)} %all_to_all.22.got), custom_call_target="tpu_custom_call" | custom-call | flops 1073741824 | bytes 1048576 | tf_op jit(solution)/shard_map/backward_tiles_0/pallas_call | solution.py:285
  80.9 0.3 collective-permute-start.4
  81.2 1.7 %collective-permute-done.4.other = bf16[2048,128]{1,0:T(8,128)(2,1)S(1)} collective-permute-done((bf16[2048,128]{1,0:T(8,128)(2,1)S(1)}, bf16[2048,128]{1,0:T(8,128)(2,1)S(1)}, u32[]{:S(2)}, u32[]{:S(2)}) %collective-permute-start.4) | collective-permute-done | bytes 524320 | tf_op jit(solution)/shard_map/ppermute | solution.py:392
  82.9 4.2 %collective-permute-done.5.came = bf16[2112,128]{1,0:T(8,128)(2,1)S(1)} collective-permute-done((bf16[2112,128]{1,0:T(8,128)(2,1)S(1)}, bf16[2112,128]{1,0:T(8,128)(2,1)S(1)}, u32[]{:S(2)}, u32[]{:S(2)}) %collective-permute-start.5) | collective-permute-done | bytes 540704 | tf_op jit(solution)/shard_map/ppermute | solution.py:390
  87.1 0.2 home_kernel.1
  87.3 22.2 %all_to_all.23.got = bf16[8,320,128]{2,1,0:T(8,128)(2,1)S(1)} all-to-all(bf16[8,320,128]{2,1,0:T(8,128)(2,1)S(1)} %home_kernel.1), channel_id=1, replica_groups=mesh['x'=4,'ylo'=2,'yhi'=2,'zq'=4,'zp'=2,'core'=2] {'yhi','zq'}, dimensions={0} | all-to-all | bytes 1310720 | tf_op jit(solution)/shard_map/all_to_all | solution.py:399
  109.5 4.2 %collective-permute-start.6 = (f32[64,128]{1,0:T(8,128)S(1)}, f32[64,128]{1,0:T(8,128)S(1)}, u32[]{:S(2)}, u32[]{:S(2)}) collective-permute-start(f32[64,128]{1,0:T(8,128)S(1)} %weight_kernel.1.mine), channel_id=1, source_target_pairs={{0,1},{1,0},{2,3},{3,2},{4,5},{5,4},{6,7},{7,6},{8,9},{9,8},{10,11... | collective-permute-start | bytes 98312 | tf_op jit(solution)/shard_map/ppermute | solution.py:401
  113.6 0.9 feats_kernel.1
  114.5 0.0 collective-permute-done.6.theirs
  114.5 0.6 join_kernel.1
  (2 shorter events, 0.0 us)
Async XLA Ops:
  28.6 6.4 %collective-permute-start = (bf16[8,256,128]{2,1,0:T(8,128)(2,1)S(1)}, bf16[8,256,128]{2,1,0:T(8,128)(2,1)S(1)}, u32[]{:S(2)}, u32[]{:S(2)}) collective-permute-start(bf16[8,256,128]{2,1,0:T(8,128)(2,1)S(1)} %all_to_all.20), channel_id=1, source_target_pairs={{0,1},{1,0},{2,3},{3,2},{4,5},{5,4},{6,7},{7,6},{8,9},{9,8},{10,11... | collective-permute-start | bytes 1572872 | tf_op jit(solution)/shard_map/ppermute | solution.py:359
  31.9 9.1 %collective-permute-start.1 = (bf16[8,256,128]{2,1,0:T(8,128)(2,1)S(1)}, bf16[8,256,128]{2,1,0:T(8,128)(2,1)S(1)}, u32[]{:S(2)}, u32[]{:S(2)}) collective-permute-start(bf16[8,256,128]{2,1,0:T(8,128)(2,1)S(1)} %all_to_all.20), channel_id=1, source_target_pairs={{0,2},{2,4},{4,6},{6,8},{8,10},{10,12},{12,14},{14,0},{1,15},{3,1}... | collective-permute-start | bytes 1572872 | tf_op jit(solution)/shard_map/ppermute | solution.py:358
  39.7 17.9 %copy-start = (bf16[128,128]{1,0:T(8,128)(2,1)S(1)}, bf16[128,128]{1,0:T(8,128)(2,1)}, u32[]{:S(2)}) copy-start(bf16[128,128]{1,0:T(8,128)(2,1)} %weight.3) | copy-start | bytes 98308
  39.7 17.9 %copy-start.1 = (bf16[1,256,128]{2,1,0:T(8,128)(2,1)S(1)}, bf16[1,256,128]{2,1,0:T(8,128)(2,1)}, u32[]{:S(2)}) copy-start(bf16[1,256,128]{2,1,0:T(8,128)(2,1)} %param.9) | copy-start | bytes 196612
  41.0 2.8 %collective-permute-start.2 = (bf16[8,256,128]{2,1,0:T(8,128)(2,1)S(1)}, bf16[8,256,128]{2,1,0:T(8,128)(2,1)S(1)}, u32[]{:S(2)}, u32[]{:S(2)}) collective-permute-start(bf16[8,256,128]{2,1,0:T(8,128)(2,1)S(1)} %collective-permute-done.1), channel_id=1, source_target_pairs={{0,1},{1,0},{2,3},{3,2},{4,5},{5,4},{6,7},{7,6},{8,9},{9,8},{10,11... | collective-permute-start | bytes 1572872 | tf_op jit(solution)/shard_map/ppermute | solution.py:364
  75.6 2.8 %collective-permute-start.3 = (bf16[2112,128]{1,0:T(8,128)(2,1)S(1)}, bf16[2112,128]{1,0:T(8,128)(2,1)S(1)}, u32[]{:S(2)}, u32[]{:S(2)}) collective-permute-start(bf16[2112,128]{1,0:T(8,128)(2,1)S(1)} %get-tuple-element.22), channel_id=1, source_target_pairs={{0,1},{1,0},{2,3},{3,2},{4,5},{5,4},{6,7},{7,6},{8,9},{9,8},{10,11... | collective-permute-start | bytes 1622024 | tf_op jit(solution)/shard_map/ppermute | solution.py:385
  78.5 8.6 %collective-permute-start.5 = (bf16[2112,128]{1,0:T(8,128)(2,1)S(1)}, bf16[2112,128]{1,0:T(8,128)(2,1)S(1)}, u32[]{:S(2)}, u32[]{:S(2)}) collective-permute-start(bf16[2112,128]{1,0:T(8,128)(2,1)S(1)} %away_kernel.1), channel_id=1, source_target_pairs={{0,2},{2,4},{4,6},{6,8},{8,10},{10,12},{12,14},{14,0},{1,15},{3,1}... | collective-permute-start | bytes 1622024 | tf_op jit(solution)/shard_map/ppermute | solution.py:390
  80.9 2.0 %collective-permute-start.4 = (bf16[2048,128]{1,0:T(8,128)(2,1)S(1)}, bf16[2048,128]{1,0:T(8,128)(2,1)S(1)}, u32[]{:S(2)}, u32[]{:S(2)}) collective-permute-start(bf16[2048,128]{1,0:T(8,128)(2,1)S(1)} %get-tuple-element.25), channel_id=1, source_target_pairs={{0,1},{1,0},{2,3},{3,2},{4,5},{5,4},{6,7},{7,6},{8,9},{9,8},{10,11... | collective-permute-start | bytes 1572872 | tf_op jit(solution)/shard_map/ppermute | solution.py:392
  109.5 5.1 %collective-permute-start.6 = (f32[64,128]{1,0:T(8,128)S(1)}, f32[64,128]{1,0:T(8,128)S(1)}, u32[]{:S(2)}, u32[]{:S(2)}) collective-permute-start(f32[64,128]{1,0:T(8,128)S(1)} %weight_kernel.1.mine), channel_id=1, source_target_pairs={{0,1},{1,0},{2,3},{3,2},{4,5},{5,4},{6,7},{7,6},{8,9},{9,8},{10,11... | collective-permute-start | bytes 98312 | tf_op jit(solution)/shard_map/ppermute | solution.py:401

commit v6 on v5

--- a/solution.py
+++ b/solution.py
@@ -10,11 +10,11 @@
 CHUNK = 32
 BLOCK = 128
 ROWS = 16
-PLACES = 32
-PART = PLACES // 2
+PART = 16
+CAP = 256
+OWN, OWN_OTHER, BESIDE, BESIDE_OTHER = PARTS = range(4)
 ROW_AT, PLACE_AT = 8, 13
-SPARE = (ROWS << ROW_AT) | (PLACES << PLACE_AT)
-CAP = 256
+SPARE = (ROWS << ROW_AT) | (PART << PLACE_AT)
 COUNT_AT = CAP
 WIDTH = CAP + 128
 SPAN = PART * BLOCK
@@ -36,7 +36,7 @@
     return pltpu.make_async_copy(tiles.at[span], buffer.at[span], sems.at[chunk])
 
 
-def tile_groups(part, lists, group, ready):
+def tile_groups(part, lists, group, ready=lambda done, need: need, done=0):
     count = lists[part, COUNT_AT]
 
     def step(k, done):
@@ -46,48 +46,15 @@
         group([lists[part, base + u] for u in range(CHUNK)])
         return done
 
-    return lax.fori_loop(0, (count + CHUNK - 1) // CHUNK, step, 0)
-
-
-def forward_kernel(part, lists, tiles, *rest):
-    if part == 0:
-        x0, x1, out, buffer, xs, acc, xsems, sems = rest
-    else:
-        before, x0, x1, out, xs, acc, xsems = rest
-        buffer = tiles
-    chunks = (lists[0, COUNT_AT] + lists[1, COUNT_AT] + CHUNK - 1) // CHUNK
-    moves = [
-        pltpu.make_async_copy(source, xs.at[pl.ds(k * PART, PART)], xsems.at[k])
-        for k, source in enumerate((x0, x1))
-    ]
-    for move in moves:
-        move.start()
-    if part == 0:
-
-        @pl.loop(0, chunks)
-        def _(c):
-            tile_copy(tiles, buffer, sems, c).start()
-
-        acc[...] = jnp.zeros_like(acc)
-    else:
-        acc[:ROWS] = before[...]
-    for move in moves:
-        move.wait()
-
-    def ready(done, need):
-        if part == 0:
-
-            @pl.loop(done, need)
-            def _(c):
-                tile_copy(tiles, buffer, sems, c).wait()
-
-        return need
-
+    return lax.fori_loop(0, (count + CHUNK - 1) // CHUNK, step, done)
+
+
+def forward_group(buffer, block_ref, acc):
     def group(codes):
         products = [
             jnp.dot(
                 buffer[code & 255],
-                xs[(code >> PLACE_AT) & (PLACES - 1)],
+                block_ref[(code >> PLACE_AT) & (PART - 1)],
                 preferred_element_type=jnp.float32,
             )
             for code in codes
@@ -95,18 +62,10 @@
         for code, product in zip(codes, products):
             acc[(code >> ROW_AT) & 31] += product
 
-    done = tile_groups(part, lists, group, ready)
-    ready(done, chunks)
-    out[...] = acc[:ROWS].astype(out.dtype)
-
-
-def backward_kernel(part, lists, buffer, got, own, other, acc, weight_sum=None):
-    acc[...] = jnp.zeros_like(acc)
-    nodes = got.shape[1] - BLOCK
-    if part == 1:
-        reps = got.shape[0]
-        weight_sum[...] = sum(got[k, nodes:].astype(jnp.float32) for k in range(reps))
-
+    return group
+
+
+def backward_group(buffer, got, acc):
     def group(codes):
         products = []
         for code in codes:
@@ -118,16 +77,53 @@
         for code, product in zip(codes, products):
             acc[code >> PLACE_AT] += product
 
-    tile_groups(part, lists, group, lambda done, need: need)
-    feats = own.shape[1]
-    own[:SPAN] = acc[:PART].reshape(SPAN, feats)
-    other[:SPAN] = acc[PART:PLACES].reshape(SPAN, feats).astype(jnp.bfloat16)
-    if part == 1:
-        core = lax.axis_index("core")
-        mine = pl.multiple_of(core * EXTRA, EXTRA)
-        theirs = pl.multiple_of((1 - core) * EXTRA, EXTRA)
-        own[SPAN:] = weight_sum[pl.ds(mine, EXTRA), :]
-        other[SPAN:] = weight_sum[pl.ds(theirs, EXTRA), :].astype(jnp.bfloat16)
+    return group
+
+
+def first_forward_kernel(lists, tiles, x0, x1, out, buffer, acc, sems):
+    chunks = (sum(lists[part, COUNT_AT] for part in PARTS) + CHUNK - 1) // CHUNK
+
+    @pl.loop(0, chunks)
+    def _(c):
+        tile_copy(tiles, buffer, sems, c).start()
+
+    acc[...] = jnp.zeros_like(acc)
+
+    def ready(done, need):
+        @pl.loop(done, need)
+        def _(c):
+            tile_copy(tiles, buffer, sems, c).wait()
+
+        return jnp.maximum(done, need)
+
+    done = tile_groups(OWN, lists, forward_group(buffer, x0, acc), ready, 0)
+    done = tile_groups(OWN_OTHER, lists, forward_group(buffer, x1, acc), ready, done)
+    ready(done, chunks)
+    out[...] = acc[:ROWS]
+
+
+def forward_kernel(part, lists, buffer, before, x, out, acc):
+    acc[:ROWS] = before[...]
+    tile_groups(part, lists, forward_group(buffer, x, acc))
+    out[...] = acc[:ROWS].astype(out.dtype)
+
+
+def away_part_kernel(part, lists, buffer, got, out, acc, weight_sum):
+    acc[...] = jnp.zeros_like(acc)
+    nodes = got.shape[1] - BLOCK
+    weight_sum[...] = sum(got[k, nodes:].astype(jnp.float32) for k in range(got.shape[0]))
+    tile_groups(part, lists, backward_group(buffer, got, acc))
+    out[:SPAN] = acc[:PART].reshape(SPAN, out.shape[1]).astype(out.dtype)
+    core = lax.axis_index("core")
+    at = pl.multiple_of((core if part == BESIDE else 1 - core) * EXTRA, EXTRA)
+    out[SPAN:] = weight_sum[pl.ds(at, EXTRA), :].astype(out.dtype)
+
+
+def home_part_kernel(lists, buffer, got, own, other, acc, acc_other):
+    for part, out, sums in ((OWN_OTHER, other, acc_other), (OWN, own, acc)):
+        sums[...] = jnp.zeros_like(sums)
+        tile_groups(part, lists, backward_group(buffer, got, sums))
+        out[...] = sums[:PART].reshape(out.shape).astype(out.dtype)
 
 
 def middle_kernel(y_parts, weight, cotangent, hidden, sent):
@@ -217,10 +213,10 @@
     block = cols[...]
     z = (block >> 2) & 7
     core = ((block >> 1) & 1) ^ lax.axis_index("core")
-    part = (z & 1) ^ lax.axis_index("zp")
-    place = core * PART + ((block >> 5) * 4 + (z >> 1)) * 2 + (block & 1)
+    part = ((z & 1) ^ lax.axis_index("zp")) * 2 + core
+    place = ((block >> 5) * 4 + (z >> 1)) * 2 + (block & 1)
     code = slots | (rows[...] << ROW_AT) | (place << PLACE_AT)
-    part = jnp.where(slots < count[0], part, 2).astype(jnp.float32)
+    part = jnp.where(slots < count[0], part, len(PARTS)).astype(jnp.float32)
     code = (code - SPARE).astype(jnp.float32)
 
     square = (CAP, CAP)
@@ -231,7 +227,7 @@
     earlier = (lane < lax.broadcasted_iota(jnp.int32, square, 0)) & (across == down)
     rank = jnp.sum(jnp.where(earlier, 1.0, 0.0), axis=1, keepdims=True)
     at_rank = rank == lane.astype(jnp.float32)
-    for p in range(2):
+    for p in PARTS:
         listed = jnp.where(at_rank & (down == p), code, 0.0)
         entries = jnp.sum(listed, axis=0, keepdims=True).astype(jnp.int32) + SPARE
         size = jnp.sum(jnp.where(part == p, 1.0, 0.0), axis=1, keepdims=True)
@@ -247,54 +243,27 @@
 ANY = pl.BlockSpec(memory_space=pl.ANY)
 
 
-def forward_pass(part, lists, tiles, parts, before=()):
-    cap = tiles.shape[0]
-    out = jax.ShapeDtypeStruct(
-        (ROWS, BLOCK, BLOCK), jnp.float32 if part == 0 else jnp.bfloat16
-    )
-    scratch = [
-        pltpu.VMEM((PLACES, BLOCK, BLOCK), jnp.bfloat16),
-        pltpu.VMEM((ROWS + 1, BLOCK, BLOCK), jnp.float32),
-        pltpu.SemaphoreType.DMA((2,)),
-    ]
-    if part == 0:
-        scratch.append(pltpu.SemaphoreType.DMA((cap // CHUNK,)))
+def tile_kernel(kernel, out_shape, lists, tiles, arrays, scratch):
+    first = kernel is first_forward_kernel
+    out_specs = (VMEM,) * len(out_shape) if isinstance(out_shape, tuple) else VMEM
     return pl.pallas_call(
-        functools.partial(forward_kernel, part),
-        out_shape=(out, pltpu.VMEM((cap, BLOCK, BLOCK), jnp.bfloat16)) if part == 0 else out,
-        in_specs=[SMEM, ANY if part == 0 else VMEM] + [VMEM] * len(before) + [ANY, ANY],
-        out_specs=(VMEM, VMEM) if part == 0 else VMEM,
+        kernel,
+        out_shape=out_shape,
+        in_specs=[SMEM, ANY if first else VMEM] + [VMEM] * len(arrays),
+        out_specs=out_specs,
         scratch_shapes=scratch,
-        compiler_params=pltpu.CompilerParams(vmem_limit_bytes=20 << 20),
-        cost_estimate=pl.CostEstimate(flops=1 << 30, bytes_accessed=9 << 20, transcendentals=0),
-        name=f"forward_tiles_{part}",
+        compiler_params=pltpu.CompilerParams(vmem_limit_bytes=16 << 20),
+        cost_estimate=pl.CostEstimate(flops=1 << 29, bytes_accessed=4 << 20, transcendentals=0),
+        name=getattr(kernel, "func", kernel).__name__,
     )(
         pltpu.with_memory_space_constraint(lists, pltpu.SMEM),
-        pltpu.with_memory_space_constraint(tiles, pltpu.HBM if part == 0 else pltpu.VMEM),
-        *before,
-        *parts,
-    )
-
-
-def backward_pass(part, lists, held, got):
-    feats = got.shape[2]
-    size = SPAN + EXTRA * part
-    scratch = [pltpu.VMEM((PLACES + 1, BLOCK, BLOCK), jnp.float32)]
-    if part == 1:
-        scratch.append(pltpu.VMEM((BLOCK, BLOCK), jnp.float32))
-    return pl.pallas_call(
-        functools.partial(backward_kernel, part),
-        out_shape=(
-            jax.ShapeDtypeStruct((size, feats), jnp.float32),
-            jax.ShapeDtypeStruct((size, feats), jnp.bfloat16),
-        ),
-        in_specs=[SMEM, VMEM, VMEM],
-        out_specs=(VMEM, VMEM),
-        scratch_shapes=scratch,
-        compiler_params=pltpu.CompilerParams(vmem_limit_bytes=20 << 20),
-        cost_estimate=pl.CostEstimate(flops=1 << 30, bytes_accessed=1 << 20, transcendentals=0),
-        name=f"backward_tiles_{part}",
-    )(pltpu.with_memory_space_constraint(lists, pltpu.SMEM), pltpu.with_memory_space_constraint(held, pltpu.VMEM), got)
+        pltpu.with_memory_space_constraint(tiles, pltpu.HBM if first else pltpu.VMEM),
+        *arrays,
+    )
+
+
+def sums(rows):
+    return pltpu.VMEM((rows + 1, BLOCK, BLOCK), jnp.float32)
 
 
 def merge(kernel, out_shape, *arrays):
@@ -328,13 +297,13 @@
 def tile_lists(count, rows, cols):
     return pl.pallas_call(
         lists_kernel,
-        out_shape=pltpu.SMEM((2, WIDTH), jnp.int32),
+        out_shape=pltpu.SMEM((len(PARTS), WIDTH), jnp.int32),
         in_specs=[SMEM, ANY, ANY],
         out_specs=SMEM,
         scratch_shapes=[
             pltpu.VMEM((1, CAP), jnp.int32),
             pltpu.VMEM((1, CAP), jnp.int32),
-            pltpu.VMEM((2, WIDTH), jnp.int32),
+            pltpu.VMEM((len(PARTS), WIDTH), jnp.int32),
             pltpu.SemaphoreType.DMA((3,)),
         ],
         compiler_params=pltpu.CompilerParams(vmem_limit_bytes=16 << 20),
@@ -351,19 +320,30 @@
     x = features[0]
     nodes, feats = x.shape
     tiles = tiles[0, 0]
-    lists = tile_lists(counts[0], row_ids[0], col_ids[0])
     blocks = (PART, BLOCK, feats)
-
     own = spread(x, PARITY)
     beside = lax.ppermute(own, ALONG, NEXT)
+    lists = tile_lists(counts[0], row_ids[0], col_ids[0])
     own_other = lax.ppermute(own, "core", SWAP)
-    y_part, held = forward_pass(
-        0, lists, tiles, (own.reshape(blocks), own_other.reshape(blocks))
+    y_shape = jax.ShapeDtypeStruct((ROWS, BLOCK, BLOCK), jnp.float32)
+    y_part, held = tile_kernel(
+        first_forward_kernel,
+        (y_shape, pltpu.VMEM(tiles.shape, jnp.bfloat16)),
+        lists,
+        tiles,
+        (own.reshape(blocks), own_other.reshape(blocks)),
+        [sums(ROWS), pltpu.SemaphoreType.DMA((CAP // CHUNK,))],
     )
     beside, y_part = lax.optimization_barrier((beside, y_part))
     beside_other = lax.ppermute(beside, "core", SWAP)
-    y_part = forward_pass(
-        1, lists, held, (beside.reshape(blocks), beside_other.reshape(blocks)), (y_part,)
+    y_part = tile_kernel(
+        functools.partial(forward_kernel, BESIDE),
+        y_shape, lists, held, (y_part, beside.reshape(blocks)), [sums(ROWS)],
+    )
+    y_part = tile_kernel(
+        functools.partial(forward_kernel, BESIDE_OTHER),
+        jax.ShapeDtypeStruct((ROWS, BLOCK, BLOCK), jnp.bfloat16),
+        lists, held, (y_part, beside_other.reshape(blocks)), [sums(ROWS)],
     )
 
     reps = lax.axis_size(REP)
@@ -381,14 +361,28 @@
         name="middle",
     )(y_parts, weight, cotangent[0])
     got = lax.all_to_all(sent, REP, 0, 0)
-    away_own, away_other = backward_pass(1, lists, held, got)
-    away_other = lax.ppermute(away_other, "core", SWAP)
+    def away_part(part, dtype):
+        return tile_kernel(
+            functools.partial(away_part_kernel, part),
+            jax.ShapeDtypeStruct((SPAN + EXTRA, feats), dtype),
+            lists, held, (got,), [sums(PART), pltpu.VMEM((BLOCK, feats), jnp.float32)],
+        )
+
+    away_other = lax.ppermute(away_part(BESIDE_OTHER, jnp.bfloat16), "core", SWAP)
+    away_own = away_part(BESIDE, jnp.float32)
     away = merge(
         away_kernel, jax.ShapeDtypeStruct(away_own.shape, jnp.bfloat16), away_own, away_other
     )
     held, away = lax.optimization_barrier((held, away))
     came = lax.ppermute(away, ALONG, NEXT)
-    home_own, home_other = backward_pass(0, lists, held, got)
+    home_own, home_other = tile_kernel(
+        home_part_kernel,
+        (
+            jax.ShapeDtypeStruct((SPAN, feats), jnp.float32),
+            jax.ShapeDtypeStruct((SPAN, feats), jnp.bfloat16),
+        ),
+        lists, held, (got,), [sums(PART), sums(PART)],
+    )
     home_other = lax.ppermute(home_other, "core", SWAP)
     peers = lax.axis_size(PARITY)
     sent = merge(

time: 116 us -> 114 us (0.983); the launches traced: 115 us -> 114 us
  blocking collectives: 74.6 us -> 79.2 us
  Pallas kernels: 17.6 us -> 13.5 us
    pallas_call x5 -> x7, Pallas kernels: 14 us -> 9.84 us  [the longest x6 8.15 us: tile_kernel(): pl.pallas_call(kernel, out_shape=out_shape, in_specs=[SMEM, ANY if first...]
    all_to_all x1, blocking collectives: 11.1 us -> 14.5 us  [local(): y_parts = lax.all_to_all(y_part.reshape(reps, nodes, feats), REP, 0, 0)]
    ppermute x1, starting transfers between devices: 4.17 us -> 2.1 us  [local(): theirs = lax.ppermute(mine, 'core', SWAP)]
    ppermute x1, waiting for transfers between devices: 1.3 us -> 2.53 us  [local(): beside = lax.ppermute(own, ALONG, NEXT)]
    all_to_all x1, blocking collectives: 22.2 us -> 23.4 us  [local(): got = lax.all_to_all(sent, PARITY, 0, 0)]
    ppermute x1, waiting for transfers between devices: 1.56 us -> 0.36 us  [local(): lax.ppermute(away_part(BESIDE_OTHER, jnp.bfloat16), 'core', SWAP)]
where the time goes in v6:
time: 114 us
  blocking collectives  79.2 us (69%)
  Pallas kernels  13.5 us (12%)
  starting transfers between devices  10.2 us (9%)
  waiting for transfers between devices  10 us (9%)
  between operations  1.4 us (1%)
    all_to_all x1, blocking collectives, spread(): return lax.all_to_all(blocks, axes, 0, 0)  27 us
    all_to_all x1, blocking collectives, local(): got = lax.all_to_all(sent, PARITY, 0, 0)  23.4 us
    all_to_all x1, blocking collectives, local(): y_parts = lax.all_to_all(y_part.reshape(reps, nodes, feats), REP, 0, 0)  14.5 us
    all_to_all x1, blocking collectives, local(): got = lax.all_to_all(sent, REP, 0, 0)  14.3 us
    pallas_call x6, Pallas kernels, tile_kernel(): pl.pallas_call(kernel, out_shape=out_shape, in_specs=[SMEM, ANY if first...  8.15 us
    ppermute x1, waiting for transfers between devices, local(): came = lax.ppermute(away, ALONG, NEXT)  5.21 us
    ppermute x1, starting transfers between devices, local(): own_other = lax.ppermute(own, 'core', SWAP)  3.26 us
    ppermute x1, waiting for transfers between devices, local(): beside = lax.ppermute(own, ALONG, NEXT)  2.53 us
  transfers between devices with their start and end apart: 7, of which 5 were waited for; matrix products, arithmetic and copies ran while one was open for 0% of the time, Pallas kernels for 8%

profile of v6, /device:TPU:1, one launch (start us, length us, event | category | flops | bytes accessed | tf_op | source)
XLA Modules:
  0.0 114.3 jit_solution(9221609816092518096)
XLA Ops:
  0.6 0.9 fan.1
  1.5 27.0 %all_to_all.20 = bf16[8,256,128]{2,1,0:T(8,128)(2,1)S(1)} all-to-all(bf16[8,256,128]{2,1,0:T(8,128)(2,1)S(1)} %fan.1), channel_id=1, replica_groups=mesh['x'=4,'ylo'=2,'yhi'=2,'zq'=4,'zp'=2,'core'=2] {'yhi','zq'}, dimensions={0} | all-to-all | bytes 1048576 | tf_op jit(solution)/shard_map/all_to_all | solution.py:294
  28.6 3.3 %collective-permute-start = (bf16[8,256,128]{2,1,0:T(8,128)(2,1)S(1)}, bf16[8,256,128]{2,1,0:T(8,128)(2,1)S(1)}, u32[]{:S(2)}, u32[]{:S(2)}) collective-permute-start(bf16[8,256,128]{2,1,0:T(8,128)(2,1)S(1)} %all_to_all.20), channel_id=1, source_target_pairs={{0,1},{1,0},{2,3},{3,2},{4,5},{5,4},{6,7},{7,6},{8,9},{9,8},{10,11... | collective-permute-start | bytes 1572872 | tf_op jit(solution)/shard_map/ppermute | solution.py:327
  31.9 0.9 collective-permute-start.1
  33.4 1.7 %lists.1 = s32[4,384]{1,0:T(4,128)S(4)} custom-call(s32[1]{0:T(128)} %bitcast.13.count, s32[1,256]{1,0:T(1,128)} %bitcast.23, s32[1,256]{1,0:T(1,128)} %bitcast.24), custom_call_target="tpu_custom_call" | custom-call | flops 1048576 | bytes 4096 | tf_op jit(solution)/shard_map/lists/pallas_call | solution.py:298
  35.1 0.0 collective-permute-done
  35.1 3.3 %first_forward_kernel.1 = (f32[16,128,128]{2,1,0:T(8,128)S(1)}, bf16[256,128,128]{2,1,0:T(8,128)(2,1)S(1)}) custom-call(s32[4,384]{1,0:T(4,128)S(4)} %lists.1, bf16[256,128,128]{2,1,0:T(8,128)(2,1)} %bitcast.20, bf16[16,128,128]{2,1,0:T(8,128)(2,1)S(1)} %bitcast.14, bf16[16,128,128]{2,1,0:T(8,128)(2,1)S(1)} %bitcast.17), custom_call_target="tpu_custom_call" | custom-call | flops 536870912 | bytes 4194304 | tf_op jit(solution)/shard_map/first_forward_kernel/pallas_call | solution.py:249
  38.5 2.5 %collective-permute-done.1 = bf16[8,256,128]{2,1,0:T(8,128)(2,1)S(1)} collective-permute-done((bf16[8,256,128]{2,1,0:T(8,128)(2,1)S(1)}, bf16[8,256,128]{2,1,0:T(8,128)(2,1)S(1)}, u32[]{:S(2)}, u32[]{:S(2)}) %collective-permute-start.1) | collective-permute-done | bytes 524320 | tf_op jit(solution)/shard_map/ppermute | solution.py:325
  41.0 1.3 %collective-permute-start.2 = (bf16[8,256,128]{2,1,0:T(8,128)(2,1)S(1)}, bf16[8,256,128]{2,1,0:T(8,128)(2,1)S(1)}, u32[]{:S(2)}, u32[]{:S(2)}) collective-permute-start(bf16[8,256,128]{2,1,0:T(8,128)(2,1)S(1)} %collective-permute-done.1), channel_id=1, source_target_pairs={{0,1},{1,0},{2,3},{3,2},{4,5},{5,4},{6,7},{7,6},{8,9},{9,8},{10,11... | collective-permute-start | bytes 1572872 | tf_op jit(solution)/shard_map/ppermute | solution.py:338
  42.2 1.1 forward_kernel.2.before
  43.4 0.0 copy-start
  43.4 0.0 copy-start.1
  43.4 0.4 collective-permute-done.2
  43.8 0.6 forward_kernel.3
  44.4 14.5 %all_to_all.21.y_parts = bf16[8,256,128]{2,1,0:T(8,128)(2,1)S(1)} all-to-all(bf16[8,256,128]{2,1,0:T(8,128)(2,1)S(1)} %bitcast.15), channel_id=1, replica_groups=mesh['x'=4,'ylo'=2,'yhi'=2,'zq'=4,'zp'=2,'core'=2] {'x','ylo'}, dimensions={0} | all-to-all | bytes 1048576 | tf_op jit(solution)/shard_map/all_to_all | solution.py:350
  58.9 0.9 middle.1
  59.8 14.3 %all_to_all.22.got = bf16[8,384,128]{2,1,0:T(8,128)(2,1)S(1)} all-to-all(bf16[8,384,128]{2,1,0:T(8,128)(2,1)S(1)} %get-tuple-element.18), channel_id=1, replica_groups=mesh['x'=4,'ylo'=2,'yhi'=2,'zq'=4,'zp'=2,'core'=2] {'x','ylo'}, dimensions={0} | all-to-all | bytes 1572864 | tf_op jit(solution)/shard_map/all_to_all | solution.py:363
  74.1 0.7 away_part_kernel.3
  74.7 2.2 %collective-permute-start.3 = (bf16[2112,128]{1,0:T(8,128)(2,1)S(1)}, bf16[2112,128]{1,0:T(8,128)(2,1)S(1)}, u32[]{:S(2)}, u32[]{:S(2)}) collective-permute-start(bf16[2112,128]{1,0:T(8,128)(2,1)S(1)} %away_part_kernel.3), channel_id=1, source_target_pairs={{0,1},{1,0},{2,3},{3,2},{4,5},{5,4},{6,7},{7,6},{8,9},{9,8},{10,11... | collective-permute-start | bytes 1622024 | tf_op jit(solution)/shard_map/ppermute | solution.py:371
  76.9 1.2 %away_part_kernel.2.own.away_own = f32[2112,128]{1,0:T(8,128)S(1)} custom-call(s32[4,384]{1,0:T(4,128)S(4)} %lists.1, bf16[256,128,128]{2,1,0:T(8,128)(2,1)S(1)} %get-tuple-element.19.buffer, bf16[8,384,128]{2,1,0:T(8,128)(2,1)S(1)} %all_to_all.22.got), custom_call_target="tpu_custom_call" | custom-call | flops 536870912 | bytes 4194304 | tf_op jit(solution)/shard_map/away_part_kernel/pallas_call | solution.py:249
  78.1 0.4 collective-permute-done.3.other.away_other
  78.5 0.1 away_kernel.1
  78.6 0.1 collective-permute-start.5
  78.7 1.3 %home_part_kernel.1 = (f32[2048,128]{1,0:T(8,128)S(1)}, bf16[2048,128]{1,0:T(8,128)(2,1)S(1)}) custom-call(s32[4,384]{1,0:T(4,128)S(4)} %lists.1, bf16[256,128,128]{2,1,0:T(8,128)(2,1)S(1)} %get-tuple-element.19.buffer, bf16[8,384,128]{2,1,0:T(8,128)(2,1)S(1)} %all_to_all.22.got), custom_call_target="tpu_custom_call" | custom-call | flops 536870912 | bytes 4194304 | tf_op jit(solution)/shard_map/home_part_kernel/pallas_call | solution.py:249
  79.9 0.5 collective-permute-start.4
  80.4 1.5 %collective-permute-done.4.other = bf16[2048,128]{1,0:T(8,128)(2,1)S(1)} collective-permute-done((bf16[2048,128]{1,0:T(8,128)(2,1)S(1)}, bf16[2048,128]{1,0:T(8,128)(2,1)S(1)}, u32[]{:S(2)}, u32[]{:S(2)}) %collective-permute-start.4) | collective-permute-done | bytes 524320 | tf_op jit(solution)/shard_map/ppermute | solution.py:386
  81.9 5.2 %collective-permute-done.5.came = bf16[2112,128]{1,0:T(8,128)(2,1)S(1)} collective-permute-done((bf16[2112,128]{1,0:T(8,128)(2,1)S(1)}, bf16[2112,128]{1,0:T(8,128)(2,1)S(1)}, u32[]{:S(2)}, u32[]{:S(2)}) %collective-permute-start.5) | collective-permute-done | bytes 540704 | tf_op jit(solution)/shard_map/ppermute | solution.py:377
  87.1 0.2 home_kernel.1
  87.3 23.4 %all_to_all.23.got = bf16[8,320,128]{2,1,0:T(8,128)(2,1)S(1)} all-to-all(bf16[8,320,128]{2,1,0:T(8,128)(2,1)S(1)} %home_kernel.1), channel_id=1, replica_groups=mesh['x'=4,'ylo'=2,'yhi'=2,'zq'=4,'zp'=2,'core'=2] {'yhi','zq'}, dimensions={0} | all-to-all | bytes 1310720 | tf_op jit(solution)/shard_map/all_to_all | solution.py:393
  110.7 2.1 %collective-permute-start.6 = (f32[64,128]{1,0:T(8,128)S(1)}, f32[64,128]{1,0:T(8,128)S(1)}, u32[]{:S(2)}, u32[]{:S(2)}) collective-permute-start(f32[64,128]{1,0:T(8,128)S(1)} %weight_kernel.1.mine), channel_id=1, source_target_pairs={{0,1},{1,0},{2,3},{3,2},{4,5},{5,4},{6,7},{7,6},{8,9},{9,8},{10,11... | collective-permute-start | bytes 98312 | tf_op jit(solution)/shard_map/ppermute | solution.py:395
  112.8 0.9 feats_kernel.1
  113.7 0.6 join_kernel.1
  (4 shorter events, 0.0 us)
Async XLA Ops:
  28.6 6.5 %collective-permute-start = (bf16[8,256,128]{2,1,0:T(8,128)(2,1)S(1)}, bf16[8,256,128]{2,1,0:T(8,128)(2,1)S(1)}, u32[]{:S(2)}, u32[]{:S(2)}) collective-permute-start(bf16[8,256,128]{2,1,0:T(8,128)(2,1)S(1)} %all_to_all.20), channel_id=1, source_target_pairs={{0,1},{1,0},{2,3},{3,2},{4,5},{5,4},{6,7},{7,6},{8,9},{9,8},{10,11... | collective-permute-start | bytes 1572872 | tf_op jit(solution)/shard_map/ppermute | solution.py:327
  31.9 9.1 %collective-permute-start.1 = (bf16[8,256,128]{2,1,0:T(8,128)(2,1)S(1)}, bf16[8,256,128]{2,1,0:T(8,128)(2,1)S(1)}, u32[]{:S(2)}, u32[]{:S(2)}) collective-permute-start(bf16[8,256,128]{2,1,0:T(8,128)(2,1)S(1)} %all_to_all.20), channel_id=1, source_target_pairs={{0,2},{2,4},{4,6},{6,8},{8,10},{10,12},{12,14},{14,0},{1,15},{3,1}... | collective-permute-start | bytes 1572872 | tf_op jit(solution)/shard_map/ppermute | solution.py:325
  41.0 2.8 %collective-permute-start.2 = (bf16[8,256,128]{2,1,0:T(8,128)(2,1)S(1)}, bf16[8,256,128]{2,1,0:T(8,128)(2,1)S(1)}, u32[]{:S(2)}, u32[]{:S(2)}) collective-permute-start(bf16[8,256,128]{2,1,0:T(8,128)(2,1)S(1)} %collective-permute-done.1), channel_id=1, source_target_pairs={{0,1},{1,0},{2,3},{3,2},{4,5},{5,4},{6,7},{7,6},{8,9},{9,8},{10,11... | collective-permute-start | bytes 1572872 | tf_op jit(solution)/shard_map/ppermute | solution.py:338
  43.4 15.5 %copy-start = (bf16[128,128]{1,0:T(8,128)(2,1)S(1)}, bf16[128,128]{1,0:T(8,128)(2,1)}, u32[]{:S(2)}) copy-start(bf16[128,128]{1,0:T(8,128)(2,1)} %weight.3) | copy-start | bytes 98308
  43.4 15.5 %copy-start.1 = (bf16[1,256,128]{2,1,0:T(8,128)(2,1)S(1)}, bf16[1,256,128]{2,1,0:T(8,128)(2,1)}, u32[]{:S(2)}) copy-start(bf16[1,256,128]{2,1,0:T(8,128)(2,1)} %param.9) | copy-start | bytes 196612
  74.7 3.7 %collective-permute-start.3 = (bf16[2112,128]{1,0:T(8,128)(2,1)S(1)}, bf16[2112,128]{1,0:T(8,128)(2,1)S(1)}, u32[]{:S(2)}, u32[]{:S(2)}) collective-permute-start(bf16[2112,128]{1,0:T(8,128)(2,1)S(1)} %away_part_kernel.3), channel_id=1, source_target_pairs={{0,1},{1,0},{2,3},{3,2},{4,5},{5,4},{6,7},{7,6},{8,9},{9,8},{10,11... | collective-permute-start | bytes 1622024 | tf_op jit(solution)/shard_map/ppermute | solution.py:371
  78.6 8.6 %collective-permute-start.5 = (bf16[2112,128]{1,0:T(8,128)(2,1)S(1)}, bf16[2112,128]{1,0:T(8,128)(2,1)S(1)}, u32[]{:S(2)}, u32[]{:S(2)}) collective-permute-start(bf16[2112,128]{1,0:T(8,128)(2,1)S(1)} %away_kernel.1), channel_id=1, source_target_pairs={{0,2},{2,4},{4,6},{6,8},{8,10},{10,12},{12,14},{14,0},{1,15},{3,1}... | collective-permute-start | bytes 1622024 | tf_op jit(solution)/shard_map/ppermute | solution.py:377
  79.9 2.0 %collective-permute-start.4 = (bf16[2048,128]{1,0:T(8,128)(2,1)S(1)}, bf16[2048,128]{1,0:T(8,128)(2,1)S(1)}, u32[]{:S(2)}, u32[]{:S(2)}) collective-permute-start(bf16[2048,128]{1,0:T(8,128)(2,1)S(1)} %get-tuple-element.21), channel_id=1, source_target_pairs={{0,1},{1,0},{2,3},{3,2},{4,5},{5,4},{6,7},{7,6},{8,9},{9,8},{10,11... | collective-permute-start | bytes 1572872 | tf_op jit(solution)/shard_map/ppermute | solution.py:386
  110.7 3.0 %collective-permute-start.6 = (f32[64,128]{1,0:T(8,128)S(1)}, f32[64,128]{1,0:T(8,128)S(1)}, u32[]{:S(2)}, u32[]{:S(2)}) collective-permute-start(f32[64,128]{1,0:T(8,128)S(1)} %weight_kernel.1.mine), channel_id=1, source_target_pairs={{0,1},{1,0},{2,3},{3,2},{4,5},{5,4},{6,7},{7,6},{8,9},{9,8},{10,11... | collective-permute-start | bytes 98312 | tf_op jit(solution)/shard_map/ppermute | solution.py:395

commit v7 on v6

v7 whole, which is shorter than its diff:
```python
import functools

import jax
import jax.numpy as jnp
from jax import lax
from jax.experimental import pallas as pl
from jax.experimental.pallas import tpu as pltpu
from jax.sharding import Mesh, PartitionSpec as P

CHUNK = 32
BLOCK = 128
ROWS = 16
PART = 16
CAP = 256
OWN, OWN_OTHER, BESIDE, BESIDE_OTHER = PARTS = range(4)
ROW_AT, PLACE_AT = 8, 13
SPARE = (ROWS << ROW_AT) | (PART << PLACE_AT)
COUNT_AT = CAP
WIDTH = CAP + 128
SPAN = PART * BLOCK
EXTRA = BLOCK // 2
SIZES = (4, 2, 2, 4, 2, 2)
AXES = ("x", "ylo", "yhi", "zq", "zp", "core")
REP = ("x", "ylo")
ROW = ("yhi", "zq", "zp", "core")
PARITY = ("yhi", "zq")
ALONG = ("zq", "zp", "core")
SWAP = ((0, 1), (1, 0))
NEXT = tuple((2 * z, 2 * ((z + 1) % 8)) for z in range(8)) + tuple(
    (2 * z + 1, 2 * ((z + 7) % 8) + 1) for z in range(8)
)


def tile_copy(tiles, buffer, sems, chunk):
    span = pl.ds(chunk * CHUNK, CHUNK)
    return pltpu.make_async_copy(tiles.at[span], buffer.at[span], sems.at[chunk])


def tile_groups(part, lists, group):
    @pl.loop(0, (lists[part, COUNT_AT] + CHUNK - 1) // CHUNK)
    def _(k):
        group([lists[part, k * CHUNK + u] for u in range(CHUNK)])


def forward_group(buffer, block_ref, acc):
    def group(codes):
        products = [
            jnp.dot(
                buffer[code & 255],
                block_ref[(code >> PLACE_AT) & (PART - 1)],
                preferred_element_type=jnp.float32,
            )
            for code in codes
        ]
        for code, product in zip(codes, products):
            acc[(code >> ROW_AT) & 31] += product

    return group


def backward_group(buffer, got, acc):
    def group(codes):
        products = []
        for code in codes:
            row = (code >> ROW_AT) & (ROWS - 1)
            grad = got[row // 2, pl.ds(pl.multiple_of((row % 2) * BLOCK, BLOCK), BLOCK), :]
            products.append(
                jnp.dot(grad, buffer[code & 255], preferred_element_type=jnp.float32)
            )
        for code, product in zip(codes, products):
            acc[code >> PLACE_AT] += product

    return group


def make_lists(count, row_ids, col_ids, out, rows, cols, held, sems):
    moves = [
        pltpu.make_async_copy(row_ids, rows, sems.at[0]),
        pltpu.make_async_copy(col_ids, cols, sems.at[1]),
    ]
    for move in moves:
        move.start()
    for move in moves:
        move.wait()
    slots = lax.broadcasted_iota(jnp.int32, (1, CAP), 1)
    block = cols[...]
    z = (block >> 2) & 7
    core = ((block >> 1) & 1) ^ lax.axis_index("core")
    part = ((z & 1) ^ lax.axis_index("zp")) * 2 + core
    place = ((block >> 5) * 4 + (z >> 1)) * 2 + (block & 1)
    code = slots | (rows[...] << ROW_AT) | (place << PLACE_AT)
    part = jnp.where(slots < count[0], part, len(PARTS)).astype(jnp.float32)
    code = (code - SPARE).astype(jnp.float32)

    square = (CAP, CAP)
    across = jnp.broadcast_to(part, square)
    down = across.T
    code = jnp.broadcast_to(code, square).T
    lane = lax.broadcasted_iota(jnp.int32, square, 1)
    earlier = (lane < lax.broadcasted_iota(jnp.int32, square, 0)) & (across == down)
    rank = jnp.sum(jnp.where(earlier, 1.0, 0.0), axis=1, keepdims=True)
    at_rank = rank == lane.astype(jnp.float32)
    for p in PARTS:
        listed = jnp.where(at_rank & (down == p), code, 0.0)
        entries = jnp.sum(listed, axis=0, keepdims=True).astype(jnp.int32) + SPARE
        size = jnp.sum(jnp.where(part == p, 1.0, 0.0), axis=1, keepdims=True)
        held[pl.ds(p, 1), :CAP] = entries
        held[pl.ds(p, 1), CAP:] = jnp.broadcast_to(size, (1, WIDTH - CAP)).astype(jnp.int32)
    copy = pltpu.make_async_copy(held, out, sems.at[2])
    copy.start()
    copy.wait()


def first_forward_kernel(
    count, row_ids, col_ids, tiles, x0, x1, out, buffer, lists, acc, rows, cols, held, sems, ids_sems
):
    chunks = (count[0] + CHUNK - 1) // CHUNK

    @pl.loop(0, chunks)
    def _(c):
        tile_copy(tiles, buffer, sems, c).start()

    make_lists(count, row_ids, col_ids, lists, rows, cols, held, ids_sems)
    acc[...] = jnp.zeros_like(acc)

    def ready(done, need):
        @pl.loop(done, need)
        def _(c):
            tile_copy(tiles, buffer, sems, c).wait()

        return jnp.maximum(done, need)

    works = ((OWN, forward_group(buffer, x0, acc)), (OWN_OTHER, forward_group(buffer, x1, acc)))
    counts = [lists[part, COUNT_AT] for part, _ in works]

    def step(k, done):
        base = k * CHUNK
        for (part, group), size in zip(works, counts):
            last = lists[part, jnp.maximum(jnp.minimum(base + CHUNK, size) - 1, 0)] & 255
            done = ready(done, jnp.where(base < size, last // CHUNK + 1, done))

            @pl.when(base < size)
            def _():
                group([lists[part, base + u] for u in range(CHUNK)])

        return done

    done = lax.fori_loop(0, (jnp.maximum(*counts) + CHUNK - 1) // CHUNK, step, 0)
    ready(done, chunks)
    out[...] = acc[:ROWS]


def forward_kernel(part, lists, buffer, before, x, out, acc):
    acc[:ROWS] = before[...]
    tile_groups(part, lists, forward_group(buffer, x, acc))
    out[...] = acc[:ROWS].astype(out.dtype)


def away_part_kernel(part, lists, buffer, got, out, acc, weight_sum):
    acc[...] = jnp.zeros_like(acc)
    nodes = got.shape[1] - BLOCK
    weight_sum[...] = sum(got[k, nodes:].astype(jnp.float32) for k in range(got.shape[0]))
    tile_groups(part, lists, backward_group(buffer, got, acc))
    out[:SPAN] = acc[:PART].reshape(SPAN, out.shape[1]).astype(out.dtype)
    core = lax.axis_index("core")
    at = pl.multiple_of((core if part == BESIDE else 1 - core) * EXTRA, EXTRA)
    out[SPAN:] = weight_sum[pl.ds(at, EXTRA), :].astype(out.dtype)


def home_part_kernel(lists, buffer, got, own, other, acc, acc_other):
    for part, out, sums in ((OWN_OTHER, other, acc_other), (OWN, own, acc)):
        sums[...] = jnp.zeros_like(sums)
        tile_groups(part, lists, backward_group(buffer, got, sums))
        out[...] = sums[:PART].reshape(out.shape).astype(out.dtype)


def middle_kernel(y_parts, weight, cotangent, z_out, sent):
    reps, nodes, feats = y_parts.shape
    y = sum(y_parts[k].astype(jnp.float32) for k in range(reps))
    z = jnp.dot(
        y,
        weight[...].astype(jnp.float32),
        precision=lax.Precision.HIGHEST,
        preferred_element_type=jnp.float32,
    )
    sigma = jax.nn.sigmoid(z)
    z_out[...] = z
    grad = cotangent[...].astype(jnp.float32) * sigma * (1.0 + z * (1.0 - sigma))
    weight_part = jnp.dot(
        y.T.astype(jnp.bfloat16), grad.astype(jnp.bfloat16), preferred_element_type=jnp.float32
    ).astype(jnp.bfloat16)
    for at in range(0, nodes, BLOCK):
        grad_t = grad[at : at + BLOCK].T.astype(jnp.bfloat16)
        for k in range(reps):
            sent[k, pl.ds(at, BLOCK), :] = grad_t
    for k in range(reps):
        sent[k, nodes:] = weight_part


def hidden_kernel(z, hidden):
    hidden[...] = (z[...] * jax.nn.sigmoid(z[...])).astype(jnp.bfloat16)


def away_kernel(own, other, out):
    out[...] = (own[...] + other[...].astype(jnp.float32)).astype(jnp.bfloat16)


def home_kernel(own, other, away_own, away_other, came, out):
    peers = out.shape[0]
    nodes = out.shape[1] - EXTRA
    weight = away_own[SPAN:] + away_other[SPAN:].astype(jnp.float32)
    weight = (weight + came[SPAN:].astype(jnp.float32)).astype(jnp.bfloat16)
    for k in range(peers):
        here = pl.ds(k * nodes, nodes)
        total = own[here, :] + other[here, :].astype(jnp.float32)
        total = total + came[here, :].astype(jnp.float32)
        out[k, :nodes] = total.astype(jnp.bfloat16)
        out[k, nodes:] = weight


def weight_kernel(got, weight_rows):
    nodes = got.shape[1] - EXTRA
    weight_rows[...] = sum(got[k, nodes:].astype(jnp.float32) for k in range(got.shape[0]))


def feats_kernel(got, weight, grad_feats):
    nodes = grad_feats.shape[0]
    for at in range(0, nodes, BLOCK):
        here = pl.ds(at, BLOCK)
        total = sum(got[k, here].astype(jnp.float32) for k in range(got.shape[0]))
        grad_feats[here, :] = lax.dot_general(
            total.T.astype(jnp.bfloat16),
            weight[...],
            (((1,), (1,)), ((), ())),
            preferred_element_type=jnp.float32,
        ).astype(jnp.bfloat16)


def join_kernel(mine, theirs, grad_weight):
    core = lax.axis_index("core")
    at = pl.multiple_of(core * EXTRA, EXTRA)
    grad_weight[pl.ds(at, EXTRA), :] = mine[...]
    at = pl.multiple_of((1 - core) * EXTRA, EXTRA)
    grad_weight[pl.ds(at, EXTRA), :] = theirs[...]


def fan_kernel(block, out, sem):
    copy = pltpu.make_async_copy(block, out.at[0], sem)
    copy.start()
    copy.wait()
    for k in range(1, out.shape[0]):
        out[k] = out[0]


SMEM = pl.BSMEM = pl.BSMEM = pl.BlockSpec(memory_space=pltpu.SMEM)
VMEM = pl.BlockSpec(memory_space=pltpu.VMEM)
ANY = pl.BlockSpec(memory_space=pl.ANY)


def tile_kernel(kernel, out_shape, lists, held, arrays, scratch):
    out_specs = (VMEM,) * len(out_shape) if isinstance(out_shape, tuple) else VMEM
    return pl.pallas_call(
        kernel,
        out_shape=out_shape,
        in_specs=[SMEM, VMEM] + [VMEM] * len(arrays),
        out_specs=out_specs,
        scratch_shapes=scratch,
        compiler_params=pltpu.CompilerParams(vmem_limit_bytes=16 << 20),
        cost_estimate=pl.CostEstimate(flops=1 << 29, bytes_accessed=4 << 20, transcendentals=0),
        name=getattr(kernel, "func", kernel).__name__,
    )(
        pltpu.with_memory_space_constraint(lists, pltpu.SMEM),
        pltpu.with_memory_space_constraint(held, pltpu.VMEM),
        *arrays,
    )


def sums(rows):
    return pltpu.VMEM((rows + 1, BLOCK, BLOCK), jnp.float32)


def merge(kernel, out_shape, *arrays):
    out_specs = (VMEM,) * len(out_shape) if isinstance(out_shape, tuple) else VMEM
    return pl.pallas_call(
        kernel,
        out_shape=out_shape,
        in_specs=[VMEM] * len(arrays),
        out_specs=out_specs,
        compiler_params=pltpu.CompilerParams(vmem_limit_bytes=16 << 20),
        cost_estimate=pl.CostEstimate(flops=1 << 20, bytes_accessed=4 << 20, transcendentals=0),
        name=kernel.__name__,
    )(*arrays)


def spread(block, axes):
    n = lax.axis_size(axes)
    blocks = pl.pallas_call(
        fan_kernel,
        out_shape=pltpu.VMEM((n, *block.shape), block.dtype),
        in_specs=[ANY],
        out_specs=VMEM,
        scratch_shapes=[pltpu.SemaphoreType.DMA],
        compiler_params=pltpu.CompilerParams(vmem_limit_bytes=16 << 20),
        cost_estimate=pl.CostEstimate(flops=0, bytes_accessed=1 << 16, transcendentals=0),
        name="fan",
    )(pltpu.with_memory_space_constraint(block, pltpu.HBM))
    return lax.all_to_all(blocks, axes, 0, 0)


def local(features, weight, cotangent, tiles, row_ids, col_ids, counts):
    x = features[0]
    nodes, feats = x.shape
    tiles = tiles[0, 0]
    blocks = (PART, BLOCK, feats)
    own = spread(x, PARITY)
    beside = lax.ppermute(own, ALONG, NEXT)
    own_other = lax.ppermute(own, "core", SWAP)
    y_shape = jax.ShapeDtypeStruct((ROWS, BLOCK, BLOCK), jnp.float32)
    y_part, held, lists = pl.pallas_call(
        first_forward_kernel,
        out_shape=(
            y_shape,
            pltpu.VMEM(tiles.shape, jnp.bfloat16),
            pltpu.SMEM((len(PARTS), WIDTH), jnp.int32),
        ),
        in_specs=[SMEM, ANY, ANY, ANY, VMEM, VMEM],
        out_specs=(VMEM, VMEM, SMEM),
        scratch_shapes=[
            sums(ROWS),
            pltpu.VMEM((1, CAP), jnp.int32),
            pltpu.VMEM((1, CAP), jnp.int32),
            pltpu.VMEM((len(PARTS), WIDTH), jnp.int32),
            pltpu.SemaphoreType.DMA((CAP // CHUNK,)),
            pltpu.SemaphoreType.DMA((3,)),
        ],
        compiler_params=pltpu.CompilerParams(vmem_limit_bytes=16 << 20),
        cost_estimate=pl.CostEstimate(flops=1 << 30, bytes_accessed=9 << 20, transcendentals=0),
        name="first_forward",
    )(
        counts[0],
        *[pltpu.with_memory_space_constraint(a, pltpu.HBM) for a in (row_ids[0], col_ids[0], tiles)],
        own.reshape(blocks),
        own_other.reshape(blocks),
    )
    beside, y_part = lax.optimization_barrier((beside, y_part))
    beside_other = lax.ppermute(beside, "core", SWAP)
    y_part = tile_kernel(
        functools.partial(forward_kernel, BESIDE),
        y_shape, lists, held, (y_part, beside.reshape(blocks)), [sums(ROWS)],
    )
    y_part = tile_kernel(
        functools.partial(forward_kernel, BESIDE_OTHER),
        jax.ShapeDtypeStruct((ROWS, BLOCK, BLOCK), jnp.bfloat16),
        lists, held, (y_part, beside_other.reshape(blocks)), [sums(ROWS)],
    )

    reps = lax.axis_size(REP)
    y_parts = lax.all_to_all(y_part.reshape(reps, nodes, feats), REP, 0, 0)
    z, sent = pl.pallas_call(
        middle_kernel,
        out_shape=(
            jax.ShapeDtypeStruct((nodes, feats), jnp.float32),
            pltpu.VMEM((reps, nodes + feats, feats), jnp.bfloat16),
        ),
        in_specs=[VMEM, VMEM, VMEM],
        out_specs=(VMEM, VMEM),
        compiler_params=pltpu.CompilerParams(vmem_limit_bytes=16 << 20),
        cost_estimate=pl.CostEstimate(flops=1 << 25, bytes_accessed=4 << 20, transcendentals=1 << 15),
        name="middle",
    )(y_parts, weight, cotangent[0])
    got = lax.all_to_all(sent, REP, 0, 0)
    def away_part(part, dtype):
        return tile_kernel(
            functools.partial(away_part_kernel, part),
            jax.ShapeDtypeStruct((SPAN + EXTRA, feats), dtype),
            lists, held, (got,), [sums(PART), pltpu.VMEM((BLOCK, feats), jnp.float32)],
        )

    away_other = lax.ppermute(away_part(BESIDE_OTHER, jnp.bfloat16), "core", SWAP)
    away_own = away_part(BESIDE, jnp.float32)
    away = merge(
        away_kernel, jax.ShapeDtypeStruct(away_own.shape, jnp.bfloat16), away_own, away_other
    )
    held, z, away = lax.optimization_barrier((held, z, away))
    came = lax.ppermute(away, ALONG, NEXT)
    home_own, home_other = tile_kernel(
        home_part_kernel,
        (
            jax.ShapeDtypeStruct((SPAN, feats), jnp.float32),
            jax.ShapeDtypeStruct((SPAN, feats), jnp.bfloat16),
        ),
        lists, held, (got,), [sums(PART), sums(PART)],
    )
    hidden = merge(hidden_kernel, jax.ShapeDtypeStruct((nodes, feats), jnp.bfloat16), z)
    home_other, hidden = lax.optimization_barrier((home_other, hidden))
    home_other = lax.ppermute(home_other, "core", SWAP)
    peers = lax.axis_size(PARITY)
    sent = merge(
        home_kernel,
        pltpu.VMEM((peers, nodes + EXTRA, feats), jnp.bfloat16),
        home_own, home_other, away_own, away_other, came,
    )
    got = lax.all_to_all(sent, PARITY, 0, 0)
    mine = merge(weight_kernel, jax.ShapeDtypeStruct((EXTRA, feats), jnp.float32), got)
    theirs = lax.ppermute(mine, "core", SWAP)
    grad_feats = merge(
        feats_kernel, jax.ShapeDtypeStruct((nodes, feats), jnp.bfloat16), got, weight
    )
    grad_weight = merge(
        join_kernel, jax.ShapeDtypeStruct((feats, feats), jnp.float32), mine, theirs
    )
    return hidden[None], grad_feats.reshape(1, nodes, feats), grad_weight


def solution(mesh):
    mesh = Mesh(mesh.devices.reshape(SIZES), AXES)
    placed = P(ROW, REP)
    return jax.shard_map(
        local,
        mesh=mesh,
        in_specs=(placed, P(), placed, placed, placed, placed, placed),
        out_specs=(placed, placed, P()),
        check_vma=False,
    )
```

time: 114 us -> 114 us (level); the launches traced: 114 us -> 113 us
  blocking collectives: 79.2 us -> 74 us
  starting transfers between devices: 10.2 us -> 14.4 us
    all_to_all x1, blocking collectives: 23.4 us -> 19.7 us  [local(): got = lax.all_to_all(sent, PARITY, 0, 0)]
    ppermute x1, starting transfers between devices: 2.1 us -> 5.57 us  [local(): theirs = lax.ppermute(mine, 'core', SWAP)]
    ppermute x1, waiting for transfers between devices: 5.21 us -> 3 us  [local(): came = lax.ppermute(away, ALONG, NEXT)]
    ppermute x1, starting transfers between devices: 0.08 us -> 1.22 us  [local(): came = lax.ppermute(away, ALONG, NEXT)]
    pallas_call x5 -> x6, Pallas kernels: 1.8 us -> 2.46 us  [merge(): pl.pallas_call(kernel, out_shape=out_shape, in_specs=[VMEM] * len(arrays)...]
    pallas_call x7 -> x6, Pallas kernels: 9.84 us -> 10.2 us  [the longest x5 5.34 us: tile_kernel(): pl.pallas_call(kernel, out_shape=out_shape, in_specs=[SMEM, VMEM] + [VMEM...]
where the time goes in v7:
time: 114 us; the launch traced here: 113 us
  blocking collectives  74 us (65%)
  starting transfers between devices  14.4 us (13%)
  Pallas kernels  14 us (12%)
  waiting for transfers between devices  9.34 us (8%)
  between operations  1.39 us (1%)
    all_to_all x1, blocking collectives, spread(): return lax.all_to_all(blocks, axes, 0, 0)  27 us
    all_to_all x1, blocking collectives, local(): got = lax.all_to_all(sent, PARITY, 0, 0)  19.7 us
    all_to_all x1, blocking collectives, local(): got = lax.all_to_all(sent, REP, 0, 0)  13.7 us
    all_to_all x1, blocking collectives, local(): y_parts = lax.all_to_all(y_part.reshape(reps, nodes, feats), REP, 0, 0)  13.6 us
    ppermute x1, starting transfers between devices, local(): theirs = lax.ppermute(mine, 'core', SWAP)  5.57 us
    pallas_call x5, Pallas kernels, tile_kernel(): pl.pallas_call(kernel, out_shape=out_shape, in_specs=[SMEM, VMEM] + [VMEM...  5.34 us
    pallas_call x1, Pallas kernels, local(): pl.pallas_call(first_forward_kernel, out_shape=(y_shape, pltpu.VMEM(tiles...  4.87 us
    ppermute x1, starting transfers between devices, local(): own_other = lax.ppermute(own, 'core', SWAP)  3.26 us
  transfers between devices with their start and end apart: 7, of which 5 were waited for; matrix products, arithmetic and copies ran while one was open for 0% of the time, Pallas kernels for 8%

profile of v7, /device:TPU:1, one launch (start us, length us, event | category | flops | bytes accessed | tf_op | source)
XLA Modules:
  0.0 113.2 jit_solution(9310680777308108589)
XLA Ops:
  0.6 0.9 fan.1
  1.5 27.0 %all_to_all.20 = bf16[8,256,128]{2,1,0:T(8,128)(2,1)S(1)} all-to-all(bf16[8,256,128]{2,1,0:T(8,128)(2,1)S(1)} %fan.1), channel_id=1, replica_groups=mesh['x'=4,'ylo'=2,'yhi'=2,'zq'=4,'zp'=2,'core'=2] {'yhi','zq'}, dimensions={0} | all-to-all | bytes 1048576 | tf_op jit(solution)/shard_map/all_to_all | solution.py:307
  28.6 3.3 %collective-permute-start = (bf16[8,256,128]{2,1,0:T(8,128)(2,1)S(1)}, bf16[8,256,128]{2,1,0:T(8,128)(2,1)S(1)}, u32[]{:S(2)}, u32[]{:S(2)}) collective-permute-start(bf16[8,256,128]{2,1,0:T(8,128)(2,1)S(1)} %all_to_all.20), channel_id=1, source_target_pairs={{0,1},{1,0},{2,3},{3,2},{4,5},{5,4},{6,7},{7,6},{8,9},{9,8},{10,11... | collective-permute-start | bytes 1572872 | tf_op jit(solution)/shard_map/ppermute | solution.py:317
  31.9 0.9 collective-permute-start.1
  33.4 0.0 collective-permute-done
  33.4 4.9 %first_forward.1 = (f32[16,128,128]{2,1,0:T(8,128)S(1)}, bf16[256,128,128]{2,1,0:T(8,128)(2,1)S(1)}, s32[4,384]{1,0:T(4,128)S(4)}) custom-call(s32[1]{0:T(128)} %bitcast.13.count, s32[1,256]{1,0:T(1,128)} %bitcast.24, s32[1,256]{1,0:T(1,128)} %bitcast.25, bf16[256,128,128]{2,1,0:T(8,128)(2,1)} %bitcast.20, bf16[16,128,128]{2,1,0:T(8,128)(2,1)S(1)} %bitcast.14, ...), custom_call_target="tpu_custom_call" | custom-call | flops 1073741824 | bytes 9437184 | tf_op jit(solution)/shard_map/first_forward/pallas_call | solution.py:319
  38.3 2.7 %collective-permute-done.1 = bf16[8,256,128]{2,1,0:T(8,128)(2,1)S(1)} collective-permute-done((bf16[8,256,128]{2,1,0:T(8,128)(2,1)S(1)}, bf16[8,256,128]{2,1,0:T(8,128)(2,1)S(1)}, u32[]{:S(2)}, u32[]{:S(2)}) %collective-permute-start.1) | collective-permute-done | bytes 524320 | tf_op jit(solution)/shard_map/ppermute | solution.py:316
  41.0 1.3 %collective-permute-start.2 = (bf16[8,256,128]{2,1,0:T(8,128)(2,1)S(1)}, bf16[8,256,128]{2,1,0:T(8,128)(2,1)S(1)}, u32[]{:S(2)}, u32[]{:S(2)}) collective-permute-start(bf16[8,256,128]{2,1,0:T(8,128)(2,1)S(1)} %collective-permute-done.1), channel_id=1, source_target_pairs={{0,1},{1,0},{2,3},{3,2},{4,5},{5,4},{6,7},{7,6},{8,9},{9,8},{10,11... | collective-permute-start | bytes 1572872 | tf_op jit(solution)/shard_map/ppermute | solution.py:346
  42.2 0.6 forward_kernel.2.before
  42.9 0.0 copy-start
  42.9 0.0 copy-start.1
  42.9 0.9 collective-permute-done.2
  43.8 1.1 forward_kernel.3
  44.9 13.6 %all_to_all.21.y_parts = bf16[8,256,128]{2,1,0:T(8,128)(2,1)S(1)} all-to-all(bf16[8,256,128]{2,1,0:T(8,128)(2,1)S(1)} %bitcast.15), channel_id=1, replica_groups=mesh['x'=4,'ylo'=2,'yhi'=2,'zq'=4,'zp'=2,'core'=2] {'x','ylo'}, dimensions={0} | all-to-all | bytes 1048576 | tf_op jit(solution)/shard_map/all_to_all | solution.py:358
  58.5 0.5 middle.1
  58.9 13.7 %all_to_all.22.got = bf16[8,384,128]{2,1,0:T(8,128)(2,1)S(1)} all-to-all(bf16[8,384,128]{2,1,0:T(8,128)(2,1)S(1)} %get-tuple-element.23), channel_id=1, replica_groups=mesh['x'=4,'ylo'=2,'yhi'=2,'zq'=4,'zp'=2,'core'=2] {'x','ylo'}, dimensions={0} | all-to-all | bytes 1572864 | tf_op jit(solution)/shard_map/all_to_all | solution.py:371
  72.6 1.2 %away_part_kernel.3 = bf16[2112,128]{1,0:T(8,128)(2,1)S(1)} custom-call(s32[4,384]{1,0:T(4,128)S(4)} %get-tuple-element.17.lists, bf16[256,128,128]{2,1,0:T(8,128)(2,1)S(1)} %get-tuple-element.24.buffer, bf16[8,384,128]{2,1,0:T(8,128)(2,1)S(1)} %all_to_all.22.got), custom_call_target="tpu_custom_call" | custom-call | flops 536870912 | bytes 4194304 | tf_op jit(solution)/shard_map/away_part_kernel/pallas_call | solution.py:262
  73.8 2.2 %collective-permute-start.3 = (bf16[2112,128]{1,0:T(8,128)(2,1)S(1)}, bf16[2112,128]{1,0:T(8,128)(2,1)S(1)}, u32[]{:S(2)}, u32[]{:S(2)}) collective-permute-start(bf16[2112,128]{1,0:T(8,128)(2,1)S(1)} %away_part_kernel.3), channel_id=1, source_target_pairs={{0,1},{1,0},{2,3},{3,2},{4,5},{5,4},{6,7},{7,6},{8,9},{9,8},{10,11... | collective-permute-start | bytes 1622024 | tf_op jit(solution)/shard_map/ppermute | solution.py:379
  75.9 0.7 away_part_kernel.2.own.away_own
  76.6 0.9 collective-permute-done.3.other.away_other
  77.5 0.1 away_kernel.1
  77.6 1.2 %collective-permute-start.5 = (bf16[2112,128]{1,0:T(8,128)(2,1)S(1)}, bf16[2112,128]{1,0:T(8,128)(2,1)S(1)}, u32[]{:S(2)}, u32[]{:S(2)}) collective-permute-start(bf16[2112,128]{1,0:T(8,128)(2,1)S(1)} %away_kernel.1), channel_id=1, source_target_pairs={{0,2},{2,4},{4,6},{6,8},{8,10},{10,12},{12,14},{14,0},{1,15},{3,1}... | collective-permute-start | bytes 1622024 | tf_op jit(solution)/shard_map/ppermute | solution.py:385
  78.8 1.8 %home_part_kernel.1 = (f32[2048,128]{1,0:T(8,128)S(1)}, bf16[2048,128]{1,0:T(8,128)(2,1)S(1)}) custom-call(s32[4,384]{1,0:T(4,128)S(4)} %get-tuple-element.17.lists, bf16[256,128,128]{2,1,0:T(8,128)(2,1)S(1)} %get-tuple-element.24.buffer, bf16[8,384,128]{2,1,0:T(8,128)(2,1)S(1)} %all_to_all.22.got), custom_call_target="tpu_custom_call" | custom-call | flops 536870912 | bytes 4194304 | tf_op jit(solution)/shard_map/home_part_kernel/pallas_call | solution.py:262
  80.6 0.7 hidden_kernel.1
  81.3 0.0 collective-permute-start.4
  81.3 1.9 %collective-permute-done.4.other = bf16[2048,128]{1,0:T(8,128)(2,1)S(1)} collective-permute-done((bf16[2048,128]{1,0:T(8,128)(2,1)S(1)}, bf16[2048,128]{1,0:T(8,128)(2,1)S(1)}, u32[]{:S(2)}, u32[]{:S(2)}) %collective-permute-start.4) | collective-permute-done | bytes 524320 | tf_op jit(solution)/shard_map/ppermute | solution.py:396
  83.2 3.0 %collective-permute-done.5.came = bf16[2112,128]{1,0:T(8,128)(2,1)S(1)} collective-permute-done((bf16[2112,128]{1,0:T(8,128)(2,1)S(1)}, bf16[2112,128]{1,0:T(8,128)(2,1)S(1)}, u32[]{:S(2)}, u32[]{:S(2)}) %collective-permute-start.5) | collective-permute-done | bytes 540704 | tf_op jit(solution)/shard_map/ppermute | solution.py:385
  86.2 0.2 home_kernel.1
  86.3 19.7 %all_to_all.23.got = bf16[8,320,128]{2,1,0:T(8,128)(2,1)S(1)} all-to-all(bf16[8,320,128]{2,1,0:T(8,128)(2,1)S(1)} %home_kernel.1), channel_id=1, replica_groups=mesh['x'=4,'ylo'=2,'yhi'=2,'zq'=4,'zp'=2,'core'=2] {'yhi','zq'}, dimensions={0} | all-to-all | bytes 1310720 | tf_op jit(solution)/shard_map/all_to_all | solution.py:403
  106.1 5.6 %collective-permute-start.6 = (f32[64,128]{1,0:T(8,128)S(1)}, f32[64,128]{1,0:T(8,128)S(1)}, u32[]{:S(2)}, u32[]{:S(2)}) collective-permute-start(f32[64,128]{1,0:T(8,128)S(1)} %weight_kernel.1.mine), channel_id=1, source_target_pairs={{0,1},{1,0},{2,3},{3,2},{4,5},{5,4},{6,7},{7,6},{8,9},{9,8},{10,11... | collective-permute-start | bytes 98312 | tf_op jit(solution)/shard_map/ppermute | solution.py:405
  111.6 0.9 feats_kernel.1
  112.5 0.6 join_kernel.1
  (4 shorter events, 0.0 us)
Async XLA Ops:
  28.6 4.8 %collective-permute-start = (bf16[8,256,128]{2,1,0:T(8,128)(2,1)S(1)}, bf16[8,256,128]{2,1,0:T(8,128)(2,1)S(1)}, u32[]{:S(2)}, u32[]{:S(2)}) collective-permute-start(bf16[8,256,128]{2,1,0:T(8,128)(2,1)S(1)} %all_to_all.20), channel_id=1, source_target_pairs={{0,1},{1,0},{2,3},{3,2},{4,5},{5,4},{6,7},{7,6},{8,9},{9,8},{10,11... | collective-permute-start | bytes 1572872 | tf_op jit(solution)/shard_map/ppermute | solution.py:317
  31.9 9.1 %collective-permute-start.1 = (bf16[8,256,128]{2,1,0:T(8,128)(2,1)S(1)}, bf16[8,256,128]{2,1,0:T(8,128)(2,1)S(1)}, u32[]{:S(2)}, u32[]{:S(2)}) collective-permute-start(bf16[8,256,128]{2,1,0:T(8,128)(2,1)S(1)} %all_to_all.20), channel_id=1, source_target_pairs={{0,2},{2,4},{4,6},{6,8},{8,10},{10,12},{12,14},{14,0},{1,15},{3,1}... | collective-permute-start | bytes 1572872 | tf_op jit(solution)/shard_map/ppermute | solution.py:316
  41.0 2.8 %collective-permute-start.2 = (bf16[8,256,128]{2,1,0:T(8,128)(2,1)S(1)}, bf16[8,256,128]{2,1,0:T(8,128)(2,1)S(1)}, u32[]{:S(2)}, u32[]{:S(2)}) collective-permute-start(bf16[8,256,128]{2,1,0:T(8,128)(2,1)S(1)} %collective-permute-done.1), channel_id=1, source_target_pairs={{0,1},{1,0},{2,3},{3,2},{4,5},{5,4},{6,7},{7,6},{8,9},{9,8},{10,11... | collective-permute-start | bytes 1572872 | tf_op jit(solution)/shard_map/ppermute | solution.py:346
  42.9 15.6 %copy-start = (bf16[128,128]{1,0:T(8,128)(2,1)S(1)}, bf16[128,128]{1,0:T(8,128)(2,1)}, u32[]{:S(2)}) copy-start(bf16[128,128]{1,0:T(8,128)(2,1)} %weight.3) | copy-start | bytes 98308
  42.9 15.6 %copy-start.1 = (bf16[1,256,128]{2,1,0:T(8,128)(2,1)S(1)}, bf16[1,256,128]{2,1,0:T(8,128)(2,1)}, u32[]{:S(2)}) copy-start(bf16[1,256,128]{2,1,0:T(8,128)(2,1)} %param.9) | copy-start | bytes 196612
  73.8 3.7 %collective-permute-start.3 = (bf16[2112,128]{1,0:T(8,128)(2,1)S(1)}, bf16[2112,128]{1,0:T(8,128)(2,1)S(1)}, u32[]{:S(2)}, u32[]{:S(2)}) collective-permute-start(bf16[2112,128]{1,0:T(8,128)(2,1)S(1)} %away_part_kernel.3), channel_id=1, source_target_pairs={{0,1},{1,0},{2,3},{3,2},{4,5},{5,4},{6,7},{7,6},{8,9},{9,8},{10,11... | collective-permute-start | bytes 1622024 | tf_op jit(solution)/shard_map/ppermute | solution.py:379
  77.6 8.6 %collective-permute-start.5 = (bf16[2112,128]{1,0:T(8,128)(2,1)S(1)}, bf16[2112,128]{1,0:T(8,128)(2,1)S(1)}, u32[]{:S(2)}, u32[]{:S(2)}) collective-permute-start(bf16[2112,128]{1,0:T(8,128)(2,1)S(1)} %away_kernel.1), channel_id=1, source_target_pairs={{0,2},{2,4},{4,6},{6,8},{8,10},{10,12},{12,14},{14,0},{1,15},{3,1}... | collective-permute-start | bytes 1622024 | tf_op jit(solution)/shard_map/ppermute | solution.py:385
  81.3 1.9 %collective-permute-start.4 = (bf16[2048,128]{1,0:T(8,128)(2,1)S(1)}, bf16[2048,128]{1,0:T(8,128)(2,1)S(1)}, u32[]{:S(2)}, u32[]{:S(2)}) collective-permute-start(bf16[2048,128]{1,0:T(8,128)(2,1)S(1)} %get-tuple-element.29), channel_id=1, source_target_pairs={{0,1},{1,0},{2,3},{3,2},{4,5},{5,4},{6,7},{7,6},{8,9},{9,8},{10,11... | collective-permute-start | bytes 1572872 | tf_op jit(solution)/shard_map/ppermute | solution.py:396
  106.1 6.5 %collective-permute-start.6 = (f32[64,128]{1,0:T(8,128)S(1)}, f32[64,128]{1,0:T(8,128)S(1)}, u32[]{:S(2)}, u32[]{:S(2)}) collective-permute-start(f32[64,128]{1,0:T(8,128)S(1)} %weight_kernel.1.mine), channel_id=1, source_target_pairs={{0,1},{1,0},{2,3},{3,2},{4,5},{5,4},{6,7},{7,6},{8,9},{9,8},{10,11... | collective-permute-start | bytes 98312 | tf_op jit(solution)/shard_map/ppermute | solution.py:405

commit v8 on v7

--- a/solution.py
+++ b/solution.py
@@ -18,7 +18,7 @@
 COUNT_AT = CAP
 WIDTH = CAP + 128
 SPAN = PART * BLOCK
-EXTRA = BLOCK // 2
+EXTRA = BLOCK // 4
 SIZES = (4, 2, 2, 4, 2, 2)
 AXES = ("x", "ylo", "yhi", "zq", "zp", "core")
 REP = ("x", "ylo")
@@ -158,7 +158,7 @@
 
 def away_part_kernel(part, lists, buffer, got, out, acc, weight_sum):
     acc[...] = jnp.zeros_like(acc)
-    nodes = got.shape[1] - BLOCK
+    nodes = got.shape[1] - BLOCK // 2
     weight_sum[...] = sum(got[k, nodes:].astype(jnp.float32) for k in range(got.shape[0]))
     tile_groups(part, lists, backward_group(buffer, got, acc))
     out[:SPAN] = acc[:PART].reshape(SPAN, out.shape[1]).astype(out.dtype)
@@ -194,7 +194,8 @@
         for k in range(reps):
             sent[k, pl.ds(at, BLOCK), :] = grad_t
     for k in range(reps):
-        sent[k, nodes:] = weight_part
+        at = k % 2 * (BLOCK // 2)
+        sent[k, nodes:] = weight_part[at : at + BLOCK // 2]
 
 
 def hidden_kernel(z, hidden):
@@ -236,12 +237,17 @@
         ).astype(jnp.bfloat16)
 
 
-def join_kernel(mine, theirs, grad_weight):
-    core = lax.axis_index("core")
-    at = pl.multiple_of(core * EXTRA, EXTRA)
-    grad_weight[pl.ds(at, EXTRA), :] = mine[...]
-    at = pl.multiple_of((1 - core) * EXTRA, EXTRA)
-    grad_weight[pl.ds(at, EXTRA), :] = theirs[...]
+def join_kernel(mine, over_core, over_ylo, over_both, grad_weight):
+    core, ylo = lax.axis_index("core"), lax.axis_index("ylo")
+    places = (
+        (mine, ylo, core),
+        (over_core, ylo, 1 - core),
+        (over_ylo, 1 - ylo, core),
+        (over_both, 1 - ylo, 1 - core),
+    )
+    for part, half, quarter in places:
+        at = pl.multiple_of((half * 2 + quarter) * EXTRA, EXTRA)
+        grad_weight[pl.ds(at, EXTRA), :] = part[...]
 
 
 def fan_kernel(block, out, sem):
@@ -360,7 +366,7 @@
         middle_kernel,
         out_shape=(
             jax.ShapeDtypeStruct((nodes, feats), jnp.float32),
-            pltpu.VMEM((reps, nodes + feats, feats), jnp.bfloat16),
+            pltpu.VMEM((reps, nodes + feats // 2, feats), jnp.bfloat16),
         ),
         in_specs=[VMEM, VMEM, VMEM],
         out_specs=(VMEM, VMEM),
@@ -373,7 +379,7 @@
         return tile_kernel(
             functools.partial(away_part_kernel, part),
             jax.ShapeDtypeStruct((SPAN + EXTRA, feats), dtype),
-            lists, held, (got,), [sums(PART), pltpu.VMEM((BLOCK, feats), jnp.float32)],
+            lists, held, (got,), [sums(PART), pltpu.VMEM((BLOCK // 2, feats), jnp.float32)],
         )
 
     away_other = lax.ppermute(away_part(BESIDE_OTHER, jnp.bfloat16), "core", SWAP)
@@ -402,12 +408,16 @@
     )
     got = lax.all_to_all(sent, PARITY, 0, 0)
     mine = merge(weight_kernel, jax.ShapeDtypeStruct((EXTRA, feats), jnp.float32), got)
-    theirs = lax.ppermute(mine, "core", SWAP)
+    others = (
+        lax.ppermute(mine, "ylo", SWAP),
+        lax.ppermute(mine, ("ylo", "core"), ((0, 3), (1, 2), (2, 1), (3, 0))),
+    )
+    over_core = lax.ppermute(mine, "core", SWAP)
     grad_feats = merge(
         feats_kernel, jax.ShapeDtypeStruct((nodes, feats), jnp.bfloat16), got, weight
     )
     grad_weight = merge(
-        join_kernel, jax.ShapeDtypeStruct((feats, feats), jnp.float32), mine, theirs
+        join_kernel, jax.ShapeDtypeStruct((feats, feats), jnp.float32), mine, over_core, *others
     )
     return hidden[None], grad_feats.reshape(1, nodes, feats), grad_weight
 

time: 114 us -> 114 us (level)
  starting transfers between devices: 14.4 us -> 18.1 us
  blocking collectives: 74 us -> 71.1 us
  Pallas kernels: 14 us -> 11.9 us
  waiting for transfers between devices: 9.34 us -> 10.7 us
    ppermute x1, starting transfers between devices: 0.01 us -> 1.7 us  [local(): home_other = lax.ppermute(home_other, 'core', SWAP)]
    pallas_call x5, Pallas kernels: 5.34 us -> 3.79 us  [tile_kernel(): pl.pallas_call(kernel, out_shape=out_shape, in_specs=[SMEM, VMEM] + [VMEM...]
    ppermute x1 -> x3, waiting for transfers between devices: 0.01 us -> 1.36 us  [the longest x1 1.35 us: local(): lax.ppermute(mine, 'ylo', SWAP)]
    ppermute x1 -> x3, starting transfers between devices: 5.57 us -> 6.31 us  [the longest x1 5.51 us: local(): lax.ppermute(mine, ('ylo', 'core'), ((0, 3), (1, 2), (2, 1), (3, 0)))]
  transfers between devices with their start and end apart: 7 -> 9, of which waited for: 5 -> 6; matrix products, arithmetic and copies ran while one was open for 0% -> 0% of each run, Pallas kernels for 8% -> 7%
where the time goes in v8:
time: 114 us; the launch traced here: 113 us
  blocking collectives  71.1 us (62%)
  starting transfers between devices  18.1 us (16%)
  Pallas kernels  11.9 us (10%)
  waiting for transfers between devices  10.7 us (9%)
  between operations  1.39 us (1%)
    all_to_all x1, blocking collectives, spread(): return lax.all_to_all(blocks, axes, 0, 0)  27 us
    all_to_all x1, blocking collectives, local(): got = lax.all_to_all(sent, PARITY, 0, 0)  18.6 us
    all_to_all x1, blocking collectives, local(): got = lax.all_to_all(sent, REP, 0, 0)  12.9 us
    all_to_all x1, blocking collectives, local(): y_parts = lax.all_to_all(y_part.reshape(reps, nodes, feats), REP, 0, 0)  12.5 us
    ppermute x1, starting transfers between devices, local(): lax.ppermute(mine, ('ylo', 'core'), ((0, 3), (1, 2), (2, 1), (3, 0)))  5.51 us
    pallas_call x1, Pallas kernels, local(): pl.pallas_call(first_forward_kernel, out_shape=(y_shape, pltpu.VMEM(tiles...  4.32 us
    pallas_call x5, Pallas kernels, tile_kernel(): pl.pallas_call(kernel, out_shape=out_shape, in_specs=[SMEM, VMEM] + [VMEM...  3.79 us
    ppermute x1, starting transfers between devices, local(): own_other = lax.ppermute(own, 'core', SWAP)  3.26 us
  transfers between devices with their start and end apart: 9, of which 6 were waited for; matrix products, arithmetic and copies ran while one was open for 0% of the time, Pallas kernels for 7%

profile of v8, /device:TPU:1, one launch (start us, length us, event | category | flops | bytes accessed | tf_op | source)
XLA Modules:
  0.0 113.3 jit_solution(12095189981422572309)
XLA Ops:
  0.6 0.9 fan.1
  1.5 27.0 %all_to_all.20 = bf16[8,256,128]{2,1,0:T(8,128)(2,1)S(1)} all-to-all(bf16[8,256,128]{2,1,0:T(8,128)(2,1)S(1)} %fan.1), channel_id=1, replica_groups=mesh['x'=4,'ylo'=2,'yhi'=2,'zq'=4,'zp'=2,'core'=2] {'yhi','zq'}, dimensions={0} | all-to-all | bytes 1048576 | tf_op jit(solution)/shard_map/all_to_all | solution.py:313
  28.6 3.3 %collective-permute-start = (bf16[8,256,128]{2,1,0:T(8,128)(2,1)S(1)}, bf16[8,256,128]{2,1,0:T(8,128)(2,1)S(1)}, u32[]{:S(2)}, u32[]{:S(2)}) collective-permute-start(bf16[8,256,128]{2,1,0:T(8,128)(2,1)S(1)} %all_to_all.20), channel_id=1, source_target_pairs={{0,1},{1,0},{2,3},{3,2},{4,5},{5,4},{6,7},{7,6},{8,9},{9,8},{10,11... | collective-permute-start | bytes 1572872 | tf_op jit(solution)/shard_map/ppermute | solution.py:323
  31.9 0.9 collective-permute-start.1
  33.4 4.3 %first_forward.1 = (f32[16,128,128]{2,1,0:T(8,128)S(1)}, bf16[256,128,128]{2,1,0:T(8,128)(2,1)S(1)}, s32[4,384]{1,0:T(4,128)S(4)}) custom-call(s32[1]{0:T(128)} %bitcast.13.count, s32[1,256]{1,0:T(1,128)} %bitcast.24, s32[1,256]{1,0:T(1,128)} %bitcast.25, bf16[256,128,128]{2,1,0:T(8,128)(2,1)} %bitcast.20, bf16[16,128,128]{2,1,0:T(8,128)(2,1)S(1)} %bitcast.14, ...), custom_call_target="tpu_custom_call" | custom-call | flops 1073741824 | bytes 9437184 | tf_op jit(solution)/shard_map/first_forward/pallas_call | solution.py:325
  37.8 3.2 %collective-permute-done.1 = bf16[8,256,128]{2,1,0:T(8,128)(2,1)S(1)} collective-permute-done((bf16[8,256,128]{2,1,0:T(8,128)(2,1)S(1)}, bf16[8,256,128]{2,1,0:T(8,128)(2,1)S(1)}, u32[]{:S(2)}, u32[]{:S(2)}) %collective-permute-start.1) | collective-permute-done | bytes 524320 | tf_op jit(solution)/shard_map/ppermute | solution.py:322
  41.0 1.3 %collective-permute-start.2 = (bf16[8,256,128]{2,1,0:T(8,128)(2,1)S(1)}, bf16[8,256,128]{2,1,0:T(8,128)(2,1)S(1)}, u32[]{:S(2)}, u32[]{:S(2)}) collective-permute-start(bf16[8,256,128]{2,1,0:T(8,128)(2,1)S(1)} %collective-permute-done.1), channel_id=1, source_target_pairs={{0,1},{1,0},{2,3},{3,2},{4,5},{5,4},{6,7},{7,6},{8,9},{9,8},{10,11... | collective-permute-start | bytes 1572872 | tf_op jit(solution)/shard_map/ppermute | solution.py:352
  42.2 0.6 forward_kernel.2.before
  42.9 0.0 copy-start
  42.9 0.9 collective-permute-done.2
  43.8 0.6 forward_kernel.3
  44.4 12.5 %all_to_all.21.y_parts = bf16[8,256,128]{2,1,0:T(8,128)(2,1)S(1)} all-to-all(bf16[8,256,128]{2,1,0:T(8,128)(2,1)S(1)} %bitcast.15), channel_id=1, replica_groups=mesh['x'=4,'ylo'=2,'yhi'=2,'zq'=4,'zp'=2,'core'=2] {'x','ylo'}, dimensions={0} | all-to-all | bytes 1048576 | tf_op jit(solution)/shard_map/all_to_all | solution.py:364
  56.9 0.5 middle.1
  57.4 12.9 %all_to_all.22.got = bf16[8,320,128]{2,1,0:T(8,128)(2,1)S(1)} all-to-all(bf16[8,320,128]{2,1,0:T(8,128)(2,1)S(1)} %get-tuple-element.23), channel_id=1, replica_groups=mesh['x'=4,'ylo'=2,'yhi'=2,'zq'=4,'zp'=2,'core'=2] {'x','ylo'}, dimensions={0} | all-to-all | bytes 1310720 | tf_op jit(solution)/shard_map/all_to_all | solution.py:377
  70.3 0.6 away_part_kernel.3
  71.0 2.9 %collective-permute-start.3 = (bf16[2080,128]{1,0:T(8,128)(2,1)S(1)}, bf16[2080,128]{1,0:T(8,128)(2,1)S(1)}, u32[]{:S(2)}, u32[]{:S(2)}) collective-permute-start(bf16[2080,128]{1,0:T(8,128)(2,1)S(1)} %away_part_kernel.3), channel_id=1, source_target_pairs={{0,1},{1,0},{2,3},{3,2},{4,5},{5,4},{6,7},{7,6},{8,9},{9,8},{10,11... | collective-permute-start | bytes 1597448 | tf_op jit(solution)/shard_map/ppermute | solution.py:385
  73.9 0.7 away_part_kernel.2.own.away_own
  74.6 0.9 collective-permute-done.3.other.away_other
  75.5 0.1 away_kernel.1
  75.6 1.8 %collective-permute-start.5 = (bf16[2080,128]{1,0:T(8,128)(2,1)S(1)}, bf16[2080,128]{1,0:T(8,128)(2,1)S(1)}, u32[]{:S(2)}, u32[]{:S(2)}) collective-permute-start(bf16[2080,128]{1,0:T(8,128)(2,1)S(1)} %away_kernel.1), channel_id=1, source_target_pairs={{0,2},{2,4},{4,6},{6,8},{8,10},{10,12},{12,14},{14,0},{1,15},{3,1}... | collective-permute-start | bytes 1597448 | tf_op jit(solution)/shard_map/ppermute | solution.py:391
  77.3 1.3 %home_part_kernel.1 = (f32[2048,128]{1,0:T(8,128)S(1)}, bf16[2048,128]{1,0:T(8,128)(2,1)S(1)}) custom-call(s32[4,384]{1,0:T(4,128)S(4)} %get-tuple-element.17.lists, bf16[256,128,128]{2,1,0:T(8,128)(2,1)S(1)} %get-tuple-element.24.buffer, bf16[8,320,128]{2,1,0:T(8,128)(2,1)S(1)} %all_to_all.22.got), custom_call_target="tpu_custom_call" | custom-call | flops 536870912 | bytes 4194304 | tf_op jit(solution)/shard_map/home_part_kernel/pallas_call | solution.py:268
  78.6 0.7 hidden_kernel.1
  79.2 1.7 %collective-permute-start.4 = (bf16[2048,128]{1,0:T(8,128)(2,1)S(1)}, bf16[2048,128]{1,0:T(8,128)(2,1)S(1)}, u32[]{:S(2)}, u32[]{:S(2)}) collective-permute-start(bf16[2048,128]{1,0:T(8,128)(2,1)S(1)} %get-tuple-element.29), channel_id=1, source_target_pairs={{0,1},{1,0},{2,3},{3,2},{4,5},{5,4},{6,7},{7,6},{8,9},{9,8},{10,11... | collective-permute-start | bytes 1572872 | tf_op jit(solution)/shard_map/ppermute | solution.py:402
  80.9 1.5 %collective-permute-done.4.other = bf16[2048,128]{1,0:T(8,128)(2,1)S(1)} collective-permute-done((bf16[2048,128]{1,0:T(8,128)(2,1)S(1)}, bf16[2048,128]{1,0:T(8,128)(2,1)S(1)}, u32[]{:S(2)}, u32[]{:S(2)}) %collective-permute-start.4) | collective-permute-done | bytes 524320 | tf_op jit(solution)/shard_map/ppermute | solution.py:402
  82.5 2.8 %collective-permute-done.5.came = bf16[2080,128]{1,0:T(8,128)(2,1)S(1)} collective-permute-done((bf16[2080,128]{1,0:T(8,128)(2,1)S(1)}, bf16[2080,128]{1,0:T(8,128)(2,1)S(1)}, u32[]{:S(2)}, u32[]{:S(2)}) %collective-permute-start.5) | collective-permute-done | bytes 532512 | tf_op jit(solution)/shard_map/ppermute | solution.py:391
  85.3 0.2 home_kernel.1
  85.5 18.6 %all_to_all.23.got = bf16[8,288,128]{2,1,0:T(8,128)(2,1)S(1)} all-to-all(bf16[8,288,128]{2,1,0:T(8,128)(2,1)S(1)} %home_kernel.1), channel_id=1, replica_groups=mesh['x'=4,'ylo'=2,'yhi'=2,'zq'=4,'zp'=2,'core'=2] {'yhi','zq'}, dimensions={0} | all-to-all | bytes 1179648 | tf_op jit(solution)/shard_map/all_to_all | solution.py:409
  104.1 5.5 %collective-permute-start.8 = (f32[32,128]{1,0:T(8,128)S(1)}, f32[32,128]{1,0:T(8,128)S(1)}, u32[]{:S(2)}, u32[]{:S(2)}) collective-permute-start(f32[32,128]{1,0:T(8,128)S(1)} %weight_kernel.1.mine), channel_id=1, source_target_pairs={{0,33},{1,32},{32,1},{33,0},{2,35},{3,34},{34,3},{35,2},{4,37},{5,... | collective-permute-start | bytes 49160 | tf_op jit(solution)/shard_map/ppermute | solution.py:413
  109.6 0.8 collective-permute-start.7
  110.4 0.9 feats_kernel.1
  111.3 1.4 %collective-permute-done.7.over_ylo = f32[32,128]{1,0:T(8,128)S(1)} collective-permute-done((f32[32,128]{1,0:T(8,128)S(1)}, f32[32,128]{1,0:T(8,128)S(1)}, u32[]{:S(2)}, u32[]{:S(2)}) %collective-permute-start.7) | collective-permute-done | bytes 16416 | tf_op jit(solution)/shard_map/ppermute | solution.py:412
  112.7 0.6 join_kernel.1
  (8 shorter events, 0.0 us)
Async XLA Ops:
  28.6 4.8 %collective-permute-start = (bf16[8,256,128]{2,1,0:T(8,128)(2,1)S(1)}, bf16[8,256,128]{2,1,0:T(8,128)(2,1)S(1)}, u32[]{:S(2)}, u32[]{:S(2)}) collective-permute-start(bf16[8,256,128]{2,1,0:T(8,128)(2,1)S(1)} %all_to_all.20), channel_id=1, source_target_pairs={{0,1},{1,0},{2,3},{3,2},{4,5},{5,4},{6,7},{7,6},{8,9},{9,8},{10,11... | collective-permute-start | bytes 1572872 | tf_op jit(solution)/shard_map/ppermute | solution.py:323
  31.9 9.1 %collective-permute-start.1 = (bf16[8,256,128]{2,1,0:T(8,128)(2,1)S(1)}, bf16[8,256,128]{2,1,0:T(8,128)(2,1)S(1)}, u32[]{:S(2)}, u32[]{:S(2)}) collective-permute-start(bf16[8,256,128]{2,1,0:T(8,128)(2,1)S(1)} %all_to_all.20), channel_id=1, source_target_pairs={{0,2},{2,4},{4,6},{6,8},{8,10},{10,12},{12,14},{14,0},{1,15},{3,1}... | collective-permute-start | bytes 1572872 | tf_op jit(solution)/shard_map/ppermute | solution.py:322
  41.0 2.8 %collective-permute-start.2 = (bf16[8,256,128]{2,1,0:T(8,128)(2,1)S(1)}, bf16[8,256,128]{2,1,0:T(8,128)(2,1)S(1)}, u32[]{:S(2)}, u32[]{:S(2)}) collective-permute-start(bf16[8,256,128]{2,1,0:T(8,128)(2,1)S(1)} %collective-permute-done.1), channel_id=1, source_target_pairs={{0,1},{1,0},{2,3},{3,2},{4,5},{5,4},{6,7},{7,6},{8,9},{9,8},{10,11... | collective-permute-start | bytes 1572872 | tf_op jit(solution)/shard_map/ppermute | solution.py:352
  42.9 14.1 %copy-start = (bf16[128,128]{1,0:T(8,128)(2,1)S(1)}, bf16[128,128]{1,0:T(8,128)(2,1)}, u32[]{:S(2)}) copy-start(bf16[128,128]{1,0:T(8,128)(2,1)} %weight.3) | copy-start | bytes 98308
  42.9 14.1 %copy-start.1 = (bf16[1,256,128]{2,1,0:T(8,128)(2,1)S(1)}, bf16[1,256,128]{2,1,0:T(8,128)(2,1)}, u32[]{:S(2)}) copy-start(bf16[1,256,128]{2,1,0:T(8,128)(2,1)} %param.9) | copy-start | bytes 196612
  71.0 4.5 %collective-permute-start.3 = (bf16[2080,128]{1,0:T(8,128)(2,1)S(1)}, bf16[2080,128]{1,0:T(8,128)(2,1)S(1)}, u32[]{:S(2)}, u32[]{:S(2)}) collective-permute-start(bf16[2080,128]{1,0:T(8,128)(2,1)S(1)} %away_part_kernel.3), channel_id=1, source_target_pairs={{0,1},{1,0},{2,3},{3,2},{4,5},{5,4},{6,7},{7,6},{8,9},{9,8},{10,11... | collective-permute-start | bytes 1597448 | tf_op jit(solution)/shard_map/ppermute | solution.py:385
  75.6 9.7 %collective-permute-start.5 = (bf16[2080,128]{1,0:T(8,128)(2,1)S(1)}, bf16[2080,128]{1,0:T(8,128)(2,1)S(1)}, u32[]{:S(2)}, u32[]{:S(2)}) collective-permute-start(bf16[2080,128]{1,0:T(8,128)(2,1)S(1)} %away_kernel.1), channel_id=1, source_target_pairs={{0,2},{2,4},{4,6},{6,8},{8,10},{10,12},{12,14},{14,0},{1,15},{3,1}... | collective-permute-start | bytes 1597448 | tf_op jit(solution)/shard_map/ppermute | solution.py:391
  79.2 3.2 %collective-permute-start.4 = (bf16[2048,128]{1,0:T(8,128)(2,1)S(1)}, bf16[2048,128]{1,0:T(8,128)(2,1)S(1)}, u32[]{:S(2)}, u32[]{:S(2)}) collective-permute-start(bf16[2048,128]{1,0:T(8,128)(2,1)S(1)} %get-tuple-element.29), channel_id=1, source_target_pairs={{0,1},{1,0},{2,3},{3,2},{4,5},{5,4},{6,7},{7,6},{8,9},{9,8},{10,11... | collective-permute-start | bytes 1572872 | tf_op jit(solution)/shard_map/ppermute | solution.py:402
  104.1 7.2 %collective-permute-start.8 = (f32[32,128]{1,0:T(8,128)S(1)}, f32[32,128]{1,0:T(8,128)S(1)}, u32[]{:S(2)}, u32[]{:S(2)}) collective-permute-start(f32[32,128]{1,0:T(8,128)S(1)} %weight_kernel.1.mine), channel_id=1, source_target_pairs={{0,33},{1,32},{32,1},{33,0},{2,35},{3,34},{34,3},{35,2},{4,37},{5,... | collective-permute-start | bytes 49160 | tf_op jit(solution)/shard_map/ppermute | solution.py:413
  109.6 3.0 %collective-permute-start.7 = (f32[32,128]{1,0:T(8,128)S(1)}, f32[32,128]{1,0:T(8,128)S(1)}, u32[]{:S(2)}, u32[]{:S(2)}) collective-permute-start(f32[32,128]{1,0:T(8,128)S(1)} %weight_kernel.1.mine), channel_id=1, source_target_pairs={{0,32},{32,0},{1,33},{33,1},{2,34},{34,2},{3,35},{35,3},{4,36},{36... | collective-permute-start | bytes 49160 | tf_op jit(solution)/shard_map/ppermute | solution.py:412
  110.4 2.3 %collective-permute-start.6 = (f32[32,128]{1,0:T(8,128)S(1)}, f32[32,128]{1,0:T(8,128)S(1)}, u32[]{:S(2)}, u32[]{:S(2)}) collective-permute-start(f32[32,128]{1,0:T(8,128)S(1)} %weight_kernel.1.mine), channel_id=1, source_target_pairs={{0,1},{1,0},{2,3},{3,2},{4,5},{5,4},{6,7},{7,6},{8,9},{9,8},{10,11... | collective-permute-start | bytes 49160 | tf_op jit(solution)/shard_map/ppermute | solution.py:415

commit v9 on v8

--- a/solution.py
+++ b/solution.py
@@ -156,15 +156,16 @@
     out[...] = acc[:ROWS].astype(out.dtype)
 
 
-def away_part_kernel(part, lists, buffer, got, out, acc, weight_sum):
+def away_part_kernel(part, lists, buffer, got, out, acc):
     acc[...] = jnp.zeros_like(acc)
     nodes = got.shape[1] - BLOCK // 2
-    weight_sum[...] = sum(got[k, nodes:].astype(jnp.float32) for k in range(got.shape[0]))
     tile_groups(part, lists, backward_group(buffer, got, acc))
     out[:SPAN] = acc[:PART].reshape(SPAN, out.shape[1]).astype(out.dtype)
     core = lax.axis_index("core")
-    at = pl.multiple_of((core if part == BESIDE else 1 - core) * EXTRA, EXTRA)
-    out[SPAN:] = weight_sum[pl.ds(at, EXTRA), :].astype(out.dtype)
+    at = nodes + pl.multiple_of((core if part == BESIDE else 1 - core) * EXTRA, EXTRA)
+    rows = pl.ds(pl.multiple_of(at, EXTRA), EXTRA)
+    total = sum(got[k, rows, :].astype(jnp.float32) for k in range(got.shape[0]))
+    out[SPAN:] = total.astype(out.dtype)
 
 
 def home_part_kernel(lists, buffer, got, own, other, acc, acc_other):
@@ -177,12 +178,10 @@
 def middle_kernel(y_parts, weight, cotangent, z_out, sent):
     reps, nodes, feats = y_parts.shape
     y = sum(y_parts[k].astype(jnp.float32) for k in range(reps))
-    z = jnp.dot(
-        y,
-        weight[...].astype(jnp.float32),
-        precision=lax.Precision.HIGHEST,
-        preferred_element_type=jnp.float32,
-    )
+    high = y.astype(jnp.bfloat16)
+    low = (y - high.astype(jnp.float32)).astype(jnp.bfloat16)
+    z = jnp.dot(high, weight[...], preferred_element_type=jnp.float32)
+    z = z + jnp.dot(low, weight[...], preferred_element_type=jnp.float32)
     sigma = jax.nn.sigmoid(z)
     z_out[...] = z
     grad = cotangent[...].astype(jnp.float32) * sigma * (1.0 + z * (1.0 - sigma))
@@ -379,7 +378,7 @@
         return tile_kernel(
             functools.partial(away_part_kernel, part),
             jax.ShapeDtypeStruct((SPAN + EXTRA, feats), dtype),
-            lists, held, (got,), [sums(PART), pltpu.VMEM((BLOCK // 2, feats), jnp.float32)],
+            lists, held, (got,), [sums(PART)],
         )
 
     away_other = lax.ppermute(away_part(BESIDE_OTHER, jnp.bfloat16), "core", SWAP)

time: 114 us -> 113 us (level); the launches traced: 113 us -> 114 us
  blocking collectives: 71.1 us -> 76.7 us
  starting transfers between devices: 18.1 us -> 13 us
    all_to_all x1, blocking collectives: 18.6 us -> 23.9 us  [local(): got = lax.all_to_all(sent, PARITY, 0, 0)]
    ppermute x1, starting transfers between devices: 5.51 us -> 1.61 us  [local(): lax.ppermute(mine, ('ylo', 'core'), ((0, 3), (1, 2), (2, 1), (3, 0)))]
    ppermute x1, starting transfers between devices: 1.75 us -> 0.08 us  [local(): came = lax.ppermute(away, ALONG, NEXT)]
where the time goes in v9:
time: 113 us; the launch traced here: 114 us
  blocking collectives  76.7 us (68%)
  starting transfers between devices  13 us (12%)
  Pallas kernels  11.5 us (10%)
  waiting for transfers between devices  11 us (10%)
  between operations  1.39 us (1%)
    all_to_all x1, blocking collectives, spread(): return lax.all_to_all(blocks, axes, 0, 0)  27 us
    all_to_all x1, blocking collectives, local(): got = lax.all_to_all(sent, PARITY, 0, 0)  23.9 us
    all_to_all x1, blocking collectives, local(): y_parts = lax.all_to_all(y_part.reshape(reps, nodes, feats), REP, 0, 0)  13.6 us
    all_to_all x1, blocking collectives, local(): got = lax.all_to_all(sent, REP, 0, 0)  12.1 us
    pallas_call x1, Pallas kernels, local(): pl.pallas_call(first_forward_kernel, out_shape=(y_shape, pltpu.VMEM(tiles...  3.97 us
    pallas_call x5, Pallas kernels, tile_kernel(): pl.pallas_call(kernel, out_shape=out_shape, in_specs=[SMEM, VMEM] + [VMEM...  3.8 us
    ppermute x1, waiting for transfers between devices, local(): beside = lax.ppermute(own, ALONG, NEXT)  3.57 us
    ppermute x1, waiting for transfers between devices, local(): came = lax.ppermute(away, ALONG, NEXT)  3.56 us
  transfers between devices with their start and end apart: 9, of which 6 were waited for; matrix products, arithmetic and copies ran while one was open for 0% of the time, Pallas kernels for 7%

profile of v9, /device:TPU:1, one launch (start us, length us, event | category | flops | bytes accessed | tf_op | source)
XLA Modules:
  0.0 113.5 jit_solution(3041237456804507154)
XLA Ops:
  0.6 0.9 fan.1
  1.5 27.0 %all_to_all.20 = bf16[8,256,128]{2,1,0:T(8,128)(2,1)S(1)} all-to-all(bf16[8,256,128]{2,1,0:T(8,128)(2,1)S(1)} %fan.1), channel_id=1, replica_groups=mesh['x'=4,'ylo'=2,'yhi'=2,'zq'=4,'zp'=2,'core'=2] {'yhi','zq'}, dimensions={0} | all-to-all | bytes 1048576 | tf_op jit(solution)/shard_map/all_to_all | solution.py:312
  28.6 3.3 %collective-permute-start = (bf16[8,256,128]{2,1,0:T(8,128)(2,1)S(1)}, bf16[8,256,128]{2,1,0:T(8,128)(2,1)S(1)}, u32[]{:S(2)}, u32[]{:S(2)}) collective-permute-start(bf16[8,256,128]{2,1,0:T(8,128)(2,1)S(1)} %all_to_all.20), channel_id=1, source_target_pairs={{0,1},{1,0},{2,3},{3,2},{4,5},{5,4},{6,7},{7,6},{8,9},{9,8},{10,11... | collective-permute-start | bytes 1572872 | tf_op jit(solution)/shard_map/ppermute | solution.py:322
  31.9 0.9 collective-permute-start.1
  33.4 4.0 %first_forward.1 = (f32[16,128,128]{2,1,0:T(8,128)S(1)}, bf16[256,128,128]{2,1,0:T(8,128)(2,1)S(1)}, s32[4,384]{1,0:T(4,128)S(4)}) custom-call(s32[1]{0:T(128)} %bitcast.13.count, s32[1,256]{1,0:T(1,128)} %bitcast.24, s32[1,256]{1,0:T(1,128)} %bitcast.25, bf16[256,128,128]{2,1,0:T(8,128)(2,1)} %bitcast.20, bf16[16,128,128]{2,1,0:T(8,128)(2,1)S(1)} %bitcast.14, ...), custom_call_target="tpu_custom_call" | custom-call | flops 1073741824 | bytes 9437184 | tf_op jit(solution)/shard_map/first_forward/pallas_call | solution.py:324
  37.4 3.6 %collective-permute-done.1 = bf16[8,256,128]{2,1,0:T(8,128)(2,1)S(1)} collective-permute-done((bf16[8,256,128]{2,1,0:T(8,128)(2,1)S(1)}, bf16[8,256,128]{2,1,0:T(8,128)(2,1)S(1)}, u32[]{:S(2)}, u32[]{:S(2)}) %collective-permute-start.1) | collective-permute-done | bytes 524320 | tf_op jit(solution)/shard_map/ppermute | solution.py:321
  41.0 1.3 %collective-permute-start.2 = (bf16[8,256,128]{2,1,0:T(8,128)(2,1)S(1)}, bf16[8,256,128]{2,1,0:T(8,128)(2,1)S(1)}, u32[]{:S(2)}, u32[]{:S(2)}) collective-permute-start(bf16[8,256,128]{2,1,0:T(8,128)(2,1)S(1)} %collective-permute-done.1), channel_id=1, source_target_pairs={{0,1},{1,0},{2,3},{3,2},{4,5},{5,4},{6,7},{7,6},{8,9},{9,8},{10,11... | collective-permute-start | bytes 1572872 | tf_op jit(solution)/shard_map/ppermute | solution.py:351
  42.2 0.6 forward_kernel.2.before
  42.9 0.0 copy-start
  42.9 0.9 collective-permute-done.2
  43.8 0.6 forward_kernel.3
  44.4 13.6 %all_to_all.21.y_parts = bf16[8,256,128]{2,1,0:T(8,128)(2,1)S(1)} all-to-all(bf16[8,256,128]{2,1,0:T(8,128)(2,1)S(1)} %bitcast.15), channel_id=1, replica_groups=mesh['x'=4,'ylo'=2,'yhi'=2,'zq'=4,'zp'=2,'core'=2] {'x','ylo'}, dimensions={0} | all-to-all | bytes 1048576 | tf_op jit(solution)/shard_map/all_to_all | solution.py:363
  58.0 0.4 middle.1
  58.3 12.1 %all_to_all.22.got = bf16[8,320,128]{2,1,0:T(8,128)(2,1)S(1)} all-to-all(bf16[8,320,128]{2,1,0:T(8,128)(2,1)S(1)} %get-tuple-element.23), channel_id=1, replica_groups=mesh['x'=4,'ylo'=2,'yhi'=2,'zq'=4,'zp'=2,'core'=2] {'x','ylo'}, dimensions={0} | all-to-all | bytes 1310720 | tf_op jit(solution)/shard_map/all_to_all | solution.py:376
  70.5 0.6 away_part_kernel.3
  71.1 3.0 %collective-permute-start.3 = (bf16[2080,128]{1,0:T(8,128)(2,1)S(1)}, bf16[2080,128]{1,0:T(8,128)(2,1)S(1)}, u32[]{:S(2)}, u32[]{:S(2)}) collective-permute-start(bf16[2080,128]{1,0:T(8,128)(2,1)S(1)} %away_part_kernel.3), channel_id=1, source_target_pairs={{0,1},{1,0},{2,3},{3,2},{4,5},{5,4},{6,7},{7,6},{8,9},{9,8},{10,11... | collective-permute-start | bytes 1597448 | tf_op jit(solution)/shard_map/ppermute | solution.py:384
  74.1 0.7 away_part_kernel.2.own.away_own
  74.8 0.9 collective-permute-done.3.other.away_other
  75.7 0.1 away_kernel.1
  75.8 0.1 collective-permute-start.5
  75.8 1.3 %home_part_kernel.1 = (f32[2048,128]{1,0:T(8,128)S(1)}, bf16[2048,128]{1,0:T(8,128)(2,1)S(1)}) custom-call(s32[4,384]{1,0:T(4,128)S(4)} %get-tuple-element.17.lists, bf16[256,128,128]{2,1,0:T(8,128)(2,1)S(1)} %get-tuple-element.24.buffer, bf16[8,320,128]{2,1,0:T(8,128)(2,1)S(1)} %all_to_all.22.got), custom_call_target="tpu_custom_call" | custom-call | flops 536870912 | bytes 4194304 | tf_op jit(solution)/shard_map/home_part_kernel/pallas_call | solution.py:267
  77.1 0.7 hidden_kernel.1
  77.8 1.4 %collective-permute-start.4 = (bf16[2048,128]{1,0:T(8,128)(2,1)S(1)}, bf16[2048,128]{1,0:T(8,128)(2,1)S(1)}, u32[]{:S(2)}, u32[]{:S(2)}) collective-permute-start(bf16[2048,128]{1,0:T(8,128)(2,1)S(1)} %get-tuple-element.29), channel_id=1, source_target_pairs={{0,1},{1,0},{2,3},{3,2},{4,5},{5,4},{6,7},{7,6},{8,9},{9,8},{10,11... | collective-permute-start | bytes 1572872 | tf_op jit(solution)/shard_map/ppermute | solution.py:401
  79.1 1.5 %collective-permute-done.4.other = bf16[2048,128]{1,0:T(8,128)(2,1)S(1)} collective-permute-done((bf16[2048,128]{1,0:T(8,128)(2,1)S(1)}, bf16[2048,128]{1,0:T(8,128)(2,1)S(1)}, u32[]{:S(2)}, u32[]{:S(2)}) %collective-permute-start.4) | collective-permute-done | bytes 524320 | tf_op jit(solution)/shard_map/ppermute | solution.py:401
  80.7 3.6 %collective-permute-done.5.came = bf16[2080,128]{1,0:T(8,128)(2,1)S(1)} collective-permute-done((bf16[2080,128]{1,0:T(8,128)(2,1)S(1)}, bf16[2080,128]{1,0:T(8,128)(2,1)S(1)}, u32[]{:S(2)}, u32[]{:S(2)}) %collective-permute-start.5) | collective-permute-done | bytes 532512 | tf_op jit(solution)/shard_map/ppermute | solution.py:390
  84.2 0.2 home_kernel.1
  84.4 23.9 %all_to_all.23.got = bf16[8,288,128]{2,1,0:T(8,128)(2,1)S(1)} all-to-all(bf16[8,288,128]{2,1,0:T(8,128)(2,1)S(1)} %home_kernel.1), channel_id=1, replica_groups=mesh['x'=4,'ylo'=2,'yhi'=2,'zq'=4,'zp'=2,'core'=2] {'yhi','zq'}, dimensions={0} | all-to-all | bytes 1179648 | tf_op jit(solution)/shard_map/all_to_all | solution.py:408
  108.4 1.6 %collective-permute-start.8 = (f32[32,128]{1,0:T(8,128)S(1)}, f32[32,128]{1,0:T(8,128)S(1)}, u32[]{:S(2)}, u32[]{:S(2)}) collective-permute-start(f32[32,128]{1,0:T(8,128)S(1)} %weight_kernel.1.mine), channel_id=1, source_target_pairs={{0,33},{1,32},{32,1},{33,0},{2,35},{3,34},{34,3},{35,2},{4,37},{5,... | collective-permute-start | bytes 49160 | tf_op jit(solution)/shard_map/ppermute | solution.py:412
  110.0 1.5 %collective-permute-start.7 = (f32[32,128]{1,0:T(8,128)S(1)}, f32[32,128]{1,0:T(8,128)S(1)}, u32[]{:S(2)}, u32[]{:S(2)}) collective-permute-start(f32[32,128]{1,0:T(8,128)S(1)} %weight_kernel.1.mine), channel_id=1, source_target_pairs={{0,32},{32,0},{1,33},{33,1},{2,34},{34,2},{3,35},{35,3},{4,36},{36... | collective-permute-start | bytes 49160 | tf_op jit(solution)/shard_map/ppermute | solution.py:411
  111.5 0.9 feats_kernel.1
  112.4 0.5 collective-permute-done.7.over_ylo
  112.9 0.6 join_kernel.1
  (8 shorter events, 0.0 us)
Async XLA Ops:
  28.6 4.8 %collective-permute-start = (bf16[8,256,128]{2,1,0:T(8,128)(2,1)S(1)}, bf16[8,256,128]{2,1,0:T(8,128)(2,1)S(1)}, u32[]{:S(2)}, u32[]{:S(2)}) collective-permute-start(bf16[8,256,128]{2,1,0:T(8,128)(2,1)S(1)} %all_to_all.20), channel_id=1, source_target_pairs={{0,1},{1,0},{2,3},{3,2},{4,5},{5,4},{6,7},{7,6},{8,9},{9,8},{10,11... | collective-permute-start | bytes 1572872 | tf_op jit(solution)/shard_map/ppermute | solution.py:322
  31.9 9.1 %collective-permute-start.1 = (bf16[8,256,128]{2,1,0:T(8,128)(2,1)S(1)}, bf16[8,256,128]{2,1,0:T(8,128)(2,1)S(1)}, u32[]{:S(2)}, u32[]{:S(2)}) collective-permute-start(bf16[8,256,128]{2,1,0:T(8,128)(2,1)S(1)} %all_to_all.20), channel_id=1, source_target_pairs={{0,2},{2,4},{4,6},{6,8},{8,10},{10,12},{12,14},{14,0},{1,15},{3,1}... | collective-permute-start | bytes 1572872 | tf_op jit(solution)/shard_map/ppermute | solution.py:321
  41.0 2.8 %collective-permute-start.2 = (bf16[8,256,128]{2,1,0:T(8,128)(2,1)S(1)}, bf16[8,256,128]{2,1,0:T(8,128)(2,1)S(1)}, u32[]{:S(2)}, u32[]{:S(2)}) collective-permute-start(bf16[8,256,128]{2,1,0:T(8,128)(2,1)S(1)} %collective-permute-done.1), channel_id=1, source_target_pairs={{0,1},{1,0},{2,3},{3,2},{4,5},{5,4},{6,7},{7,6},{8,9},{9,8},{10,11... | collective-permute-start | bytes 1572872 | tf_op jit(solution)/shard_map/ppermute | solution.py:351
  42.9 15.1 %copy-start = (bf16[128,128]{1,0:T(8,128)(2,1)S(1)}, bf16[128,128]{1,0:T(8,128)(2,1)}, u32[]{:S(2)}) copy-start(bf16[128,128]{1,0:T(8,128)(2,1)} %weight.3) | copy-start | bytes 98308
  42.9 15.1 %copy-start.1 = (bf16[1,256,128]{2,1,0:T(8,128)(2,1)S(1)}, bf16[1,256,128]{2,1,0:T(8,128)(2,1)}, u32[]{:S(2)}) copy-start(bf16[1,256,128]{2,1,0:T(8,128)(2,1)} %param.9) | copy-start | bytes 196612
  71.1 4.5 %collective-permute-start.3 = (bf16[2080,128]{1,0:T(8,128)(2,1)S(1)}, bf16[2080,128]{1,0:T(8,128)(2,1)S(1)}, u32[]{:S(2)}, u32[]{:S(2)}) collective-permute-start(bf16[2080,128]{1,0:T(8,128)(2,1)S(1)} %away_part_kernel.3), channel_id=1, source_target_pairs={{0,1},{1,0},{2,3},{3,2},{4,5},{5,4},{6,7},{7,6},{8,9},{9,8},{10,11... | collective-permute-start | bytes 1597448 | tf_op jit(solution)/shard_map/ppermute | solution.py:384
  75.8 8.5 %collective-permute-start.5 = (bf16[2080,128]{1,0:T(8,128)(2,1)S(1)}, bf16[2080,128]{1,0:T(8,128)(2,1)S(1)}, u32[]{:S(2)}, u32[]{:S(2)}) collective-permute-start(bf16[2080,128]{1,0:T(8,128)(2,1)S(1)} %away_kernel.1), channel_id=1, source_target_pairs={{0,2},{2,4},{4,6},{6,8},{8,10},{10,12},{12,14},{14,0},{1,15},{3,1}... | collective-permute-start | bytes 1597448 | tf_op jit(solution)/shard_map/ppermute | solution.py:390
  77.8 2.9 %collective-permute-start.4 = (bf16[2048,128]{1,0:T(8,128)(2,1)S(1)}, bf16[2048,128]{1,0:T(8,128)(2,1)S(1)}, u32[]{:S(2)}, u32[]{:S(2)}) collective-permute-start(bf16[2048,128]{1,0:T(8,128)(2,1)S(1)} %get-tuple-element.29), channel_id=1, source_target_pairs={{0,1},{1,0},{2,3},{3,2},{4,5},{5,4},{6,7},{7,6},{8,9},{9,8},{10,11... | collective-permute-start | bytes 1572872 | tf_op jit(solution)/shard_map/ppermute | solution.py:401
  108.4 4.0 %collective-permute-start.8 = (f32[32,128]{1,0:T(8,128)S(1)}, f32[32,128]{1,0:T(8,128)S(1)}, u32[]{:S(2)}, u32[]{:S(2)}) collective-permute-start(f32[32,128]{1,0:T(8,128)S(1)} %weight_kernel.1.mine), channel_id=1, source_target_pairs={{0,33},{1,32},{32,1},{33,0},{2,35},{3,34},{34,3},{35,2},{4,37},{5,... | collective-permute-start | bytes 49160 | tf_op jit(solution)/shard_map/ppermute | solution.py:412
  110.0 2.9 %collective-permute-start.7 = (f32[32,128]{1,0:T(8,128)S(1)}, f32[32,128]{1,0:T(8,128)S(1)}, u32[]{:S(2)}, u32[]{:S(2)}) collective-permute-start(f32[32,128]{1,0:T(8,128)S(1)} %weight_kernel.1.mine), channel_id=1, source_target_pairs={{0,32},{32,0},{1,33},{33,1},{2,34},{34,2},{3,35},{35,3},{4,36},{36... | collective-permute-start | bytes 49160 | tf_op jit(solution)/shard_map/ppermute | solution.py:411
  111.5 1.4 %collective-permute-start.6 = (f32[32,128]{1,0:T(8,128)S(1)}, f32[32,128]{1,0:T(8,128)S(1)}, u32[]{:S(2)}, u32[]{:S(2)}) collective-permute-start(f32[32,128]{1,0:T(8,128)S(1)} %weight_kernel.1.mine), channel_id=1, source_target_pairs={{0,1},{1,0},{2,3},{3,2},{4,5},{5,4},{6,7},{7,6},{8,9},{9,8},{10,11... | collective-permute-start | bytes 49160 | tf_op jit(solution)/shard_map/ppermute | solution.py:414

commit v10 on v9

--- a/solution.py
+++ b/solution.py
@@ -186,7 +186,7 @@
     z_out[...] = z
     grad = cotangent[...].astype(jnp.float32) * sigma * (1.0 + z * (1.0 - sigma))
     weight_part = jnp.dot(
-        y.T.astype(jnp.bfloat16), grad.astype(jnp.bfloat16), preferred_element_type=jnp.float32
+        high.T, grad.astype(jnp.bfloat16), preferred_element_type=jnp.float32
     ).astype(jnp.bfloat16)
     for at in range(0, nodes, BLOCK):
         grad_t = grad[at : at + BLOCK].T.astype(jnp.bfloat16)

time: 113 us -> 114 us (level)
  blocking collectives: 76.7 us -> 73.5 us
  starting transfers between devices: 13 us -> 15.9 us
  waiting for transfers between devices: 11 us -> 12.4 us
    ppermute x1, starting transfers between devices: 1.61 us -> 6.33 us  [local(): lax.ppermute(mine, ('ylo', 'core'), ((0, 3), (1, 2), (2, 1), (3, 0)))]
    all_to_all x1, blocking collectives: 23.9 us -> 20.2 us  [local(): got = lax.all_to_all(sent, PARITY, 0, 0)]
    ppermute x1, starting transfers between devices: 1.46 us -> 0.01 us  [local(): lax.ppermute(mine, 'ylo', SWAP)]
where the time goes in v10:
time: 114 us; the launch traced here: 115 us
  blocking collectives  73.5 us (64%)
  starting transfers between devices  15.9 us (14%)
  waiting for transfers between devices  12.4 us (11%)
  Pallas kernels  11.5 us (10%)
  between operations  1.39 us (1%)
    all_to_all x1, blocking collectives, spread(): return lax.all_to_all(blocks, axes, 0, 0)  27 us
    all_to_all x1, blocking collectives, local(): got = lax.all_to_all(sent, PARITY, 0, 0)  20.2 us
    all_to_all x1, blocking collectives, local(): y_parts = lax.all_to_all(y_part.reshape(reps, nodes, feats), REP, 0, 0)  13.5 us
    all_to_all x1, blocking collectives, local(): got = lax.all_to_all(sent, REP, 0, 0)  12.8 us
    ppermute x1, starting transfers between devices, local(): lax.ppermute(mine, ('ylo', 'core'), ((0, 3), (1, 2), (2, 1), (3, 0)))  6.33 us
    ppermute x1, waiting for transfers between devices, local(): came = lax.ppermute(away, ALONG, NEXT)  4.3 us
    pallas_call x1, Pallas kernels, local(): pl.pallas_call(first_forward_kernel, out_shape=(y_shape, pltpu.VMEM(tiles...  3.97 us
    pallas_call x5, Pallas kernels, tile_kernel(): pl.pallas_call(kernel, out_shape=out_shape, in_specs=[SMEM, VMEM] + [VMEM...  3.8 us
  transfers between devices with their start and end apart: 9, of which 6 were waited for; matrix products, arithmetic and copies ran while one was open for 0% of the time, Pallas kernels for 7%

profile of v10, /device:TPU:1, one launch (start us, length us, event | category | flops | bytes accessed | tf_op | source)
XLA Modules:
  0.0 114.7 jit_solution(12245444191686412880)
XLA Ops:
  0.6 0.9 fan.1
  1.5 27.0 %all_to_all.20 = bf16[8,256,128]{2,1,0:T(8,128)(2,1)S(1)} all-to-all(bf16[8,256,128]{2,1,0:T(8,128)(2,1)S(1)} %fan.1), channel_id=1, replica_groups=mesh['x'=4,'ylo'=2,'yhi'=2,'zq'=4,'zp'=2,'core'=2] {'yhi','zq'}, dimensions={0} | all-to-all | bytes 1048576 | tf_op jit(solution)/shard_map/all_to_all | solution.py:312
  28.6 3.3 %collective-permute-start = (bf16[8,256,128]{2,1,0:T(8,128)(2,1)S(1)}, bf16[8,256,128]{2,1,0:T(8,128)(2,1)S(1)}, u32[]{:S(2)}, u32[]{:S(2)}) collective-permute-start(bf16[8,256,128]{2,1,0:T(8,128)(2,1)S(1)} %all_to_all.20), channel_id=1, source_target_pairs={{0,1},{1,0},{2,3},{3,2},{4,5},{5,4},{6,7},{7,6},{8,9},{9,8},{10,11... | collective-permute-start | bytes 1572872 | tf_op jit(solution)/shard_map/ppermute | solution.py:322
  31.9 0.9 collective-permute-start.1
  33.4 4.0 %first_forward.1 = (f32[16,128,128]{2,1,0:T(8,128)S(1)}, bf16[256,128,128]{2,1,0:T(8,128)(2,1)S(1)}, s32[4,384]{1,0:T(4,128)S(4)}) custom-call(s32[1]{0:T(128)} %bitcast.13.count, s32[1,256]{1,0:T(1,128)} %bitcast.24, s32[1,256]{1,0:T(1,128)} %bitcast.25, bf16[256,128,128]{2,1,0:T(8,128)(2,1)} %bitcast.20, bf16[16,128,128]{2,1,0:T(8,128)(2,1)S(1)} %bitcast.14, ...), custom_call_target="tpu_custom_call" | custom-call | flops 1073741824 | bytes 9437184 | tf_op jit(solution)/shard_map/first_forward/pallas_call | solution.py:324
  37.4 3.6 %collective-permute-done.1 = bf16[8,256,128]{2,1,0:T(8,128)(2,1)S(1)} collective-permute-done((bf16[8,256,128]{2,1,0:T(8,128)(2,1)S(1)}, bf16[8,256,128]{2,1,0:T(8,128)(2,1)S(1)}, u32[]{:S(2)}, u32[]{:S(2)}) %collective-permute-start.1) | collective-permute-done | bytes 524320 | tf_op jit(solution)/shard_map/ppermute | solution.py:321
  41.0 1.3 %collective-permute-start.2 = (bf16[8,256,128]{2,1,0:T(8,128)(2,1)S(1)}, bf16[8,256,128]{2,1,0:T(8,128)(2,1)S(1)}, u32[]{:S(2)}, u32[]{:S(2)}) collective-permute-start(bf16[8,256,128]{2,1,0:T(8,128)(2,1)S(1)} %collective-permute-done.1), channel_id=1, source_target_pairs={{0,1},{1,0},{2,3},{3,2},{4,5},{5,4},{6,7},{7,6},{8,9},{9,8},{10,11... | collective-permute-start | bytes 1572872 | tf_op jit(solution)/shard_map/ppermute | solution.py:351
  42.2 0.6 forward_kernel.2.before
  42.9 0.9 collective-permute-done.2
  43.8 0.6 forward_kernel.3
  44.4 13.5 %all_to_all.21.y_parts = bf16[8,256,128]{2,1,0:T(8,128)(2,1)S(1)} all-to-all(bf16[8,256,128]{2,1,0:T(8,128)(2,1)S(1)} %bitcast.15), channel_id=1, replica_groups=mesh['x'=4,'ylo'=2,'yhi'=2,'zq'=4,'zp'=2,'core'=2] {'x','ylo'}, dimensions={0} | all-to-all | bytes 1048576 | tf_op jit(solution)/shard_map/all_to_all | solution.py:363
  57.9 0.4 middle.1
  58.2 12.8 %all_to_all.22.got = bf16[8,320,128]{2,1,0:T(8,128)(2,1)S(1)} all-to-all(bf16[8,320,128]{2,1,0:T(8,128)(2,1)S(1)} %get-tuple-element.23), channel_id=1, replica_groups=mesh['x'=4,'ylo'=2,'yhi'=2,'zq'=4,'zp'=2,'core'=2] {'x','ylo'}, dimensions={0} | all-to-all | bytes 1310720 | tf_op jit(solution)/shard_map/all_to_all | solution.py:376
  71.0 0.6 away_part_kernel.3
  71.7 2.9 %collective-permute-start.3 = (bf16[2080,128]{1,0:T(8,128)(2,1)S(1)}, bf16[2080,128]{1,0:T(8,128)(2,1)S(1)}, u32[]{:S(2)}, u32[]{:S(2)}) collective-permute-start(bf16[2080,128]{1,0:T(8,128)(2,1)S(1)} %away_part_kernel.3), channel_id=1, source_target_pairs={{0,1},{1,0},{2,3},{3,2},{4,5},{5,4},{6,7},{7,6},{8,9},{9,8},{10,11... | collective-permute-start | bytes 1597448 | tf_op jit(solution)/shard_map/ppermute | solution.py:384
  74.6 0.7 away_part_kernel.2.own.away_own
  75.3 0.9 collective-permute-done.3.other.away_other
  76.2 0.1 away_kernel.1
  76.3 0.1 collective-permute-start.5
  76.3 1.3 %home_part_kernel.1 = (f32[2048,128]{1,0:T(8,128)S(1)}, bf16[2048,128]{1,0:T(8,128)(2,1)S(1)}) custom-call(s32[4,384]{1,0:T(4,128)S(4)} %get-tuple-element.17.lists, bf16[256,128,128]{2,1,0:T(8,128)(2,1)S(1)} %get-tuple-element.24.buffer, bf16[8,320,128]{2,1,0:T(8,128)(2,1)S(1)} %all_to_all.22.got), custom_call_target="tpu_custom_call" | custom-call | flops 536870912 | bytes 4194304 | tf_op jit(solution)/shard_map/home_part_kernel/pallas_call | solution.py:267
  77.6 0.7 hidden_kernel.1
  78.3 0.6 collective-permute-start.4
  78.9 1.5 %collective-permute-done.4.other = bf16[2048,128]{1,0:T(8,128)(2,1)S(1)} collective-permute-done((bf16[2048,128]{1,0:T(8,128)(2,1)S(1)}, bf16[2048,128]{1,0:T(8,128)(2,1)S(1)}, u32[]{:S(2)}, u32[]{:S(2)}) %collective-permute-start.4) | collective-permute-done | bytes 524320 | tf_op jit(solution)/shard_map/ppermute | solution.py:401
  80.5 4.3 %collective-permute-done.5.came = bf16[2080,128]{1,0:T(8,128)(2,1)S(1)} collective-permute-done((bf16[2080,128]{1,0:T(8,128)(2,1)S(1)}, bf16[2080,128]{1,0:T(8,128)(2,1)S(1)}, u32[]{:S(2)}, u32[]{:S(2)}) %collective-permute-start.5) | collective-permute-done | bytes 532512 | tf_op jit(solution)/shard_map/ppermute | solution.py:390
  84.8 0.2 home_kernel.1
  84.9 20.2 %all_to_all.23.got = bf16[8,288,128]{2,1,0:T(8,128)(2,1)S(1)} all-to-all(bf16[8,288,128]{2,1,0:T(8,128)(2,1)S(1)} %home_kernel.1), channel_id=1, replica_groups=mesh['x'=4,'ylo'=2,'yhi'=2,'zq'=4,'zp'=2,'core'=2] {'yhi','zq'}, dimensions={0} | all-to-all | bytes 1179648 | tf_op jit(solution)/shard_map/all_to_all | solution.py:408
  105.1 6.3 %collective-permute-start.8 = (f32[32,128]{1,0:T(8,128)S(1)}, f32[32,128]{1,0:T(8,128)S(1)}, u32[]{:S(2)}, u32[]{:S(2)}) collective-permute-start(f32[32,128]{1,0:T(8,128)S(1)} %weight_kernel.1.mine), channel_id=1, source_target_pairs={{0,33},{1,32},{32,1},{33,0},{2,35},{3,34},{34,3},{35,2},{4,37},{5,... | collective-permute-start | bytes 49160 | tf_op jit(solution)/shard_map/ppermute | solution.py:412
  111.5 0.5 collective-permute-start.6
  112.0 0.9 feats_kernel.1
  112.9 0.0 collective-permute-done.8.over_both
  112.9 1.2 %collective-permute-done.7.over_ylo = f32[32,128]{1,0:T(8,128)S(1)} collective-permute-done((f32[32,128]{1,0:T(8,128)S(1)}, f32[32,128]{1,0:T(8,128)S(1)}, u32[]{:S(2)}, u32[]{:S(2)}) %collective-permute-start.7) | collective-permute-done | bytes 16416 | tf_op jit(solution)/shard_map/ppermute | solution.py:411
  114.1 0.6 join_kernel.1
  (8 shorter events, 0.0 us)
Async XLA Ops:
  28.6 4.8 %collective-permute-start = (bf16[8,256,128]{2,1,0:T(8,128)(2,1)S(1)}, bf16[8,256,128]{2,1,0:T(8,128)(2,1)S(1)}, u32[]{:S(2)}, u32[]{:S(2)}) collective-permute-start(bf16[8,256,128]{2,1,0:T(8,128)(2,1)S(1)} %all_to_all.20), channel_id=1, source_target_pairs={{0,1},{1,0},{2,3},{3,2},{4,5},{5,4},{6,7},{7,6},{8,9},{9,8},{10,11... | collective-permute-start | bytes 1572872 | tf_op jit(solution)/shard_map/ppermute | solution.py:322
  31.9 9.1 %collective-permute-start.1 = (bf16[8,256,128]{2,1,0:T(8,128)(2,1)S(1)}, bf16[8,256,128]{2,1,0:T(8,128)(2,1)S(1)}, u32[]{:S(2)}, u32[]{:S(2)}) collective-permute-start(bf16[8,256,128]{2,1,0:T(8,128)(2,1)S(1)} %all_to_all.20), channel_id=1, source_target_pairs={{0,2},{2,4},{4,6},{6,8},{8,10},{10,12},{12,14},{14,0},{1,15},{3,1}... | collective-permute-start | bytes 1572872 | tf_op jit(solution)/shard_map/ppermute | solution.py:321
  41.0 2.8 %collective-permute-start.2 = (bf16[8,256,128]{2,1,0:T(8,128)(2,1)S(1)}, bf16[8,256,128]{2,1,0:T(8,128)(2,1)S(1)}, u32[]{:S(2)}, u32[]{:S(2)}) collective-permute-start(bf16[8,256,128]{2,1,0:T(8,128)(2,1)S(1)} %collective-permute-done.1), channel_id=1, source_target_pairs={{0,1},{1,0},{2,3},{3,2},{4,5},{5,4},{6,7},{7,6},{8,9},{9,8},{10,11... | collective-permute-start | bytes 1572872 | tf_op jit(solution)/shard_map/ppermute | solution.py:351
  42.9 15.0 %copy-start = (bf16[128,128]{1,0:T(8,128)(2,1)S(1)}, bf16[128,128]{1,0:T(8,128)(2,1)}, u32[]{:S(2)}) copy-start(bf16[128,128]{1,0:T(8,128)(2,1)} %weight.3) | copy-start | bytes 98308
  42.9 15.0 %copy-start.1 = (bf16[1,256,128]{2,1,0:T(8,128)(2,1)S(1)}, bf16[1,256,128]{2,1,0:T(8,128)(2,1)}, u32[]{:S(2)}) copy-start(bf16[1,256,128]{2,1,0:T(8,128)(2,1)} %param.9) | copy-start | bytes 196612
  71.7 4.5 %collective-permute-start.3 = (bf16[2080,128]{1,0:T(8,128)(2,1)S(1)}, bf16[2080,128]{1,0:T(8,128)(2,1)S(1)}, u32[]{:S(2)}, u32[]{:S(2)}) collective-permute-start(bf16[2080,128]{1,0:T(8,128)(2,1)S(1)} %away_part_kernel.3), channel_id=1, source_target_pairs={{0,1},{1,0},{2,3},{3,2},{4,5},{5,4},{6,7},{7,6},{8,9},{9,8},{10,11... | collective-permute-start | bytes 1597448 | tf_op jit(solution)/shard_map/ppermute | solution.py:384
  76.3 8.5 %collective-permute-start.5 = (bf16[2080,128]{1,0:T(8,128)(2,1)S(1)}, bf16[2080,128]{1,0:T(8,128)(2,1)S(1)}, u32[]{:S(2)}, u32[]{:S(2)}) collective-permute-start(bf16[2080,128]{1,0:T(8,128)(2,1)S(1)} %away_kernel.1), channel_id=1, source_target_pairs={{0,2},{2,4},{4,6},{6,8},{8,10},{10,12},{12,14},{14,0},{1,15},{3,1}... | collective-permute-start | bytes 1597448 | tf_op jit(solution)/shard_map/ppermute | solution.py:390
  78.3 2.2 %collective-permute-start.4 = (bf16[2048,128]{1,0:T(8,128)(2,1)S(1)}, bf16[2048,128]{1,0:T(8,128)(2,1)S(1)}, u32[]{:S(2)}, u32[]{:S(2)}) collective-permute-start(bf16[2048,128]{1,0:T(8,128)(2,1)S(1)} %get-tuple-element.29), channel_id=1, source_target_pairs={{0,1},{1,0},{2,3},{3,2},{4,5},{5,4},{6,7},{7,6},{8,9},{9,8},{10,11... | collective-permute-start | bytes 1572872 | tf_op jit(solution)/shard_map/ppermute | solution.py:401
  105.1 7.8 %collective-permute-start.8 = (f32[32,128]{1,0:T(8,128)S(1)}, f32[32,128]{1,0:T(8,128)S(1)}, u32[]{:S(2)}, u32[]{:S(2)}) collective-permute-start(f32[32,128]{1,0:T(8,128)S(1)} %weight_kernel.1.mine), channel_id=1, source_target_pairs={{0,33},{1,32},{32,1},{33,0},{2,35},{3,34},{34,3},{35,2},{4,37},{5,... | collective-permute-start | bytes 49160 | tf_op jit(solution)/shard_map/ppermute | solution.py:412
  111.5 2.6 %collective-permute-start.7 = (f32[32,128]{1,0:T(8,128)S(1)}, f32[32,128]{1,0:T(8,128)S(1)}, u32[]{:S(2)}, u32[]{:S(2)}) collective-permute-start(f32[32,128]{1,0:T(8,128)S(1)} %weight_kernel.1.mine), channel_id=1, source_target_pairs={{0,32},{32,0},{1,33},{33,1},{2,34},{34,2},{3,35},{35,3},{4,36},{36... | collective-permute-start | bytes 49160 | tf_op jit(solution)/shard_map/ppermute | solution.py:411
  111.5 2.6 %collective-permute-start.6 = (f32[32,128]{1,0:T(8,128)S(1)}, f32[32,128]{1,0:T(8,128)S(1)}, u32[]{:S(2)}, u32[]{:S(2)}) collective-permute-start(f32[32,128]{1,0:T(8,128)S(1)} %weight_kernel.1.mine), channel_id=1, source_target_pairs={{0,1},{1,0},{2,3},{3,2},{4,5},{5,4},{6,7},{7,6},{8,9},{9,8},{10,11... | collective-permute-start | bytes 49160 | tf_op jit(solution)/shard_map/ppermute | solution.py:414
